TPU v7x, 256 devices: a whole 4x4x8 slice. The times are simulated.
256 devices in a mesh: dp: 4 (over x_hi, core), seq: 64 (over y, x_lo, z).
Axes of the slice: x: 4 (x_hi: 2, x_lo: 2; x = x_hi * 2 + x_lo), y: 4, z: 8, core: 2. Of those that a mesh axis runs over, the one named last changes fastest.
Arguments:
- tokens: bfloat16 [4, 64, 128, 1152], P('dp', 'seq'), may hold values from -6 to 6
- modulation: float32 [4, 2, 3, 1152], P('dp'), may hold values from -3 to 3
- frame_pos: int32 [64], replicated, may hold values from 0 to 63, each once
- qkv_weight: bfloat16 [2, 1152, 1728], replicated, may hold values from -2 to 2
- out_weight: bfloat16 [2, 576, 1152], replicated, may hold values from -0.25 to 0.25
- seed_grad: bfloat16 [4, 64, 128, 1152], P('dp', None, 'seq'), may hold values from -6 to 6
Outputs:
- block_out: bfloat16 [4, 64, 128, 1152], P('dp', None, 'seq')
- tokens_grad: bfloat16 [4, 64, 128, 1152], P('dp', 'seq')
- qkv_grad: float32 [1152, 1728], P('dp', 'seq')
- proj_grad: float32 [576, 1152], P('seq', 'dp')
Inputs may be any that keep to these rules, and one draw needn't show every extreme that they name: `frame_pos`: each of 0 to 63 appears once.
All inputs are finite; a program needn't handle non-finite values.
Results may differ from a plain program's by a relative error of at most 0.022.
Values may be sent and summed in bfloat16 or wider, within the bound.
No kernel may reach another device: no remote copies, remote signals or barrier semaphores. Data moves between devices by JAX's collectives and lax.ppermute only.
A program may use at most 128 MiB of HBM per device.

v0:
```python
from functools import partial
import math

import jax
import jax.numpy as jnp
from jax import lax
from jax.sharding import PartitionSpec as P

HEADS = 8
HEAD_DIM = 72


EPS = 1e-06
ROPE_BASE = 10000.0


def premix(inputs, shift_row, scale_row):
    average = jnp.mean(inputs, axis=-1, keepdims=True)
    centered = inputs - average
    variance = jnp.mean(centered * centered, axis=-1, keepdims=True)
    normed = centered * lax.rsqrt(variance + EPS)
    return (normed * (1.0 + scale_row) + shift_row).astype(jnp.bfloat16)


def softmax_rows(scores):
    largest = lax.stop_gradient(jnp.max(scores, axis=-1, keepdims=True))
    exponent = jnp.exp(scores - largest)
    return (exponent / jnp.sum(exponent, axis=-1, keepdims=True)).astype(jnp.bfloat16)


def spatial_core(query, keys, values):
    scores = jnp.einsum(
        "cflhe,cfmhe->cfhlm", query, keys, preferred_element_type=jnp.float32
    ) * HEAD_DIM ** (-0.5)
    probability = softmax_rows(scores)
    return jnp.einsum(
        "cfhlm,cfmhe->cflhe", probability, values, preferred_element_type=jnp.float32
    ).astype(jnp.bfloat16)


def rotate_half(tensor, cosines, sines):
    half_dim = tensor.shape[-1] // 2
    first = tensor[..., :half_dim]
    second = tensor[..., half_dim:]
    return jnp.concatenate(
        [first * cosines - second * sines, second * cosines + first * sines], axis=-1
    )


def rope_tables(frame_pos):
    half_dim = HEAD_DIM // 2
    frequency = jnp.exp(
        jnp.arange(half_dim, dtype=jnp.float32) * (-2.0 * math.log(ROPE_BASE) / HEAD_DIM)
    )
    angles = frame_pos.astype(jnp.float32)[:, None] * frequency[None, :]
    return (jnp.cos(angles)[None, :, None, None, :], jnp.sin(angles)[None, :, None, None, :])


def temporal_core(query, keys, values, cosines, sines):
    rot_query = rotate_half(query.astype(jnp.float32), cosines, sines).astype(jnp.bfloat16)
    rot_keys = rotate_half(keys.astype(jnp.float32), cosines, sines).astype(jnp.bfloat16)
    scores = jnp.einsum(
        "cflhe,cglhe->clhfg", rot_query, rot_keys, preferred_element_type=jnp.float32
    ) * HEAD_DIM ** (-0.5)
    probability = softmax_rows(scores)
    return jnp.einsum(
        "clhfg,cglhe->cflhe", probability, values, preferred_element_type=jnp.float32
    ).astype(jnp.bfloat16)


def sublayer_forward(tokens, modulate_row, qkv_weight, out_weight, attend):
    width_attn = out_weight.shape[0]
    inputs_full = tokens.astype(jnp.float32)
    shift_row = modulate_row[:, 0][:, None, None, :]
    scale_row = modulate_row[:, 1][:, None, None, :]
    gate_row = modulate_row[:, 2][:, None, None, :]
    normed, premix_back = jax.vjp(lambda inputs: premix(inputs, shift_row, scale_row), inputs_full)
    projected = jnp.dot(normed, qkv_weight, preferred_element_type=jnp.float32).astype(jnp.bfloat16)
    head_shape = projected.shape[:-1] + (HEADS, HEAD_DIM)
    query = projected[..., :width_attn].reshape(head_shape)
    keys = projected[..., width_attn : 2 * width_attn].reshape(head_shape)
    values = projected[..., 2 * width_attn :].reshape(head_shape)
    attended, attend_back = jax.vjp(attend, query, keys, values)
    flat_attended = attended.reshape(projected.shape[:-1] + (width_attn,))
    branch = jnp.dot(flat_attended, out_weight, preferred_element_type=jnp.float32)
    result = (inputs_full + gate_row * branch).astype(jnp.bfloat16)
    return (result, (normed, flat_attended, gate_row, premix_back, attend_back))


def sublayer_backward(upstream, kept_state, qkv_weight, out_weight, want_weights):
    normed, flat_attended, gate_row, premix_back, attend_back = kept_state
    width_attn = out_weight.shape[0]
    width_model = out_weight.shape[1]
    contract = (((0,), (0,)), ((), ()))
    grad_full = upstream.astype(jnp.float32)
    branch_grad = (gate_row * grad_full).astype(jnp.bfloat16)
    attended_grad = jnp.dot(branch_grad, out_weight.T, preferred_element_type=jnp.float32).astype(
        jnp.bfloat16
    )
    head_shape = attended_grad.shape[:-1] + (HEADS, HEAD_DIM)
    query_grad, keys_grad, values_grad = attend_back(attended_grad.reshape(head_shape))
    flat_shape = attended_grad.shape
    projected_grad = jnp.concatenate(
        [
            query_grad.reshape(flat_shape),
            keys_grad.reshape(flat_shape),
            values_grad.reshape(flat_shape),
        ],
        axis=-1,
    )
    normed_grad = jnp.dot(projected_grad, qkv_weight.T, preferred_element_type=jnp.float32).astype(
        jnp.bfloat16
    )
    (inputs_grad,) = premix_back(normed_grad)
    input_result = (grad_full + inputs_grad).astype(jnp.bfloat16)
    if want_weights:
        proj_part = lax.dot_general(
            flat_attended.reshape(-1, width_attn),
            branch_grad.reshape(-1, width_model),
            contract,
            preferred_element_type=jnp.float32,
        )
        qkv_part = lax.dot_general(
            normed.reshape(-1, width_model),
            projected_grad.reshape(-1, 3 * width_attn),
            contract,
            preferred_element_type=jnp.float32,
        )
        return (input_result, qkv_part, proj_part)
    return (input_result, None, None)


def shards(tokens, modulation, frame_pos, qkv_weight, out_weight, seed_grad):
    spatial_out, spatial_kept = sublayer_forward(
        tokens, modulation[:, 0], qkv_weight[0], out_weight[0], spatial_core
    )
    located = lax.all_to_all(spatial_out, "seq", split_axis=2, concat_axis=1, tiled=True)
    cosines, sines = rope_tables(frame_pos)
    attend_time = partial(temporal_core, cosines=cosines, sines=sines)
    block_out, temporal_kept = sublayer_forward(
        located, modulation[:, 1], qkv_weight[1], out_weight[1], attend_time
    )
    located_grad, temporal_qkv, temporal_proj = sublayer_backward(
        seed_grad, temporal_kept, qkv_weight[1], out_weight[1], True
    )
    framed_grad = lax.all_to_all(located_grad, "seq", split_axis=1, concat_axis=2, tiled=True)
    tokens_grad, unused_qkv, unused_proj = sublayer_backward(
        framed_grad, spatial_kept, qkv_weight[0], out_weight[0], False
    )
    parted = (
        lax.psum_scatter(temporal_qkv, "seq", scatter_dimension=1, tiled=True),
        lax.psum_scatter(temporal_proj, "seq", scatter_dimension=0, tiled=True),
    )
    qkv_sum, proj_sum = (
        lax.psum_scatter(
            parted[0].astype(jnp.bfloat16), "dp", scatter_dimension=0, tiled=True
        ).astype(jnp.float32),
        lax.psum_scatter(
            parted[1].astype(jnp.bfloat16), "dp", scatter_dimension=1, tiled=True
        ).astype(jnp.float32),
    )
    return (block_out, tokens_grad, qkv_sum, proj_sum)


def solution(mesh):
    return jax.shard_map(
        shards,
        mesh=mesh,
        in_specs=(
            P("dp", "seq", None, None),
            P("dp", None, None, None),
            P(),
            P(),
            P(),
            P("dp", None, "seq", None),
        ),
        out_specs=(
            P("dp", None, "seq", None),
            P("dp", "seq", None, None),
            P("dp", "seq"),
            P("seq", "dp"),
        ),
        check_vma=False,
    )
```

profile of v0, /device:TPU:32, one launch (start us, length us, event | category | flops | bytes accessed | tf_op | source)
XLA Modules:
  0.0 755.1 jit_solution(4072705639193161070)
XLA Ops:
  7.2 1.1 convert_reduce_fusion
  8.3 1.2 fusion.87
  12.1 3.7 fusion.48
  16.5 2.2 fusion.139
  18.7 1.5 convolution_convert_fusion.9
  21.7 3.1 reduce.40
  24.8 1.8 reshape.655
  26.6 12.7 %all-to-all-start = ((bf16[64,2,1152]{2,1,0:T(2,128)(2,1)}), bf16[64,2,1152]{2,1,0:T(2,128)(2,1)S(1)}, u32[]{:S(2)}, u32[]{:S(2)}) async-start(bf16[64,2,1152]{2,1,0:T(2,128)(2,1)} %reshape.655), calls=%async_computation | async-start | bytes 589824 | tf_op jit(solution)/shard_map/all_to_all | solution.py:137
  39.3 1.0 fusion.85
  40.3 1.2 fusion.75
  43.4 1.9 reshape.619
  45.3 1.3 fusion.137
  47.9 1.3 multiply_divide_fusion.1
  50.0 3.0 all-to-all-done
  53.4 4.5 convert_reduce_fusion.2
  57.9 2.0 multiply_reduce_fusion.1
  61.3 2.9 convert_reduce_fusion.3
  64.3 3.5 fusion.45
  68.2 1.0 reshape.616
  69.8 2.2 fusion.105
  72.0 1.7 fusion.140
  73.8 1.0 fusion.63
  74.8 0.9 fusion.70
  76.6 1.4 fusion.69
  78.1 1.7 fusion.66
  79.8 1.1 copy.114
  81.8 1.1 multiply_add_fusion.1
  84.3 4.3 convolution_bitcast_fusion
  88.6 188.3 %fusion = f32[1152,32]{0,1:T(8,128)S(1)} fusion(f32[1152,1728]{0,1:T(8,128)} %convolution_bitcast_fusion), kind=kCustom, calls=%all-reduce-scatter | all-reduce-scatter fusion | flops 2359297 | bytes 8111104
  278.3 1.9 collective-permute-start.1
  280.2 1.9 collective-permute-start.2
  282.1 1.9 collective-permute-start.3
  284.0 1.9 collective-permute-start.4
  287.6 3.0 multiply_reduce_fusion
  291.2 1.0 copy.119
  292.2 12.7 %all-to-all-start.1 = ((bf16[1,64,2,1152]{3,2,0,1:T(2,128)(2,1)}), bf16[1,64,2,1152]{3,2,0,1:T(2,128)(2,1)}, u32[]{:S(2)}, u32[]{:S(2)}) async-start(bf16[1,64,2,1152]{3,2,0,1:T(2,128)(2,1)} %copy.119), calls=%async_computation.1 | async-start | bytes 589824 | tf_op jit(solution)/shard_map/all_to_all | solution.py:146
  304.9 1.6 fusion.141
  306.5 5.8 collective-permute-start.9
  312.4 331.0 %all-reduce.8 = bf16[576,1152]{1,0:T(8,128)(2,1)} all-reduce(f32[576,1152]{1,0:T(8,128)S(1)} %fusion.141), channel_id=4, replica_groups=mesh['dp'=4,'seq'=64] {'seq'}, use_global_device_ids=true, to_apply=%region_16.0.clone | all-reduce | flops 663552 | bytes 3981312
  643.4 2.2 collective-permute-start.5
  645.6 1.9 collective-permute-start.6
  647.5 1.9 collective-permute-start.7
  649.4 1.9 collective-permute-start.8
  651.3 3.6 collective-permute-start
  654.9 1.5 dynamic-slice_convert_fusion.1
  656.4 1.8 copy.106
  658.2 1.9 reshape.617
  660.0 1.7 copy.135
  661.8 17.0 %concatenate.38 = bf16[1152,347]{0,1:T(8,128)(2,1)} concatenate(bf16[1152,27]{0,1:T(8,128)(2,1)} %collective-permute-done.9, bf16[1152,32]{0,1:T(8,128)(2,1)} %collective-permute-done.8, bf16[1152,32]{0,1:T(8,128)(2,1)} %collective-permute-done.7, bf16[1152,32]{0,1:T(8,128)(2,1)} %collective-permute-done.6, bf16[1152,32]{0,1:T(8,128)(2,1)} %collective-permute-done.5, ...), dimensions={1} | concatenate | bytes 1672704
  678.9 1.5 dynamic-slice_convert_fusion
  680.4 1.8 copy.133
  682.2 1.3 fusion.44
  683.6 1.0 copy.126
  684.6 14.3 %reduce-scatter.11.cloned.1.call-done = bf16[288,9]{1,0:T(8,128)(2,1)} async-done(((bf16[1152,9]{1,0:T(8,128)(2,1)}), bf16[288,9]{1,0:T(8,128)(2,1)}) %reduce-scatter.11.cloned.1.call-update) | async-done | bytes 5200
  698.9 1.0 copy.136
  700.5 33.2 %reduce-scatter.9.cloned.1.call-done = bf16[288,27]{1,0:T(8,128)(2,1)} async-done(((bf16[1152,27]{1,0:T(8,128)(2,1)}), bf16[288,27]{1,0:T(8,128)(2,1)}) %reduce-scatter.9.cloned.1.call-update) | async-done | bytes 15568
  733.6 1.0 copy.134
  735.2 1.2 multiply_convert_fusion
  737.3 1.5 fusion.78
  738.8 1.5 convolution_convert_fusion.6
  740.3 1.3 multiply_reduce_fusion.2
  742.9 3.0 fusion.91
  746.2 1.1 reshape.635
  747.3 1.0 add_convert_fusion
  (140 shorter events, 20.7 us)
Async XLA Ops:
  8.3 3.2 copy-start.26
  9.5 0.5 copy-start.32
  10.0 1.5 copy-start.30
  11.5 0.6 copy-start.22
  12.1 8.2 %copy-start = (bf16[1,1,128,1152]{3,2,1,0:T(8,128)(2,1)S(1)}, bf16[1,1,128,1152]{3,2,1,0:T(8,128)(2,1)}, u32[]{:S(2)}) copy-start(bf16[1,1,128,1152]{3,2,1,0:T(8,128)(2,1)} %param.6) | copy-start | bytes 884740
  12.1 8.2 %copy-start.1 = (bf16[2,576,1152]{2,1,0:T(8,128)(2,1)S(1)}, bf16[2,576,1152]{2,1,0:T(8,128)(2,1)}, u32[]{:S(2)}) copy-start(bf16[2,576,1152]{2,1,0:T(8,128)(2,1)} %param.10) | copy-start | bytes 7962628
  16.5 3.8 copy-start.11
  18.7 1.5 copy-start.28
  26.6 26.4 %all-to-all-start = ((bf16[64,2,1152]{2,1,0:T(2,128)(2,1)}), bf16[64,2,1152]{2,1,0:T(2,128)(2,1)S(1)}, u32[]{:S(2)}, u32[]{:S(2)}) async-start(bf16[64,2,1152]{2,1,0:T(2,128)(2,1)} %reshape.655), calls=%async_computation | async-start | bytes 589824 | tf_op jit(solution)/shard_map/all_to_all | solution.py:137
  64.3 3.6 copy-start.4
  69.8 4.0 copy-start.8
  69.8 5.0 copy-start.7
  72.0 4.6 copy-start.13
  72.0 4.6 copy-start.14
  72.0 4.6 copy-start.15
  72.0 4.6 copy-start.16
  73.8 1.0 copy-start.24
  76.0 0.6 copy-start.25
  82.9 1.2 copy-start.10
  82.9 1.4 copy-start.5
  88.6 197.6 %copy-start.34 = (f32[128]{0:T(128)S(1)}, f32[128]{0:T(128)}, u32[]{:S(2)}) copy-start(f32[128]{0:T(128)} %get-tuple-element.67) | copy-start | bytes 1540
  88.6 197.8 %copy-start.19 = (f32[64,2]{1,0:T(8,128)S(1)}, f32[64,2]{1,0:T(8,128)}, u32[]{:S(2)}) copy-start(f32[64,2]{1,0:T(8,128)} %div.98) | copy-start | bytes 1540
  88.6 197.9 %copy-start.9 = (bf16[1,64,2,8,72]{4,1,3,2,0:T(8,128)(2,1)S(1)}, bf16[1,64,2,8,72]{4,1,3,2,0:T(8,128)(2,1)}, u32[]{:S(2)}) copy-start(bf16[1,64,2,8,72]{4,1,3,2,0:T(8,128)(2,1)} %fusion.63) | copy-start | bytes 442372
  88.6 199.0 %copy-start.20 = (f32[1152]{0:T(1024)S(1)}, f32[1152]{0:T(1024)}, u32[]{:S(2)}) copy-start(f32[1152]{0:T(1024)} %get-tuple-element.24) | copy-start | bytes 13828
  276.9 28.0 %copy-start.3 = (f32[1152,32]{0,1:T(8,128)}, f32[1152,32]{0,1:T(8,128)S(1)}, u32[]{:S(2)}) copy-start(f32[1152,32]{0,1:T(8,128)S(1)} %fusion) | copy-start | bytes 442372
  278.3 367.3 %collective-permute-start.1 = (bf16[1152,32]{0,1:T(8,128)(2,1)}, bf16[1152,32]{0,1:T(8,128)(2,1)}, u32[]{:S(2)}, u32[]{:S(2)}) collective-permute-start(bf16[1152,32]{0,1:T(8,128)(2,1)} %convert.66), channel_id=1, source_target_pairs={{0,2},{1,3},{2,4},{3,5},{4,6},{5,7},{6,8},{7,9},{8,10},{9,11},{10,... | collective-permute-start | bytes 221192
  280.2 367.3 %collective-permute-start.2 = (bf16[1152,32]{0,1:T(8,128)(2,1)}, bf16[1152,32]{0,1:T(8,128)(2,1)}, u32[]{:S(2)}, u32[]{:S(2)}) collective-permute-start(bf16[1152,32]{0,1:T(8,128)(2,1)} %convert.66), channel_id=1, source_target_pairs={{0,3},{1,4},{2,5},{3,6},{4,7},{5,8},{6,9},{7,10},{8,11},{9,12},{10... | collective-permute-start | bytes 221192
  282.1 367.3 %collective-permute-start.3 = (bf16[1152,32]{0,1:T(8,128)(2,1)}, bf16[1152,32]{0,1:T(8,128)(2,1)}, u32[]{:S(2)}, u32[]{:S(2)}) collective-permute-start(bf16[1152,32]{0,1:T(8,128)(2,1)} %convert.66), channel_id=1, source_target_pairs={{0,4},{1,5},{2,6},{3,7},{4,8},{5,9},{6,10},{7,11},{8,12},{9,13},{1... | collective-permute-start | bytes 221192
  284.0 367.3 %collective-permute-start.4 = (bf16[1152,32]{0,1:T(8,128)(2,1)}, bf16[1152,32]{0,1:T(8,128)(2,1)}, u32[]{:S(2)}, u32[]{:S(2)}) collective-permute-start(bf16[1152,32]{0,1:T(8,128)(2,1)} %convert.66), channel_id=1, source_target_pairs={{0,5},{1,6},{2,7},{3,8},{4,9},{5,10},{6,11},{7,12},{8,13},{9,14},{... | collective-permute-start | bytes 221192
  287.6 3.3 copy-start.6
  292.2 443.0 %all-to-all-start.1 = ((bf16[1,64,2,1152]{3,2,0,1:T(2,128)(2,1)}), bf16[1,64,2,1152]{3,2,0,1:T(2,128)(2,1)}, u32[]{:S(2)}, u32[]{:S(2)}) async-start(bf16[1,64,2,1152]{3,2,0,1:T(2,128)(2,1)} %copy.119), calls=%async_computation.1 | async-start | bytes 589824 | tf_op jit(solution)/shard_map/all_to_all | solution.py:146
  304.9 394.0 %reduce-scatter.11.cloned.1.call-start = ((), (), s32[]{:S(2)}) async-start(), calls=%async_computation.5 | async-start | bytes 368640
  306.5 336.8 %collective-permute-start.9 = (bf16[1152,27]{0,1:T(8,128)(2,1)}, bf16[1152,27]{0,1:T(8,128)(2,1)}, u32[]{:S(2)}, u32[]{:S(2)}) collective-permute-start(bf16[1152,27]{0,1:T(8,128)(2,1)} %slice.108), channel_id=1, source_target_pairs={{0,10},{1,11},{2,12},{3,13},{4,14},{5,15},{6,16},{7,17},{8,18},{9,... | collective-permute-start | bytes 186632
  643.4 38.8 %copy-start.2 = (bf16[2,576,1152]{2,1,0:T(8,128)(2,1)S(1)}, bf16[2,576,1152]{2,1,0:T(8,128)(2,1)}, u32[]{:S(2)}) copy-start(bf16[2,576,1152]{2,1,0:T(8,128)(2,1)} %param.10) | copy-start | bytes 7962628
  643.4 18.4 %collective-permute-start.5 = (bf16[1152,32]{0,1:T(8,128)(2,1)}, bf16[1152,32]{0,1:T(8,128)(2,1)}, u32[]{:S(2)}, u32[]{:S(2)}) collective-permute-start(bf16[1152,32]{0,1:T(8,128)(2,1)} %convert.66), channel_id=1, source_target_pairs={{0,6},{1,7},{2,8},{3,9},{4,10},{5,11},{6,12},{7,13},{8,14},{9,15},... | collective-permute-start | bytes 221192
  645.6 16.3 %collective-permute-start.6 = (bf16[1152,32]{0,1:T(8,128)(2,1)}, bf16[1152,32]{0,1:T(8,128)(2,1)}, u32[]{:S(2)}, u32[]{:S(2)}) collective-permute-start(bf16[1152,32]{0,1:T(8,128)(2,1)} %convert.66), channel_id=1, source_target_pairs={{0,7},{1,8},{2,9},{3,10},{4,11},{5,12},{6,13},{7,14},{8,15},{9,16}... | collective-permute-start | bytes 221192
  647.5 14.3 %collective-permute-start.7 = (bf16[1152,32]{0,1:T(8,128)(2,1)}, bf16[1152,32]{0,1:T(8,128)(2,1)}, u32[]{:S(2)}, u32[]{:S(2)}) collective-permute-start(bf16[1152,32]{0,1:T(8,128)(2,1)} %convert.66), channel_id=1, source_target_pairs={{0,8},{1,9},{2,10},{3,11},{4,12},{5,13},{6,14},{7,15},{8,16},{9,17... | collective-permute-start | bytes 221192
  649.4 12.4 %collective-permute-start.8 = (bf16[1152,32]{0,1:T(8,128)(2,1)}, bf16[1152,32]{0,1:T(8,128)(2,1)}, u32[]{:S(2)}, u32[]{:S(2)}) collective-permute-start(bf16[1152,32]{0,1:T(8,128)(2,1)} %convert.66), channel_id=1, source_target_pairs={{0,9},{1,10},{2,11},{3,12},{4,13},{5,14},{6,15},{7,16},{8,17},{9,1... | collective-permute-start | bytes 221192
  651.3 10.5 %collective-permute-start = (bf16[1152,32]{0,1:T(8,128)(2,1)}, bf16[1152,32]{0,1:T(8,128)(2,1)}, u32[]{:S(2)}, u32[]{:S(2)}) collective-permute-start(bf16[1152,32]{0,1:T(8,128)(2,1)} %convert.66), channel_id=1, source_target_pairs={{0,1},{1,2},{2,3},{3,4},{4,5},{5,6},{6,7},{7,8},{8,9},{9,10},{10,1... | collective-permute-start | bytes 221192
  661.7 71.9 %reduce-scatter.9.cloned.1.call-start = ((), (), s32[]{:S(2)}) async-start(), calls=%async_computation.4 | async-start | bytes 368640
  683.5 55.3 %copy-start.17 = (bf16[1,1,128,576]{2,3,1,0:T(8,128)(2,1)S(1)}, bf16[1,1,128,576]{2,3,1,0:T(8,128)(2,1)}, u32[]{:S(2)}) copy-start(bf16[1,1,128,576]{2,3,1,0:T(8,128)(2,1)} %get-tuple-element.43) | copy-start | bytes 442372
  683.5 55.3 %copy-start.29 = (f32[8,128]{1,0:T(8,128)S(1)}, f32[8,128]{1,0:T(8,128)}, u32[]{:S(2)}) copy-start(f32[8,128]{1,0:T(8,128)} %copy-done.28) | copy-start | bytes 12292
  683.6 56.8 %copy-start.12 = (bf16[1,1,128,576]{2,3,1,0:T(8,128)(2,1)S(1)}, bf16[1,1,128,576]{2,3,1,0:T(8,128)(2,1)}, u32[]{:S(2)}) copy-start(bf16[1,1,128,576]{2,3,1,0:T(8,128)(2,1)} %copy-done.11) | copy-start | bytes 442372
  683.6 56.8 %copy-start.21 = (f32[8,128]{1,0:T(8,128)S(1)}, f32[8,128]{1,0:T(8,128)}, u32[]{:S(2)}) copy-start(f32[8,128]{1,0:T(8,128)} %multiply_divide_fusion.1) | copy-start | bytes 12292
  737.3 4.4 copy-start.18
  740.3 2.6 copy-start.23
  740.3 2.6 copy-start.27
  742.8 3.1 copy-start.33
  742.9 3.1 copy-start.31
Sparse Core Ops, SparseCore 0:
  661.9 36.9 reduce-scatter.10
  701.8 31.7 reduce-scatter.8
where the time goes:
time: 759 us; the launch traced here: 755 us
  blocking collectives  519 us (68%)
  local copies, waits for them, and re-layouts  51.9 us (7%)
  starting transfers between devices  50.4 us (7%)
  waiting for transfers between devices  50.4 us (7%)
  matrix products  38.5 us (5%)
  other arithmetic  28.6 us (4%)
  between operations  16 us (2%)
    unnamed x2, blocking collectives  519 us
    unnamed x14, waiting for transfers between devices  47.5 us
    unnamed x81, local copies, waits for them, and re-layouts  29.9 us
    unnamed x12, starting transfers between devices  25 us
  transfers between devices with their start and end apart: 14, of which 3 were waited for; matrix products, arithmetic and copies ran while one was open for 7% of the time, Pallas kernels for 0%

commit v1 on v0

v1 whole, which is shorter than its diff:
```python
from functools import partial
import math

import jax
import jax.numpy as jnp
import numpy as np
from jax import lax
from jax.experimental import pallas as pl
from jax.experimental.pallas import tpu as pltpu
from jax.sharding import Mesh, PartitionSpec as P

D = 1152
HEADS = 8
HEAD_DIM = 72
HALF = HEAD_DIM // 2
HW = 576
LOC = 128
FRAMES = 64
TOK = 128
SCALE = HEAD_DIM ** (-0.5)
EPS = 1e-06
ROPE_BASE = 10000.0
QKV_COLS = 27
PROJ_ROWS = 9
BLOCK = QKV_COLS + PROJ_ROWS
F32 = jnp.float32
BF16 = jnp.bfloat16

NN = (((1,), (0,)), ((), ()))
NT = (((1,), (1,)), ((), ()))
TN = (((0,), (0,)), ((), ()))


def dot(a, b, dims=NN):
    return lax.dot_general(a, b, dims, preferred_element_type=F32)


def layer_norm(x):
    centered = x - jnp.mean(x, axis=-1, keepdims=True)
    inverse = lax.rsqrt(jnp.mean(centered * centered, axis=-1, keepdims=True) + EPS)
    return centered * inverse, inverse


def layer_norm_back(grad, unit, inverse):
    first = jnp.mean(grad, axis=-1, keepdims=True)
    second = jnp.mean(grad * unit, axis=-1, keepdims=True)
    return inverse * (grad - first - unit * second)


def split_heads(x):
    lane = lax.broadcasted_iota(jnp.int32, (1, HW), 1)
    parts = []
    for h in range(HEADS):
        mine = ((lane >= h * HEAD_DIM) & (lane < (h + 1) * HEAD_DIM)).astype(F32).astype(BF16)
        parts.append(x * mine)
    return jnp.concatenate(parts, axis=0)


def head(x, h):
    return x[:, h * TOK : (h + 1) * TOK]


def rows_of(parts):
    return jnp.concatenate(parts, axis=0)


def lanes_of(parts):
    return jnp.concatenate(parts, axis=1)


def attend(query, keys_by_head, values_by_head, allowed):
    scores = dot(query, keys_by_head, NT)
    probs = []
    for h in range(HEADS):
        s = head(scores, h) * SCALE
        if allowed is not None:
            s = jnp.where(allowed, s, -1e30)
        e = jnp.exp(s - jnp.max(s, axis=-1, keepdims=True))
        probs.append((e / jnp.sum(e, axis=-1, keepdims=True)).astype(BF16))
    return probs, dot(lanes_of(probs), values_by_head).astype(BF16)


def attend_back(probs, attended_grad, query, keys_by_head, values_by_head):
    prob_grads = dot(attended_grad, values_by_head, NT)
    values_grad = dot(rows_of(probs), split_heads(attended_grad), TN)
    score_grads = []
    for h in range(HEADS):
        p = probs[h].astype(F32)
        g = head(prob_grads, h)
        s = p * (g - jnp.sum(g * p, axis=-1, keepdims=True)) * SCALE
        score_grads.append(s.astype(BF16))
    query_grad = dot(lanes_of(score_grads), keys_by_head)
    keys_grad = dot(rows_of(score_grads), split_heads(query), TN)
    return query_grad, keys_grad, values_grad


def swap_halves(x):
    lane = lax.broadcasted_iota(jnp.int32, (1, HW), 1)
    first = lax.rem(lane, HEAD_DIM) < HALF
    later = jnp.concatenate([x[:, HALF:], x[:, :HALF]], axis=1)
    earlier = jnp.concatenate([x[:, HW - HALF :], x[:, : HW - HALF]], axis=1)
    return jnp.where(first, later, earlier)


def spatial_forward_kernel(tokens, mod, qkv_w, out_w, x1, q_out, k_out, v_out, p_out):
    x = tokens[...].reshape(TOK, D).astype(F32)
    unit, _ = layer_norm(x)
    shift, scale, gate = mod[0, 0, 0:1, :], mod[0, 0, 1:2, :], mod[0, 0, 2:3, :]
    normed = (unit * (1.0 + scale) + shift).astype(BF16)
    projected = dot(normed, qkv_w[0])
    q = projected[:, :HW].astype(BF16)
    k = projected[:, HW : 2 * HW].astype(BF16)
    v = projected[:, 2 * HW :].astype(BF16)
    q_out[...] = q
    k_out[...] = k
    v_out[...] = v
    probs, attended = attend(q, split_heads(k), split_heads(v), None)
    for h in range(HEADS):
        p_out[h] = probs[h]
    branch = dot(attended, out_w[0])
    x1[...] = (x + gate * branch).astype(BF16).reshape(FRAMES, 2, D)


def spatial_backward_kernel(grad, tokens, mod, qkv_w, out_w, q_in, k_in, v_in, p_in, result):
    g = grad[...].reshape(TOK, D).astype(F32)
    unit, inverse = layer_norm(tokens[...].reshape(TOK, D).astype(F32))
    scale, gate = mod[0, 0, 1:2, :], mod[0, 0, 2:3, :]
    branch_grad = (gate * g).astype(BF16)
    attended_grad = dot(branch_grad, out_w[0], NT).astype(BF16)
    probs = [p_in[h] for h in range(HEADS)]
    grads = attend_back(probs, attended_grad, q_in[...], split_heads(k_in[...]), split_heads(v_in[...]))
    projected_grad = lanes_of(grads).astype(BF16)
    normed_grad = dot(projected_grad, qkv_w[0], NT).astype(BF16).astype(F32)
    x_grad = layer_norm_back(normed_grad * (1.0 + scale), unit, inverse)
    result[...] = (g + x_grad).astype(BF16).reshape(result.shape)


def branch_grad_kernel(seed, mod, out):
    g = seed[...].reshape(TOK, D).astype(F32)
    out[...] = (mod[0, 0, 2:3, :] * g).astype(BF16)


def temporal_kernel(
    located, seed, cosines, sines, mod, qkv_w, out_w, block_out, x_grad_out, normed_out, factors, wide
):
    x = located[...].reshape(TOK, D).astype(F32)
    unit, inverse = layer_norm(x)
    shift, scale, gate = mod[0, 0, 0:1, :], mod[0, 0, 1:2, :], mod[0, 0, 2:3, :]
    normed = (unit * (1.0 + scale) + shift).astype(BF16)
    normed_out[...] = normed
    projected = dot(normed, qkv_w[0]).astype(BF16).astype(F32)
    cos, sin = cosines[...], sines[...]

    def rotate(t):
        return (t * cos + swap_halves(t) * sin).astype(BF16)

    def rotate_back(t):
        t = t.astype(BF16).astype(F32)
        return t * cos + swap_halves(t * sin)

    q = rotate(projected[:, :HW])
    k = rotate(projected[:, HW : 2 * HW])
    v = projected[:, 2 * HW :].astype(BF16)
    keys_by_head, values_by_head = split_heads(k), split_heads(v)
    row = lax.broadcasted_iota(jnp.int32, (TOK, TOK), 0)
    column = lax.broadcasted_iota(jnp.int32, (TOK, TOK), 1)
    same = lax.rem(row, 2) == lax.rem(column, 2)
    probs, attended = attend(q, keys_by_head, values_by_head, same)
    branch = dot(attended, out_w[0])
    block_out[...] = (x + gate * branch).astype(BF16).reshape(block_out.shape)

    g = seed[...].reshape(TOK, D).astype(F32)
    branch_grad = (gate * g).astype(BF16)
    attended_grad = dot(branch_grad, out_w[0], NT).astype(BF16)
    q_grad, k_grad, v_grad = attend_back(probs, attended_grad, q, keys_by_head, values_by_head)
    grads = lanes_of([rotate_back(q_grad), rotate_back(k_grad), v_grad])
    normed_grad = dot(grads.astype(BF16), qkv_w[0], NT).astype(BF16).astype(F32)
    x_grad = layer_norm_back(normed_grad * (1.0 + scale), unit, inverse)
    x_grad_out[...] = (g + x_grad).astype(BF16).reshape(FRAMES, 2, D)

    wide[: 3 * HW, :] = grads.T
    wide[3 * HW :, :] = attended.astype(F32).T
    for z in range(8):
        parts = [wide[pl.ds((g * 8 + z) * QKV_COLS, QKV_COLS), :] for g in range(8)]
        parts += [wide[pl.ds(3 * HW + (g * 8 + z) * PROJ_ROWS, PROJ_ROWS), :] for g in range(8)]
        factors[z] = jnp.concatenate(parts, axis=0).astype(BF16)


def weight_grad_kernel(core, normed, branch_grad, factors, keep, send):
    left = lanes_of([factors[z] for z in range(8)])
    qkv = dot(left[: 8 * QKV_COLS], normed[...])
    proj = dot(left[8 * QKV_COLS :], branch_grad[...])
    width = D // 4
    first = core[0] == 0
    for x in range(2):
        for g in range(8):
            rows = jnp.concatenate(
                [qkv[g * QKV_COLS : (g + 1) * QKV_COLS], proj[g * PROJ_ROWS : (g + 1) * PROJ_ROWS]], axis=0
            )
            a = rows[:, (2 * x) * width : (2 * x + 1) * width]
            b = rows[:, (2 * x + 1) * width : (2 * x + 2) * width]
            keep[x * 8 + g] = jnp.where(first, a, b)
            send[x * 8 + g] = jnp.where(first, b, a).astype(BF16)


def vmem(n):
    return [pl.BlockSpec(memory_space=pltpu.VMEM)] * n


def sub(s):
    return [
        pl.BlockSpec((1, 1, 3, D), lambda i: (0, s, 0, 0)),
        pl.BlockSpec((1, D, 3 * HW), lambda i: (s, 0, 0)),
        pl.BlockSpec((1, HW, D), lambda i: (s, 0, 0)),
    ]


def whole(*shape):
    return pl.BlockSpec(shape, lambda i: (0,) * len(shape))


def params(mib):
    return pltpu.CompilerParams(vmem_limit_bytes=mib * 2**20)


def shards(tokens, modulation, frame_pos, qkv_weight, out_weight, seed_grad):
    shape = jax.ShapeDtypeStruct
    seed = seed_grad.reshape(FRAMES, 2, D)
    tokens = tokens.reshape(TOK, D)

    branch_grad = pl.pallas_call(
        branch_grad_kernel,
        grid=(1,),
        out_shape=shape((TOK, D), BF16),
        in_specs=[whole(FRAMES, 2, D), sub(1)[0]],
        out_specs=whole(TOK, D),
        compiler_params=params(16),
        name="branch_grad",
    )(seed, modulation)
    branch_all = lax.all_gather(branch_grad, "z", tiled=True)

    x1, q, k, v, p = pl.pallas_call(
        spatial_forward_kernel,
        grid=(1,),
        out_shape=(
            shape((FRAMES, 2, D), BF16),
            shape((TOK, HW), BF16),
            shape((TOK, HW), BF16),
            shape((TOK, HW), BF16),
            shape((HEADS, TOK, TOK), BF16),
        ),
        in_specs=[whole(TOK, D), *sub(0)],
        out_specs=(whole(FRAMES, 2, D), whole(TOK, HW), whole(TOK, HW), whole(TOK, HW), whole(HEADS, TOK, TOK)),
        compiler_params=params(40),
        name="spatial_forward",
    )(tokens, modulation, qkv_weight, out_weight)

    seq = ("y", "xl", "z")
    located = lax.all_to_all(x1, seq, split_axis=0, concat_axis=0, tiled=True)

    frequency = jnp.exp(jnp.arange(HALF, dtype=F32) * (-2.0 * math.log(ROPE_BASE) / HEAD_DIM))
    lane_frequency = jnp.tile(frequency, 2 * HEADS)
    angles = jnp.repeat(frame_pos.astype(F32), 2)[:, None] * lane_frequency[None, :]
    sign = np.tile(np.repeat(np.array([-1.0, 1.0], np.float32), HALF), HEADS)
    cosines = jnp.cos(angles)
    sines = jnp.sin(angles) * sign[None, :]

    block_out, located_grad, normed, factors = pl.pallas_call(
        temporal_kernel,
        grid=(1,),
        out_shape=(
            shape((FRAMES, 2, D), BF16),
            shape((FRAMES, 2, D), BF16),
            shape((TOK, D), BF16),
            shape((8, 8 * BLOCK, TOK), BF16),
        ),
        in_specs=[whole(FRAMES, 2, D), whole(FRAMES, 2, D), whole(TOK, HW), whole(TOK, HW), *sub(1)],
        out_specs=(whole(FRAMES, 2, D), whole(FRAMES, 2, D), whole(TOK, D), whole(8, 8 * BLOCK, TOK)),
        scratch_shapes=[pltpu.VMEM((4 * HW, TOK), F32)],
        compiler_params=params(48),
        name="temporal",
    )(located, seed, cosines, sines, modulation, qkv_weight, out_weight)

    normed_all = lax.all_gather(normed, "z", tiled=True)
    framed_grad = lax.all_to_all(located_grad, seq, split_axis=0, concat_axis=0, tiled=True)

    tokens_grad = pl.pallas_call(
        spatial_backward_kernel,
        grid=(1,),
        out_shape=shape((TOK, D), BF16),
        in_specs=[
            whole(FRAMES, 2, D),
            whole(TOK, D),
            *sub(0),
            whole(TOK, HW),
            whole(TOK, HW),
            whole(TOK, HW),
            whole(HEADS, TOK, TOK),
        ],
        out_specs=whole(TOK, D),
        compiler_params=params(48),
        name="spatial_backward",
    )(framed_grad, tokens, modulation, qkv_weight, out_weight, q, k, v, p)

    factors = lax.all_to_all(factors, "z", split_axis=0, concat_axis=0, tiled=True)
    core = lax.axis_index("core").reshape(1).astype(jnp.int32)
    keep, send = pl.pallas_call(
        weight_grad_kernel,
        out_shape=(shape((16, BLOCK, D // 4), F32), shape((16, BLOCK, D // 4), BF16)),
        in_specs=[pl.BlockSpec(memory_space=pltpu.SMEM), *vmem(3)],
        out_specs=tuple(vmem(2)),
        compiler_params=params(40),
        name="weight_grad",
    )(core, normed_all, branch_all, factors)
    received = lax.ppermute(send, "core", [(0, 1), (1, 0)])
    both = (keep + received.astype(F32)).astype(BF16)
    parts = lax.all_to_all(both, ("xh", "y", "xl"), split_axis=0, concat_axis=0, tiled=True)
    total = jnp.sum(parts.astype(F32), axis=0)
    return (
        block_out.reshape(1, FRAMES, 2, D),
        tokens_grad.reshape(1, 1, LOC, D),
        total[:QKV_COLS].T,
        total[QKV_COLS:],
    )


def solution(mesh):
    sizes = (2, 2, 4, 2, 8)
    split = Mesh(mesh.devices.reshape(sizes), ("xh", "core", "y", "xl", "z"))
    dp, seq = ("xh", "core"), ("y", "xl", "z")
    return jax.shard_map(
        shards,
        mesh=split,
        in_specs=(
            P(dp, seq, None, None),
            P(dp, None, None, None),
            P(),
            P(),
            P(),
            P(dp, None, seq, None),
        ),
        out_specs=(
            P(dp, None, seq, None),
            P(dp, seq, None, None),
            P(dp, seq),
            P(seq, dp),
        ),
        check_vma=False,
    )
```

time: 759 us -> 173 us (0.23)
  blocking collectives: 519 us -> 0 us
  matrix products: 38.5 us -> 0 us
  other arithmetic: 28.6 us -> 4.56 us
  Pallas kernels: 0 us -> 23.4 us
  local copies, waits for them, and re-layouts: 51.9 us -> 31.5 us
  starting transfers between devices: 50.4 us -> 30.4 us
  waiting for transfers between devices: 50.4 us -> 67.8 us
    unnamed x2 -> x0, blocking collectives: 519 us -> none
    unnamed x14 -> x2, waiting for transfers between devices: 47.5 us -> 0.03 us
    all_to_all x2 -> x4, waiting for transfers between devices: 2.96 us -> 49.7 us  [the longest x1 21.1 us: shards(): lax.all_to_all(factors, 'z', split_axis=0, concat_axis=0, tiled=True)]
    dot_general x20 -> x0, matrix products: 34.5 us -> none  [the longest x2 7.16 us: sublayer_forward(): jnp.dot(normed, qkv_weight, preferred_element_type=jnp.float32)]
    unnamed x12 -> x0, starting transfers between devices: 25 us -> none
    pallas_call x0 -> x5, Pallas kernels: none -> 23.4 us  [the longest x1 8.91 us: shards(): pl.pallas_call(temporal_kernel, grid=(1,), out_shape=(shape((FRAMES, 2, D...]
    all_gather x0 -> x2, waiting for transfers between devices: none -> 18.1 us  [the longest x1 18.1 us: shards(): normed_all = lax.all_gather(normed, 'z', tiled=True)]
    convert_element_type x12 -> x2, other arithmetic: 13.3 us -> 2.21 us  [the longest x1 2.2 us: shards(): both = (keep + received.astype(F32)).astype(BF16)]
  transfers between devices with their start and end apart: 14 -> 7, of which waited for: 3 -> 5; matrix products, arithmetic and copies ran while one was open for 7% -> 9% of each run, Pallas kernels for 0% -> 11%
where the time goes in v1:
time: 173 us; the launch traced here: 172 us
  waiting for transfers between devices  67.8 us (39%)
  local copies, waits for them, and re-layouts  31.5 us (18%)
  starting transfers between devices  30.4 us (18%)
  Pallas kernels  23.4 us (14%)
  between operations  14.2 us (8%)
  other arithmetic  4.56 us (3%)
    unnamed x46, local copies, waits for them, and re-layouts  29.9 us
    all_to_all x1, waiting for transfers between devices, shards(): lax.all_to_all(factors, 'z', split_axis=0, concat_axis=0, tiled=True)  21.1 us
    all_gather x1, waiting for transfers between devices, shards(): normed_all = lax.all_gather(normed, 'z', tiled=True)  18.1 us
    all_to_all x1, waiting for transfers between devices, shards(): located = lax.all_to_all(x1, seq, split_axis=0, concat_axis=0, tiled=True)  15.1 us
    all_to_all x1, starting transfers between devices, shards(): located = lax.all_to_all(x1, seq, split_axis=0, concat_axis=0, tiled=True)  12.9 us
    all_to_all x1, waiting for transfers between devices, shards(): lax.all_to_all(located_grad, seq, split_axis=0, concat_axis=0, tiled=True)  12 us
    pallas_call x1, Pallas kernels, shards(): pl.pallas_call(temporal_kernel, grid=(1,), out_shape=(shape((FRAMES, 2, D...  8.91 us
    all_to_all x1, starting transfers between devices, shards(): lax.all_to_all(located_grad, seq, split_axis=0, concat_axis=0, tiled=True)  8.24 us
  transfers between devices with their start and end apart: 7, of which 5 were waited for; matrix products, arithmetic and copies ran while one was open for 9% of the time, Pallas kernels for 11%

profile of v1, /device:TPU:32, one launch (start us, length us, event | category | flops | bytes accessed | tf_op | source)
XLA Modules:
  0.0 171.8 jit_solution(3489032030223679439)
XLA Ops:
  7.2 0.0 all-gather.5.cloned.1.call-start
  7.2 0.8 copy.18.mod
  8.0 0.0 copy-start.6
  8.0 1.0 copy-done.6
  8.9 0.8 branch_grad.1
  9.8 0.0 all-gather.5.cloned.1.call-update
  9.8 0.0 copy-start.1
  9.8 0.0 copy-start.4
  9.8 11.7 %copy.19.qkv_w = bf16[2,1152,1728]{2,1,0:T(8,128)(2,1)} copy(bf16[2,1152,1728]{1,2,0:T(8,128)(2,1)} %param.10) | data formatting | bytes 15925248 | tf_op args[3]
  21.5 0.0 copy-done.1
  21.5 0.0 copy-done.4
  21.5 0.0 copy-start
  21.5 3.4 %copy-done = bf16[2,1152,1728]{2,1,0:T(8,128)(2,1)S(1)} copy-done((bf16[2,1152,1728]{2,1,0:T(8,128)(2,1)S(1)}, bf16[2,1152,1728]{2,1,0:T(8,128)(2,1)}, u32[]{:S(2)}) %copy-start) | copy-done | bytes 7962648
  25.0 0.0 copy-start.21
  25.0 0.0 copy-start.20
  25.0 3.1 %spatial_forward.1 = (bf16[64,2,1152]{2,1,0:T(2,128)(2,1)}, bf16[128,576]{1,0:T(8,128)(2,1)S(1)}, bf16[128,576]{1,0:T(8,128)(2,1)S(1)}, bf16[128,576]{1,0:T(8,128)(2,1)S(1)}, bf16[8,128,128]{2,1,0:T(8,128)(2,1)S(1)}) custom-call(bf16[128,1152]{1,0:T(8,128)(2,1)S(1)} %bitcast.7, f32[1,2,3,1152]{3,2,1,0:T(4,128)S(1)} %copy.18.mod, ...), custom_call_target="tpu_custom_call" | custom-call | tf_op jit(solution)/shard_map/spatial_forward/pallas_call | solution.py:242
  28.1 0.0 copy-start.12
  28.1 0.7 copy-done.12
  28.8 0.0 copy-start.14
  28.8 0.7 copy-done.14
  29.4 0.0 copy-start.16
  29.4 0.7 copy-done.16
  30.1 0.0 copy-start.18
  30.1 0.7 copy-done.18
  30.8 12.9 %all-to-all-start = ((bf16[64,2,1152]{2,1,0:T(2,128)(2,1)}), bf16[64,2,1152]{2,1,0:T(2,128)(2,1)}, u32[]{:S(2)}, u32[]{:S(2)}) async-start(bf16[64,2,1152]{2,1,0:T(2,128)(2,1)} %get-tuple-element.15), calls=%async_computation | async-start | bytes 589824 | tf_op jit(solution)/shard_map/all_to_all | solution.py:259
  43.6 0.0 all-gather.3.cloned.1.call-start
  43.7 0.1 mul.41
  43.8 0.0 copy-done.21
  43.8 0.1 broadcast_in_dim.3
  43.9 0.1 mul.37
  44.0 0.0 copy-done.20
  44.1 1.2 fusion
  45.3 15.1 %all-to-all-done.located = bf16[64,2,1152]{2,1,0:T(2,128)(2,1)} async-done(((bf16[64,2,1152]{2,1,0:T(2,128)(2,1)}), bf16[64,2,1152]{2,1,0:T(2,128)(2,1)}, u32[]{:S(2)}, u32[]{:S(2)}) %all-to-all-start) | async-done | bytes 294944 | tf_op jit(solution)/shard_map/all_to_all | solution.py:259
  60.4 1.0 copy-done.7
  61.3 8.9 %temporal.1 = (bf16[64,2,1152]{2,1,0:T(2,128)(2,1)}, bf16[64,2,1152]{2,1,0:T(2,128)(2,1)S(1)}, bf16[128,1152]{1,0:T(8,128)(2,1)S(1)}, bf16[8,288,128]{2,1,0:T(8,128)(2,1)S(1)}) custom-call(bf16[64,2,1152]{2,1,0:T(2,128)(2,1)} %all-to-all-done.located, bf16[64,2,1152]{2,1,0:T(2,128)(2,1)S(1)} %bitcast.10, f32[128,576]{1,0:T(8,128)S(1)} %get-tuple-element.27.cosines, ...), custom_call_target="tpu_custom_call" | custom-call | tf_op jit(solution)/shard_map/temporal/pallas_call | solution.py:268
  70.2 0.0 copy-start.9
  70.3 0.8 copy-done.9
  71.1 0.7 copy-done.10
  71.8 0.7 copy-done.11
  72.5 0.0 all-gather.3.cloned.1.call-update
  72.5 4.7 %all-to-all-start.2 = ((bf16[8,288,128]{2,1,0:T(8,128)(2,1)}), bf16[8,288,128]{2,1,0:T(8,128)(2,1)S(1)}, u32[]{:S(2)}, u32[]{:S(2)}) async-start(bf16[8,288,128]{2,1,0:T(8,128)(2,1)} %copy-done.9), calls=%async_computation.2 | async-start | bytes 1179648 | tf_op jit(solution)/shard_map/all_to_all | solution.py:305
  77.2 21.1 %all-to-all-done.2.factors = bf16[8,288,128]{2,1,0:T(8,128)(2,1)S(1)} async-done(((bf16[8,288,128]{2,1,0:T(8,128)(2,1)}), bf16[8,288,128]{2,1,0:T(8,128)(2,1)S(1)}, u32[]{:S(2)}, u32[]{:S(2)}) %all-to-all-start.2) | async-done | bytes 589856 | tf_op jit(solution)/shard_map/all_to_all | solution.py:305
  98.3 18.1 %all-gather.3.cloned.1.call-done.normed = bf16[1024,1152]{1,0:T(8,128)(2,1)} async-done(((bf16[128,1152]{1,0:T(8,128)(2,1)}), bf16[1024,1152]{1,0:T(8,128)(2,1)}) %all-gather.3.cloned.1.call-update) | async-done | bytes 2359312 | tf_op jit(solution)/shard_map/all_gather | solution.py:284
  116.4 1.7 copy-done.2
  118.1 1.7 copy-done.3
  119.7 4.4 %weight_grad.1 = (f32[16,36,288]{2,1,0:T(8,128)S(1)}, bf16[16,36,288]{2,1,0:T(8,128)(2,1)}) custom-call(s32[1]{0:T(128)} %bitcast.4.core, bf16[1024,1152]{1,0:T(8,128)(2,1)S(1)} %copy-done.3, bf16[1024,1152]{1,0:T(8,128)(2,1)S(1)} %copy-done.2, bf16[8,288,128]{2,1,0:T(8,128)(2,1)S(1)} %all-to-all-done.2.factors), custom_call_target="tpu_custom_call" | custom-call | tf_op jit(solution)/shard_map/weight_grad/pallas_call | solution.py:307
  124.1 1.0 copy-done.8
  125.2 0.0 collective-permute-start
  125.2 8.2 %all-to-all-start.1 = ((bf16[64,2,1152]{2,1,0:T(2,128)(2,1)}), bf16[64,2,1152]{2,1,0:T(2,128)(2,1)S(1)}, u32[]{:S(2)}, u32[]{:S(2)}) async-start(bf16[64,2,1152]{2,1,0:T(2,128)(2,1)} %copy-done.10), calls=%async_computation.1 | async-start | bytes 589824 | tf_op jit(solution)/shard_map/all_to_all | solution.py:285
  133.4 0.0 collective-permute-done
  133.4 2.2 %add_convert_fusion = bf16[16,36,288]{2,1,0:T(8,128)(2,1)} fusion(f32[16,36,288]{2,1,0:T(8,128)} %copy-done.8, bf16[16,36,288]{2,1,0:T(8,128)(2,1)} %collective-permute-done), kind=kLoop, calls=%fused_computation.1 | loop fusion | flops 497664 | bytes 1327104 | tf_op jit(solution)/shard_map/convert_element_type | solution.py:316
  135.6 12.0 %all-to-all-done.1.grad = bf16[64,2,1152]{2,1,0:T(2,128)(2,1)S(1)} async-done(((bf16[64,2,1152]{2,1,0:T(2,128)(2,1)}), bf16[64,2,1152]{2,1,0:T(2,128)(2,1)S(1)}, u32[]{:S(2)}, u32[]{:S(2)}) %all-to-all-start.1) | async-done | bytes 294944 | tf_op jit(solution)/shard_map/all_to_all | solution.py:285
  147.6 4.5 %all-to-all-start.3 = ((bf16[16,36,288]{2,1,0:T(8,128)(2,1)}), bf16[16,36,288]{2,1,0:T(8,128)(2,1)}, u32[]{:S(2)}, u32[]{:S(2)}) async-start(bf16[16,36,288]{2,1,0:T(8,128)(2,1)} %add_convert_fusion), calls=%async_computation.3 | async-start | bytes 983040 | tf_op jit(solution)/shard_map/all_to_all | solution.py:317
  152.2 0.0 copy-done.5
  152.2 0.0 copy-done.13
  152.2 0.0 copy-start.15
  152.2 0.9 copy-done.15
  153.1 0.9 copy-done.17
  154.0 0.9 copy-done.19
  154.9 6.2 %spatial_backward.1 = bf16[128,1152]{1,0:T(8,128)(2,1)} custom-call(bf16[64,2,1152]{2,1,0:T(2,128)(2,1)S(1)} %all-to-all-done.1.grad, bf16[128,1152]{1,0:T(8,128)(2,1)S(1)} %bitcast.8, f32[1,2,3,1152]{3,2,1,0:T(4,128)S(1)} %copy.18.mod, bf16[2,1152,1728]{2,1,0:T(8,128)(2,1)} %copy.19.qkv_w, bf16[2,576,1152]{2,1,0:T(8,128)(2,1)S(1)} %copy-done.1, ...), custom_call_target="tpu_custom_call" | custom-call | tf_op jit(solution)/shard_map/spatial_backward/pallas_call | solution.py:287
  161.1 1.5 all-to-all-done.3
  162.6 1.1 convert_reduce_fusion
  163.7 0.6 slice_bitcast_fusion
  164.3 0.6 slice.9
  (14 shorter events, 0.0 us)
Async XLA Ops:
  7.2 91.1 %all-gather.5.cloned.1.call-start = ((), (), s32[]{:S(2)}) async-start(), calls=%async_computation.5 | async-start | bytes 2654208 | tf_op jit(solution)/shard_map/all_gather | solution.py:240
  8.0 1.0 copy-start.6
  9.8 11.8 %copy-start.1 = (bf16[2,576,1152]{2,1,0:T(8,128)(2,1)S(1)}, bf16[2,576,1152]{2,1,0:T(8,128)(2,1)}, u32[]{:S(2)}) copy-start(bf16[2,576,1152]{2,1,0:T(8,128)(2,1)} %out_w.5) | copy-start | bytes 7962628
  9.8 11.7 %copy-start.4 = (bf16[1,1,128,1152]{3,2,1,0:T(8,128)(2,1)S(1)}, bf16[1,1,128,1152]{3,2,1,0:T(8,128)(2,1)}, u32[]{:S(2)}) copy-start(bf16[1,1,128,1152]{3,2,1,0:T(8,128)(2,1)} %param.7) | copy-start | bytes 884740
  21.5 3.4 %copy-start = (bf16[2,1152,1728]{2,1,0:T(8,128)(2,1)S(1)}, bf16[2,1152,1728]{2,1,0:T(8,128)(2,1)}, u32[]{:S(2)}) copy-start(bf16[2,1152,1728]{2,1,0:T(8,128)(2,1)} %copy.19.qkv_w) | copy-start | bytes 23887876
  25.0 18.8 %copy-start.21 = (s32[64]{0:T(128)S(1)}, s32[64]{0:T(128)}, u32[]{:S(2)}) copy-start(s32[64]{0:T(128)} %param.9) | copy-start | bytes 772
  25.0 19.1 %copy-start.20 = (f32[576]{0:T(1024)S(1)}, f32[576]{0:T(1024)}, u32[]{:S(2)}) copy-start(f32[576]{0:T(1024)} %constant.16) | copy-start | bytes 6916
  28.1 0.7 copy-start.12
  28.8 0.7 copy-start.14
  29.4 0.7 copy-start.16
  30.1 0.7 copy-start.18
  30.8 29.6 %all-to-all-start = ((bf16[64,2,1152]{2,1,0:T(2,128)(2,1)}), bf16[64,2,1152]{2,1,0:T(2,128)(2,1)}, u32[]{:S(2)}, u32[]{:S(2)}) async-start(bf16[64,2,1152]{2,1,0:T(2,128)(2,1)} %get-tuple-element.15), calls=%async_computation | async-start | bytes 589824 | tf_op jit(solution)/shard_map/all_to_all | solution.py:259
  43.6 72.8 %all-gather.3.cloned.1.call-start = ((), (), s32[]{:S(2)}) async-start(), calls=%async_computation.4 | async-start | bytes 2654208 | tf_op jit(solution)/shard_map/all_gather | solution.py:284
  60.4 1.0 copy-start.7
  70.2 0.8 copy-start.9
  71.1 0.7 copy-start.10
  71.8 0.7 copy-start.11
  72.5 25.8 %all-to-all-start.2 = ((bf16[8,288,128]{2,1,0:T(8,128)(2,1)}), bf16[8,288,128]{2,1,0:T(8,128)(2,1)S(1)}, u32[]{:S(2)}, u32[]{:S(2)}) async-start(bf16[8,288,128]{2,1,0:T(8,128)(2,1)} %copy-done.9), calls=%async_computation.2 | async-start | bytes 1179648 | tf_op jit(solution)/shard_map/all_to_all | solution.py:305
  116.4 1.7 copy-start.2
  118.1 1.7 copy-start.3
  124.1 1.0 copy-start.8
  125.2 27.0 %copy-start.5 = (bf16[1,1,128,1152]{3,2,1,0:T(8,128)(2,1)S(1)}, bf16[1,1,128,1152]{3,2,1,0:T(8,128)(2,1)}, u32[]{:S(2)}) copy-start(bf16[1,1,128,1152]{3,2,1,0:T(8,128)(2,1)} %param.7) | copy-start | bytes 884740
  125.2 27.0 %copy-start.13 = (bf16[8,128,128]{2,1,0:T(8,128)(2,1)S(1)}, bf16[8,128,128]{2,1,0:T(8,128)(2,1)}, u32[]{:S(2)}) copy-start(bf16[8,128,128]{2,1,0:T(8,128)(2,1)} %copy-done.12) | copy-start | bytes 786436
  125.2 8.3 %collective-permute-start = (bf16[16,36,288]{2,1,0:T(8,128)(2,1)}, bf16[16,36,288]{2,1,0:T(8,128)(2,1)}, u32[]{:S(2)}, u32[]{:S(2)}) collective-permute-start(bf16[16,36,288]{2,1,0:T(8,128)(2,1)} %get-tuple-element.25), channel_id=1, source_target_pairs={{0,64},{64,0},{1,65},{65,1},{2,66},{66,2},{3,67},{67,3},{4,68},{68... | collective-permute-start | bytes 995336 | tf_op jit(solution)/shard_map/ppermute | solution.py:315
  125.2 22.5 %all-to-all-start.1 = ((bf16[64,2,1152]{2,1,0:T(2,128)(2,1)}), bf16[64,2,1152]{2,1,0:T(2,128)(2,1)S(1)}, u32[]{:S(2)}, u32[]{:S(2)}) async-start(bf16[64,2,1152]{2,1,0:T(2,128)(2,1)} %copy-done.10), calls=%async_computation.1 | async-start | bytes 589824 | tf_op jit(solution)/shard_map/all_to_all | solution.py:285
  147.6 15.0 %all-to-all-start.3 = ((bf16[16,36,288]{2,1,0:T(8,128)(2,1)}), bf16[16,36,288]{2,1,0:T(8,128)(2,1)}, u32[]{:S(2)}, u32[]{:S(2)}) async-start(bf16[16,36,288]{2,1,0:T(8,128)(2,1)} %add_convert_fusion), calls=%async_computation.3 | async-start | bytes 983040 | tf_op jit(solution)/shard_map/all_to_all | solution.py:317
  152.2 0.9 copy-start.15
  153.1 0.9 copy-start.17
  154.0 0.9 copy-start.19
Sparse Core Ops, SparseCore 0:
  9.9 48.7 all-gather.4
  72.6 43.7 all-gather.2

commit v2 on v1

v2 whole, which is shorter than its diff:
```python
from functools import partial
import math

import jax
import jax.numpy as jnp
import numpy as np
from jax import lax
from jax.experimental import pallas as pl
from jax.experimental.pallas import tpu as pltpu
from jax.sharding import Mesh, PartitionSpec as P

D = 1152
HEADS = 8
HEAD_DIM = 72
HALF = HEAD_DIM // 2
HW = 576
LOC = 128
FRAMES = 64
TOK = 128
SCALE = HEAD_DIM ** (-0.5)
EPS = 1e-06
ROPE_BASE = 10000.0
QKV_COLS = 27
PROJ_ROWS = 9
BLOCK = 40
Y = 4
PARTS = 16
WIDTH = D // 4
F32 = jnp.float32
BF16 = jnp.bfloat16

NN = (((1,), (0,)), ((), ()))
NT = (((1,), (1,)), ((), ()))
TN = (((0,), (0,)), ((), ()))


def dot(a, b, dims=NN):
    return lax.dot_general(a, b, dims, preferred_element_type=F32)


def layer_norm(x):
    centered = x - jnp.mean(x, axis=-1, keepdims=True)
    inverse = lax.rsqrt(jnp.mean(centered * centered, axis=-1, keepdims=True) + EPS)
    return centered * inverse, inverse


def layer_norm_back(grad, unit, inverse):
    first = jnp.mean(grad, axis=-1, keepdims=True)
    second = jnp.mean(grad * unit, axis=-1, keepdims=True)
    return inverse * (grad - first - unit * second)


def split_heads(x):
    lane = lax.broadcasted_iota(jnp.int32, (1, HW), 1)
    parts = []
    for h in range(HEADS):
        mine = ((lane >= h * HEAD_DIM) & (lane < (h + 1) * HEAD_DIM)).astype(F32).astype(BF16)
        parts.append(x * mine)
    return jnp.concatenate(parts, axis=0)


def head(x, h):
    return x[:, h * TOK : (h + 1) * TOK]


def rows_of(parts):
    return jnp.concatenate(parts, axis=0)


def lanes_of(parts):
    return jnp.concatenate(parts, axis=1)


def attend(query, keys_by_head, values_by_head, allowed):
    scores = dot(query, keys_by_head, NT)
    probs = []
    for h in range(HEADS):
        s = head(scores, h) * SCALE
        if allowed is not None:
            s = jnp.where(allowed, s, -1e30)
        e = jnp.exp(s - jnp.max(s, axis=-1, keepdims=True))
        probs.append((e / jnp.sum(e, axis=-1, keepdims=True)).astype(BF16))
    return probs, dot(lanes_of(probs), values_by_head).astype(BF16)


def attend_back(probs, attended_grad, query, keys_by_head, values_by_head):
    prob_grads = dot(attended_grad, values_by_head, NT)
    values_grad = dot(rows_of(probs), split_heads(attended_grad), TN)
    score_grads = []
    for h in range(HEADS):
        p = probs[h].astype(F32)
        g = head(prob_grads, h)
        s = p * (g - jnp.sum(g * p, axis=-1, keepdims=True)) * SCALE
        score_grads.append(s.astype(BF16))
    query_grad = dot(lanes_of(score_grads), keys_by_head)
    keys_grad = dot(rows_of(score_grads), split_heads(query), TN)
    return query_grad, keys_grad, values_grad


def swap_halves(x):
    lane = lax.broadcasted_iota(jnp.int32, (1, HW), 1)
    first = lax.rem(lane, HEAD_DIM) < HALF
    later = jnp.concatenate([x[:, HALF:], x[:, :HALF]], axis=1)
    earlier = jnp.concatenate([x[:, HW - HALF :], x[:, : HW - HALF]], axis=1)
    return jnp.where(first, later, earlier)


def fetch(pairs, sems):
    copies = [pltpu.make_async_copy(src, dst, sems.at[i]) for i, (src, dst) in enumerate(pairs)]
    for c in copies:
        c.start()
    return copies


def store(pairs, sems):
    return fetch(pairs, sems)


def wait_all(copies):
    for c in copies:
        c.wait()


def regroup(x):
    main = [x[:, d * WIDTH : d * WIDTH + 256] for d in range(4)]
    tail = [x[:, d * WIDTH + 256 : (d + 1) * WIDTH] for d in range(4)]
    return jnp.concatenate(main + tail, axis=1)


def branch_grad_kernel(seed, mod, out):
    g = seed[...].reshape(TOK, D).astype(F32)
    out[...] = regroup((mod[0, 2, 1:2, :] * g).astype(BF16))


def temporal_normed_kernel(located, mod, out):
    unit, _ = layer_norm(located[...].reshape(TOK, D).astype(F32))
    out[...] = regroup((unit * (1.0 + mod[0, 1, 1:2, :]) + mod[0, 0, 1:2, :]).astype(BF16))


def spatial_forward_kernel(
    tokens, mod, qkv_w, out_w, x1, q_out, k_out, v_out, p_out,
    tokens_v, mod_v, w_v, o_v, x1_v, q_v, k_v, v_v, p_v, in_sem, out_sem,
):
    copies = fetch(
        [(tokens, tokens_v), (mod, mod_v)]
        + [(qkv_w.at[0, pl.ds(i * HW, HW)], w_v.at[pl.ds(i * HW, HW)]) for i in range(3)]
        + [(out_w.at[0], o_v)],
        in_sem,
    )
    wait_all(copies[:2])
    x = tokens_v[...].astype(F32)
    unit, _ = layer_norm(x)
    shift, scale, gate = mod_v[0, 0, 0:1, :], mod_v[0, 1, 0:1, :], mod_v[0, 2, 0:1, :]
    normed = (unit * (1.0 + scale) + shift).astype(BF16)
    parts = []
    for i, out in enumerate((q_v, k_v, v_v)):
        copies[2 + i].wait()
        part = dot(normed, w_v[i * HW : (i + 1) * HW, :], NT).astype(BF16)
        out[...] = part
        parts.append(part)
    q, k, v = parts
    saves = store([(q_v, q_out), (k_v, k_out), (v_v, v_out)], out_sem)
    probs, attended = attend(q, split_heads(k), split_heads(v), None)
    for h in range(HEADS):
        p_v[h] = probs[h]
    save_p = pltpu.make_async_copy(p_v, p_out, out_sem.at[3])
    save_p.start()
    copies[5].wait()
    branch = dot(attended, o_v[...])
    x1_v[...] = (x + gate * branch).astype(BF16).reshape(FRAMES, 2, D)
    save_x = pltpu.make_async_copy(x1_v, x1, out_sem.at[4])
    save_x.start()
    wait_all(saves + [save_p, save_x])


def spatial_attention_back_kernel(
    grad, mod, out_w, q_in, k_in, v_in, p_in, result,
    grad_v, mod_v, o_v, q_v, k_v, v_v, p_v, result_v, in_sem, out_sem,
):
    copies = fetch(
        [(grad, grad_v), (mod, mod_v), (out_w.at[0], o_v), (v_in, v_v), (p_in, p_v), (k_in, k_v), (q_in, q_v)], in_sem
    )
    wait_all(copies)
    g = grad_v[...].reshape(TOK, D).astype(F32)
    branch_grad = (mod_v[0, 2, 0:1, :] * g).astype(BF16)
    attended_grad = dot(branch_grad, o_v[...], NT).astype(BF16)
    probs = [p_v[h] for h in range(HEADS)]
    grads = attend_back(probs, attended_grad, q_v[...], split_heads(k_v[...]), split_heads(v_v[...]))
    result_v[...] = lanes_of(grads).astype(BF16)
    save = pltpu.make_async_copy(result_v, result, out_sem)
    save.start()
    save.wait()


def spatial_input_back_kernel(
    grad, tokens, mod, qkv_w, projected_grad, result,
    grad_v, tokens_v, mod_v, w_v, p_v, result_v, in_sem, out_sem,
):
    copies = fetch([(projected_grad, p_v), (qkv_w.at[0], w_v), (tokens, tokens_v), (mod, mod_v), (grad, grad_v)], in_sem)
    wait_all(copies)
    g = grad_v[...].reshape(TOK, D).astype(F32)
    unit, inverse = layer_norm(tokens_v[...].astype(F32))
    normed_grad = dot(p_v[...], w_v[...]).astype(BF16).astype(F32)
    x_grad = layer_norm_back(normed_grad * (1.0 + mod_v[0, 1, 0:1, :]), unit, inverse)
    result_v[...] = (g + x_grad).astype(BF16)
    save = pltpu.make_async_copy(result_v, result, out_sem)
    save.start()
    save.wait()


def temporal_kernel(
    located, seed, cosines, sines, mod, qkv_w, out_w, block_out, x_grad_out, factors,
    located_v, seed_v, cos_v, sin_v, mod_v, w_v, o_v, block_v, x_grad_v, factors_v, wide, in_sem, out_sem,
):
    copies = fetch(
        [(located, located_v), (mod, mod_v)]
        + [(qkv_w.at[1, pl.ds(i * HW, HW)], w_v.at[pl.ds(i * HW, HW)]) for i in range(3)]
        + [(cosines, cos_v), (sines, sin_v), (out_w.at[1], o_v), (seed, seed_v)],
        in_sem,
    )
    wait_all(copies[:2])
    x = located_v[...].reshape(TOK, D).astype(F32)
    unit, inverse = layer_norm(x)
    shift, scale, gate = mod_v[0, 0, 1:2, :], mod_v[0, 1, 1:2, :], mod_v[0, 2, 1:2, :]
    normed = (unit * (1.0 + scale) + shift).astype(BF16)
    parts = []
    for i in range(3):
        copies[2 + i].wait()
        parts.append(dot(normed, w_v[i * HW : (i + 1) * HW, :], NT).astype(BF16))
    wait_all(copies[5:7])
    cos, sin = cos_v[...], sin_v[...]

    def rotate(t):
        t = t.astype(F32)
        return (t * cos + swap_halves(t) * sin).astype(BF16)

    def rotate_back(t):
        t = t.astype(BF16).astype(F32)
        return t * cos + swap_halves(t * sin)

    q, k, v = rotate(parts[0]), rotate(parts[1]), parts[2]
    keys_by_head, values_by_head = split_heads(k), split_heads(v)
    row = lax.broadcasted_iota(jnp.int32, (TOK, TOK), 0)
    column = lax.broadcasted_iota(jnp.int32, (TOK, TOK), 1)
    same = lax.rem(row, 2) == lax.rem(column, 2)
    probs, attended = attend(q, keys_by_head, values_by_head, same)
    copies[7].wait()
    branch = dot(attended, o_v[...])
    block_v[...] = (x + gate * branch).astype(BF16).reshape(FRAMES, 2, D)
    save_block = pltpu.make_async_copy(block_v, block_out, out_sem.at[0])
    save_block.start()

    copies[8].wait()
    g = seed_v[...].reshape(TOK, D).astype(F32)
    branch_grad = (gate * g).astype(BF16)
    attended_grad = dot(branch_grad, o_v[...], NT).astype(BF16)
    q_grad, k_grad, v_grad = attend_back(probs, attended_grad, q, keys_by_head, values_by_head)
    grads = lanes_of([rotate_back(q_grad), rotate_back(k_grad), v_grad])

    wide[: 3 * HW, :] = grads.T
    wide[3 * HW :, :] = attended.astype(F32).T
    empty = jnp.zeros((BLOCK - QKV_COLS - PROJ_ROWS, TOK), F32)
    for y in range(Y):
        pieces = []
        for s in range(PARTS):
            i = y * PARTS + s
            pieces += [
                wide[pl.ds(i * QKV_COLS, QKV_COLS), :],
                wide[pl.ds(3 * HW + i * PROJ_ROWS, PROJ_ROWS), :],
                empty,
            ]
        factors_v[y] = jnp.concatenate(pieces, axis=0).astype(BF16)
    save_factors = pltpu.make_async_copy(factors_v, factors, out_sem.at[1])
    save_factors.start()

    normed_grad = dot(grads.astype(BF16), w_v[...]).astype(BF16).astype(F32)
    x_grad = layer_norm_back(normed_grad * (1.0 + scale), unit, inverse)
    x_grad_v[...] = (g + x_grad).astype(BF16).reshape(FRAMES, 2, D)
    save_grad = pltpu.make_async_copy(x_grad_v, x_grad_out, out_sem.at[2])
    save_grad.start()
    wait_all([save_block, save_factors, save_grad])


def weight_grad_kernel(core, normed, branch_grad, factors, keep, send, n_v, b_v, f_v, in_sem):
    copies = fetch([(normed, n_v), (factors, f_v), (branch_grad, b_v)], in_sem)
    wait_all(copies)
    left = lanes_of([f_v[y] for y in range(Y)])
    is_qkv = lax.rem(lax.broadcasted_iota(jnp.int32, (PARTS * BLOCK, 1), 0), BLOCK) < QKV_COLS
    sums = jnp.where(is_qkv, dot(left, n_v[...]), dot(left, b_v[...]))
    first = core[0] == 0

    def quarter(d):
        main = sums[:, d * 256 : (d + 1) * 256]
        tail = sums[:, 1024 + d * 32 : 1024 + (d + 1) * 32]
        return main.reshape(2, 8, BLOCK, 256), tail.reshape(2, 8, BLOCK, 32)

    for x in range(2):
        for half, (a, b) in enumerate(zip(quarter(2 * x), quarter(2 * x + 1), strict=True)):
            lanes = slice(0, 256) if half == 0 else slice(256, WIDTH)
            keep[:, x, :, :, lanes] = jnp.where(first, a, b).astype(BF16)
            send[:, x, :, :, lanes] = jnp.where(first, b, a).astype(BF16)


def add_cores_kernel(xl, keep, received, mine, send):
    own, other = xl[0], 1 - xl[0]
    mine[...] = (keep[own].astype(F32) + received[own].astype(F32)).astype(BF16)
    send[...] = (keep[other].astype(F32) + received[other].astype(F32)).astype(BF16)


def hbm(n):
    return [pl.BlockSpec(memory_space=pltpu.HBM)] * n


def vmem(n):
    return [pl.BlockSpec(memory_space=pltpu.VMEM)] * n


def whole(*shape):
    return pl.BlockSpec(shape, lambda i: (0,) * len(shape))


def params(mib):
    return pltpu.CompilerParams(vmem_limit_bytes=mib * 2**20)


def out(dtype, *shape):
    return pltpu.HBM(shape, dtype)


def buf(dtype, *shape):
    return pltpu.VMEM(shape, dtype)


def dma(*n):
    return pltpu.SemaphoreType.DMA(n) if n else pltpu.SemaphoreType.DMA


PAIRS = (FRAMES, 2, D)
MOD = (1, 3, 2, D)
QKV_W = (3 * HW, D)
OUT_W = (HW, D)
ATT = (TOK, HW)
PROB = (HEADS, TOK, TOK)
CHUNK = (BLOCK, WIDTH)


def shards(tokens, modulation, frame_pos, qkv_weight, out_weight, seed_grad):
    seed = seed_grad.reshape(PAIRS)
    tokens = tokens.reshape(TOK, D)
    mod = modulation.transpose(0, 2, 1, 3)
    qkv_w = qkv_weight.swapaxes(1, 2)

    branch_grad = pl.pallas_call(
        branch_grad_kernel,
        grid=(1,),
        out_shape=out(BF16, TOK, D),
        in_specs=[whole(*PAIRS), whole(*MOD)],
        out_specs=whole(TOK, D),
        compiler_params=params(16),
        name="branch_grad",
    )(seed, mod)
    branch_all = lax.all_gather(branch_grad, "y", tiled=True)

    x1, q, k, v, p = pl.pallas_call(
        spatial_forward_kernel,
        out_shape=(out(BF16, *PAIRS), out(BF16, *ATT), out(BF16, *ATT), out(BF16, *ATT), out(BF16, *PROB)),
        in_specs=hbm(4),
        out_specs=tuple(hbm(5)),
        scratch_shapes=[
            buf(BF16, TOK, D), buf(F32, *MOD), buf(BF16, *QKV_W), buf(BF16, *OUT_W), buf(BF16, *PAIRS),
            buf(BF16, *ATT), buf(BF16, *ATT), buf(BF16, *ATT), buf(BF16, *PROB), dma(6), dma(5),
        ],
        compiler_params=params(40),
        name="spatial_forward",
    )(tokens, mod, qkv_w, out_weight)

    seq = ("y", "xl", "z")
    located = lax.all_to_all(x1, seq, split_axis=0, concat_axis=0, tiled=True)

    frequency = jnp.exp(jnp.arange(HALF, dtype=F32) * (-2.0 * math.log(ROPE_BASE) / HEAD_DIM))
    lane_frequency = jnp.tile(frequency, 2 * HEADS)
    angles = jnp.repeat(frame_pos.astype(F32), 2)[:, None] * lane_frequency[None, :]
    sign = np.tile(np.repeat(np.array([-1.0, 1.0], np.float32), HALF), HEADS)
    cosines = jnp.cos(angles)
    sines = jnp.sin(angles) * sign[None, :]

    normed = pl.pallas_call(
        temporal_normed_kernel,
        grid=(1,),
        out_shape=out(BF16, TOK, D),
        in_specs=[whole(*PAIRS), whole(*MOD)],
        out_specs=whole(TOK, D),
        compiler_params=params(16),
        name="temporal_normed",
    )(located, mod)
    normed_all = lax.all_gather(normed, "y", tiled=True)

    block_out, located_grad, factors = pl.pallas_call(
        temporal_kernel,
        out_shape=(out(BF16, *PAIRS), out(BF16, *PAIRS), out(BF16, Y, PARTS * BLOCK, TOK)),
        in_specs=hbm(7),
        out_specs=tuple(hbm(3)),
        scratch_shapes=[
            buf(BF16, *PAIRS), buf(BF16, *PAIRS), buf(F32, *ATT), buf(F32, *ATT), buf(F32, *MOD),
            buf(BF16, *QKV_W), buf(BF16, *OUT_W), buf(BF16, *PAIRS), buf(BF16, *PAIRS),
            buf(BF16, Y, PARTS * BLOCK, TOK), buf(F32, 4 * HW, TOK), dma(9), dma(3),
        ],
        compiler_params=params(48),
        name="temporal",
    )(located, seed, cosines, sines, mod, qkv_w, out_weight)

    factors = lax.all_to_all(factors, "y", split_axis=0, concat_axis=0, tiled=True)
    framed_grad = lax.all_to_all(located_grad, seq, split_axis=0, concat_axis=0, tiled=True)

    core = lax.axis_index("core").reshape(1).astype(jnp.int32)
    keep, send = pl.pallas_call(
        weight_grad_kernel,
        out_shape=(out(BF16, 2, 2, 8, *CHUNK), out(BF16, 2, 2, 8, *CHUNK)),
        grid=(1,),
        in_specs=[pl.BlockSpec(memory_space=pltpu.SMEM), *hbm(3)],
        out_specs=(whole(2, 2, 8, *CHUNK), whole(2, 2, 8, *CHUNK)),
        scratch_shapes=[buf(BF16, Y * TOK, D), buf(BF16, Y * TOK, D), buf(BF16, Y, PARTS * BLOCK, TOK), dma(3)],
        compiler_params=params(48),
        name="weight_grad",
    )(core, normed_all, branch_all, factors)
    received = lax.ppermute(send, "core", [(0, 1), (1, 0)])

    projected_grad = pl.pallas_call(
        spatial_attention_back_kernel,
        out_shape=out(BF16, TOK, 3 * HW),
        in_specs=hbm(7),
        out_specs=hbm(1)[0],
        scratch_shapes=[
            buf(BF16, *PAIRS), buf(F32, *MOD), buf(BF16, *OUT_W), buf(BF16, *ATT), buf(BF16, *ATT), buf(BF16, *ATT),
            buf(BF16, *PROB), buf(BF16, TOK, 3 * HW), dma(7), dma(),
        ],
        compiler_params=params(40),
        name="spatial_attention_back",
    )(framed_grad, mod, out_weight, q, k, v, p)

    xl = lax.axis_index("xl").reshape(1).astype(jnp.int32)
    mine, send = pl.pallas_call(
        add_cores_kernel,
        grid=(1,),
        out_shape=(out(BF16, 2, 8, *CHUNK), out(BF16, 2, 8, *CHUNK)),
        in_specs=[pl.BlockSpec(memory_space=pltpu.SMEM), whole(2, 2, 8, *CHUNK), whole(2, 2, 8, *CHUNK)],
        out_specs=(whole(2, 8, *CHUNK), whole(2, 8, *CHUNK)),
        compiler_params=params(24),
        name="add_cores",
    )(xl, keep, received)
    received = lax.ppermute(send, "xl", [(0, 1), (1, 0)])

    tokens_grad = pl.pallas_call(
        spatial_input_back_kernel,
        out_shape=out(BF16, TOK, D),
        in_specs=hbm(5),
        out_specs=hbm(1)[0],
        scratch_shapes=[
            buf(BF16, *PAIRS), buf(BF16, TOK, D), buf(F32, *MOD), buf(BF16, *QKV_W), buf(BF16, TOK, 3 * HW),
            buf(BF16, TOK, D), dma(5), dma(),
        ],
        compiler_params=params(32),
        name="spatial_input_back",
    )(framed_grad, tokens, mod, qkv_w, projected_grad)

    both = (mine.astype(F32) + received.astype(F32)).astype(BF16).reshape(16, *CHUNK)
    parts = lax.all_to_all(both, ("xh", "z"), split_axis=0, concat_axis=0, tiled=True)
    total = jnp.sum(parts.astype(F32), axis=0)
    return (
        block_out.reshape(1, FRAMES, 2, D),
        tokens_grad.reshape(1, 1, LOC, D),
        total[:QKV_COLS].T,
        total[QKV_COLS : QKV_COLS + PROJ_ROWS],
    )


def solution(mesh):
    sizes = (2, 2, 4, 2, 8)
    split = Mesh(mesh.devices.reshape(sizes), ("xh", "core", "y", "xl", "z"))
    dp, seq = ("xh", "core"), ("y", "xl", "z")
    return jax.shard_map(
        shards,
        mesh=split,
        in_specs=(
            P(dp, seq, None, None),
            P(dp, None, None, None),
            P(),
            P(),
            P(),
            P(dp, None, seq, None),
        ),
        out_specs=(
            P(dp, None, seq, None),
            P(dp, seq, None, None),
            P(dp, seq),
            P(seq, dp),
        ),
        check_vma=False,
    )
```

time: 173 us -> 146 us (0.84)
  waiting for transfers between devices: 67.8 us -> 30.3 us
  blocking collectives: 0 us -> 26.3 us
  local copies, waits for them, and re-layouts: 31.5 us -> 20.8 us
  starting transfers between devices: 30.4 us -> 20.6 us
  Pallas kernels: 23.4 us -> 28.6 us
    all_to_all x0 -> x1, blocking collectives: none -> 26.3 us  [shards(): located = lax.all_to_all(x1, seq, split_axis=0, concat_axis=0, tiled=True)]
    all_to_all x3 -> x2, waiting for transfers between devices: 37.7 us -> 15.8 us  [the longest x1 14.2 us: shards(): lax.all_to_all(factors, 'y', split_axis=0, concat_axis=0, tiled=True)]
    all_gather x2, waiting for transfers between devices: 18.1 us -> 0.01 us  [the longest x1 0.01 us: shards(): branch_all = lax.all_gather(branch_grad, 'y', tiled=True)]
    all_to_all x3 -> x2, starting transfers between devices: 22.1 us -> 9.74 us  [the longest x1 6.06 us: shards(): lax.all_to_all(both, ('xh', 'z'), split_axis=0, concat_axis=0, tiled=True)]
    unnamed x46 -> x42, local copies, waits for them, and re-layouts: 29.9 us -> 19.2 us
    pallas_call x5 -> x8, Pallas kernels: 23.4 us -> 28.6 us  [the longest x1 9.12 us: shards(): pl.pallas_call(temporal_kernel, out_shape=(out(BF16, *PAIRS), out(BF16, *...]
    all_to_all x1, waiting for transfers between devices: 12 us -> 8.07 us  [shards(): lax.all_to_all(located_grad, seq, split_axis=0, concat_axis=0, tiled=True)]
    ppermute x0 -> x1, waiting for transfers between devices: none -> 3.55 us  [shards(): received = lax.ppermute(send, 'xl', [(0, 1), (1, 0)])]
  transfers between devices with their start and end apart: 7 -> 7, of which waited for: 5 -> 5; matrix products, arithmetic and copies ran while one was open for 9% -> 2% of each run, Pallas kernels for 11% -> 15%
where the time goes in v2:
time: 146 us; the launch traced here: 145 us
  waiting for transfers between devices  30.3 us (21%)
  Pallas kernels  28.6 us (20%)
  blocking collectives  26.3 us (18%)
  local copies, waits for them, and re-layouts  20.8 us (14%)
  starting transfers between devices  20.6 us (14%)
  between operations  14.3 us (10%)
  other arithmetic  4.42 us (3%)
    all_to_all x1, blocking collectives, shards(): located = lax.all_to_all(x1, seq, split_axis=0, concat_axis=0, tiled=True)  26.3 us
    unnamed x42, local copies, waits for them, and re-layouts  19.2 us
    all_to_all x1, waiting for transfers between devices, shards(): lax.all_to_all(factors, 'y', split_axis=0, concat_axis=0, tiled=True)  14.2 us
    all_to_all x1, starting transfers between devices, shards(): lax.all_to_all(located_grad, seq, split_axis=0, concat_axis=0, tiled=True)  9.19 us
    pallas_call x1, Pallas kernels, shards(): pl.pallas_call(temporal_kernel, out_shape=(out(BF16, *PAIRS), out(BF16, *...  9.12 us
    all_to_all x1, waiting for transfers between devices, shards(): lax.all_to_all(located_grad, seq, split_axis=0, concat_axis=0, tiled=True)  8.07 us
    all_to_all x1, starting transfers between devices, shards(): lax.all_to_all(both, ('xh', 'z'), split_axis=0, concat_axis=0, tiled=True)  6.06 us
    pallas_call x1, Pallas kernels, shards(): pl.pallas_call(spatial_forward_kernel, out_shape=(out(BF16, *PAIRS), out(...  4.85 us
  transfers between devices with their start and end apart: 7, of which 5 were waited for; matrix products, arithmetic and copies ran while one was open for 2% of the time, Pallas kernels for 15%

profile of v2, /device:TPU:32, one launch (start us, length us, event | category | flops | bytes accessed | tf_op | source)
XLA Modules:
  0.0 145.2 jit_solution(4468908133970965513)
XLA Ops:
  7.2 0.0 all-gather.5.cloned.1.call-start
  7.2 0.0 copy-start.7
  7.2 1.0 copy-done.7
  8.2 0.0 copy-start.11
  8.2 0.7 copy-done.11
  8.9 0.9 branch_grad.1
  9.8 0.0 all-gather.5.cloned.1.call-update
  9.9 0.0 all-gather.3.cloned.1.call-start
  9.9 0.0 copy-start
  9.9 3.3 %copy-done = bf16[2,1152,1728]{1,2,0:T(8,128)(2,1)S(1)} copy-done((bf16[2,1152,1728]{1,2,0:T(8,128)(2,1)S(1)}, bf16[2,1152,1728]{1,2,0:T(8,128)(2,1)}, u32[]{:S(2)}) %copy-start) | copy-done | bytes 7962648
  13.2 0.0 copy-start.2
  13.2 1.7 %copy-done.2 = bf16[2,576,1152]{2,1,0:T(8,128)(2,1)S(1)} copy-done((bf16[2,576,1152]{2,1,0:T(8,128)(2,1)S(1)}, bf16[2,576,1152]{2,1,0:T(8,128)(2,1)}, u32[]{:S(2)}) %copy-start.2) | copy-done | bytes 2654232
  14.9 0.0 copy-start.5
  14.9 1.0 copy-done.5
  15.9 0.0 copy-start.12
  15.9 0.7 copy-done.12
  16.6 0.0 copy-start.20
  16.6 0.0 copy-start.19
  16.6 0.0 copy-start.3
  16.6 0.0 copy-start.13
  16.7 4.8 %spatial_forward.1 = (bf16[64,2,1152]{2,1,0:T(2,128)(2,1)}, bf16[128,576]{1,0:T(8,128)(2,1)}, bf16[128,576]{1,0:T(8,128)(2,1)}, bf16[128,576]{1,0:T(8,128)(2,1)}, bf16[8,128,128]{2,1,0:T(8,128)(2,1)}) custom-call(bf16[128,1152]{1,0:T(8,128)(2,1)S(1)} %bitcast.14, f32[1,3,2,1152]{3,2,1,0:T(2,128)S(1)} %bitcast.19, bf16[2,1728,1152]{2,1,0:T(8,128)(2,1)S(1)} %bitcast.12, ...), custom_call_target="tpu_custom_call" | custom-call | tf_op jit(solution)/shard_map/spatial_forward/pallas_call | solution.py:364
  21.5 26.3 %all_to_all.20.located = bf16[64,2,1152]{2,1,0:T(2,128)(2,1)S(1)} all-to-all(bf16[64,2,1152]{2,1,0:T(2,128)(2,1)} %get-tuple-element.16), channel_id=1, replica_groups=mesh['xh'=2,'core'=2,'y'=4,'xl'=2,'z'=8] {'y','xl','z'}, dimensions={0} | all-to-all | bytes 589824 | tf_op jit(solution)/shard_map/all_to_all | solution.py:378
  47.9 1.2 temporal_normed.1
  49.1 0.0 all-gather.3.cloned.1.call-update
  49.1 0.0 copy-done.20
  49.2 0.1 mul.41
  49.3 0.1 broadcast_in_dim.3
  49.3 0.1 mul.37
  49.5 0.0 copy-done.19
  49.5 1.2 fusion
  50.7 0.0 copy-done.3
  50.7 0.0 copy-done.8
  50.7 0.0 copy-done.13
  50.7 9.1 %temporal.1 = (bf16[64,2,1152]{2,1,0:T(2,128)(2,1)}, bf16[64,2,1152]{2,1,0:T(2,128)(2,1)}, bf16[4,640,128]{2,1,0:T(8,128)(2,1)}) custom-call(bf16[64,2,1152]{2,1,0:T(2,128)(2,1)S(1)} %all_to_all.20.located, bf16[64,2,1152]{2,1,0:T(2,128)(2,1)S(1)} %bitcast.17, f32[128,576]{1,0:T(8,128)S(1)} %get-tuple-element.29.cosines, ...), custom_call_target="tpu_custom_call" | custom-call | tf_op jit(solution)/shard_map/temporal/pallas_call | solution.py:398
  59.9 3.7 %all-to-all-start.2 = ((bf16[4,640,128]{2,1,0:T(8,128)(2,1)}), bf16[4,640,128]{2,1,0:T(8,128)(2,1)S(1)}, u32[]{:S(2)}, u32[]{:S(2)}) async-start(bf16[4,640,128]{2,1,0:T(8,128)(2,1)} %get-tuple-element.23), calls=%async_computation.2 | async-start | bytes 1310720 | tf_op jit(solution)/shard_map/all_to_all | solution.py:412
  63.5 14.2 %all-to-all-done.2.factors = bf16[4,640,128]{2,1,0:T(8,128)(2,1)S(1)} async-done(((bf16[4,640,128]{2,1,0:T(8,128)(2,1)}), bf16[4,640,128]{2,1,0:T(8,128)(2,1)S(1)}, u32[]{:S(2)}, u32[]{:S(2)}) %all-to-all-start.2) | async-done | bytes 655392 | tf_op jit(solution)/shard_map/all_to_all | solution.py:412
  77.8 1.3 copy-done.9
  79.0 1.3 copy-done.10
  80.3 4.2 %weight_grad.1 = (bf16[2,2,8,40,288]{4,3,2,1,0:T(8,128)(2,1)}, bf16[2,2,8,40,288]{4,3,2,1,0:T(8,128)(2,1)}) custom-call(s32[1]{0:T(128)} %bitcast.7.core, bf16[512,1152]{1,0:T(8,128)(2,1)S(1)} %copy-done.10, bf16[512,1152]{1,0:T(8,128)(2,1)S(1)} %copy-done.9, bf16[4,640,128]{2,1,0:T(8,128)(2,1)S(1)} %all-to-all-done.2.factors), custom_call_target="tpu_custom_call" | custom-call | tf_op jit(solution)/shard_map/weight_grad/pallas_call | solution.py:416
  84.5 0.1 collective-permute-start
  84.6 2.9 %collective-permute-done.received = bf16[2,2,8,40,288]{4,3,2,1,0:T(8,128)(2,1)} collective-permute-done((bf16[2,2,8,40,288]{4,3,2,1,0:T(8,128)(2,1)}, bf16[2,2,8,40,288]{4,3,2,1,0:T(8,128)(2,1)}, u32[]{:S(2)}, u32[]{:S(2)}) %collective-permute-start) | collective-permute-done | bytes 737312 | tf_op jit(solution)/shard_map/ppermute | solution.py:426
  87.5 1.2 copy-done.14
  88.7 2.3 %add_cores.1 = (bf16[2,8,40,288]{3,2,1,0:T(8,128)(2,1)}, bf16[2,8,40,288]{3,2,1,0:T(8,128)(2,1)}) custom-call(s32[1]{0:T(128)} %bitcast.6.xl, bf16[2,2,8,40,288]{4,3,2,1,0:T(8,128)(2,1)S(1)} %copy-done.14, bf16[2,2,8,40,288]{4,3,2,1,0:T(8,128)(2,1)} %collective-permute-done.received), custom_call_target="tpu_custom_call" | custom-call | tf_op jit(solution)/shard_map/add_cores/pallas_call | solution.py:442
  90.9 1.5 %collective-permute-start.1 = (bf16[2,8,40,288]{3,2,1,0:T(8,128)(2,1)}, bf16[2,8,40,288]{3,2,1,0:T(8,128)(2,1)}, u32[]{:S(2)}, u32[]{:S(2)}) collective-permute-start(bf16[2,8,40,288]{3,2,1,0:T(8,128)(2,1)} %get-tuple-element.27), channel_id=1, source_target_pairs={{0,8},{8,0},{1,9},{9,1},{2,10},{10,2},{3,11},{11,3},{4,12},{12,4},... | collective-permute-start | bytes 1105928 | tf_op jit(solution)/shard_map/ppermute | solution.py:451
  92.4 9.2 %all-to-all-start.1 = ((bf16[64,2,1152]{2,1,0:T(2,128)(2,1)}), bf16[64,2,1152]{2,1,0:T(2,128)(2,1)S(1)}, u32[]{:S(2)}, u32[]{:S(2)}) async-start(bf16[64,2,1152]{2,1,0:T(2,128)(2,1)} %get-tuple-element.18), calls=%async_computation.1 | async-start | bytes 589824 | tf_op jit(solution)/shard_map/all_to_all | solution.py:413
  101.6 3.5 %collective-permute-done.1 = bf16[2,8,40,288]{3,2,1,0:T(8,128)(2,1)} collective-permute-done((bf16[2,8,40,288]{3,2,1,0:T(8,128)(2,1)}, bf16[2,8,40,288]{3,2,1,0:T(8,128)(2,1)}, u32[]{:S(2)}, u32[]{:S(2)}) %collective-permute-start.1) | collective-permute-done | bytes 368672 | tf_op jit(solution)/shard_map/ppermute | solution.py:451
  105.2 2.1 %add_convert_fusion = bf16[2,8,40,288]{3,2,1,0:T(8,128)(2,1)} fusion(bf16[2,8,40,288]{3,2,1,0:T(8,128)(2,1)} %collective-permute-done.1, bf16[2,8,40,288]{3,2,1,0:T(8,128)(2,1)} %get-tuple-element.26), kind=kLoop, calls=%fused_computation.1 | loop fusion | flops 737280 | bytes 1105920 | tf_op jit(solution)/shard_map/convert_element_type | solution.py:466
  107.2 8.1 %all-to-all-done.1.grad = bf16[64,2,1152]{2,1,0:T(2,128)(2,1)S(1)} async-done(((bf16[64,2,1152]{2,1,0:T(2,128)(2,1)}), bf16[64,2,1152]{2,1,0:T(2,128)(2,1)S(1)}, u32[]{:S(2)}, u32[]{:S(2)}) %all-to-all-start.1) | async-done | bytes 294944 | tf_op jit(solution)/shard_map/all_to_all | solution.py:413
  115.3 6.1 %all-to-all-start.3 = ((bf16[16,40,288]{2,1,0:T(8,128)(2,1)}), bf16[16,40,288]{2,1,0:T(8,128)(2,1)}, u32[]{:S(2)}, u32[]{:S(2)}) async-start(bf16[16,40,288]{2,1,0:T(8,128)(2,1)} %bitcast.24), calls=%async_computation.3 | async-start | bytes 983040 | tf_op jit(solution)/shard_map/all_to_all | solution.py:467
  121.4 0.0 copy-done.16
  121.4 0.0 copy-start.15
  121.4 0.9 copy-done.15
  122.3 0.9 copy-done.17
  123.2 0.9 copy-done.18
  124.2 3.4 %spatial_attention_back.1.projected_grad = bf16[128,1728]{1,0:T(8,128)(2,1)} custom-call(bf16[64,2,1152]{2,1,0:T(2,128)(2,1)S(1)} %all-to-all-done.1.grad, f32[1,3,2,1152]{3,2,1,0:T(2,128)S(1)} %bitcast.22, bf16[2,576,1152]{2,1,0:T(8,128)(2,1)S(1)} %copy-done.3, bf16[128,576]{1,0:T(8,128)(2,1)S(1)} %copy-done.16, bf16[128,576]{1,0:T(8,128)(2,1)S(1)} %copy-done.17, ...), custom_call_target="tpu_custom_call" | custom-call | tf_op jit(solution)/shard_map/spatial_attention_back/pallas_call | solution.py:428
  127.6 0.0 copy-done.6
  127.6 0.0 copy-start.1
  127.6 3.3 %copy-done.1 = bf16[2,1152,1728]{1,2,0:T(8,128)(2,1)S(1)} copy-done((bf16[2,1152,1728]{1,2,0:T(8,128)(2,1)S(1)}, bf16[2,1152,1728]{1,2,0:T(8,128)(2,1)}, u32[]{:S(2)}) %copy-start.1) | copy-done | bytes 7962648
  130.8 1.0 copy-done.4
  131.9 2.6 %spatial_input_back.1 = bf16[128,1152]{1,0:T(8,128)(2,1)} custom-call(bf16[64,2,1152]{2,1,0:T(2,128)(2,1)S(1)} %all-to-all-done.1.grad, bf16[128,1152]{1,0:T(8,128)(2,1)S(1)} %bitcast.15, f32[1,3,2,1152]{3,2,1,0:T(2,128)S(1)} %bitcast.23, bf16[2,1728,1152]{2,1,0:T(8,128)(2,1)S(1)} %bitcast.13, bf16[128,1728]{1,0:T(8,128)(2,1)S(1)} %copy-done.4), custom_call_target="tpu_custom_call" | custom-call | tf_op jit(solution)/shard_map/spatial_input_back/pallas_call | solution.py:453
  134.5 1.5 %all-to-all-done.3 = bf16[16,40,288]{2,1,0:T(8,128)(2,1)} async-done(((bf16[16,40,288]{2,1,0:T(8,128)(2,1)}), bf16[16,40,288]{2,1,0:T(8,128)(2,1)}, u32[]{:S(2)}, u32[]{:S(2)}) %all-to-all-start.3) | async-done | bytes 368672 | tf_op jit(solution)/shard_map/all_to_all | solution.py:467
  136.0 1.1 convert_reduce_fusion
  137.2 0.6 slice.9
  137.8 0.6 slice_bitcast_fusion
  (14 shorter events, 0.0 us)
Async XLA Ops:
  7.2 70.6 %all-gather.5.cloned.1.call-start = ((), (), s32[]{:S(2)}) async-start(), calls=%async_computation.5 | async-start | bytes 1474560 | tf_op jit(solution)/shard_map/all_gather | solution.py:362
  7.2 1.0 copy-start.7
  8.2 0.7 copy-start.11
  9.9 67.9 %all-gather.3.cloned.1.call-start = ((), (), s32[]{:S(2)}) async-start(), calls=%async_computation.4 | async-start | bytes 1474560 | tf_op jit(solution)/shard_map/all_gather | solution.py:396
  9.9 3.3 %copy-start = (bf16[2,1152,1728]{1,2,0:T(8,128)(2,1)S(1)}, bf16[2,1152,1728]{1,2,0:T(8,128)(2,1)}, u32[]{:S(2)}) copy-start(bf16[2,1152,1728]{1,2,0:T(8,128)(2,1)} %param.10) | copy-start | bytes 23887876
  13.2 1.7 %copy-start.2 = (bf16[2,576,1152]{2,1,0:T(8,128)(2,1)S(1)}, bf16[2,576,1152]{2,1,0:T(8,128)(2,1)}, u32[]{:S(2)}) copy-start(bf16[2,576,1152]{2,1,0:T(8,128)(2,1)} %out_w.5) | copy-start | bytes 7962628
  14.9 1.0 copy-start.5
  15.9 0.7 copy-start.12
  16.6 32.5 %copy-start.20 = (s32[64]{0:T(128)S(1)}, s32[64]{0:T(128)}, u32[]{:S(2)}) copy-start(s32[64]{0:T(128)} %param.9) | copy-start | bytes 772
  16.6 32.8 %copy-start.19 = (f32[576]{0:T(1024)S(1)}, f32[576]{0:T(1024)}, u32[]{:S(2)}) copy-start(f32[576]{0:T(1024)} %constant.20) | copy-start | bytes 6916
  16.6 34.1 %copy-start.3 = (bf16[2,576,1152]{2,1,0:T(8,128)(2,1)S(1)}, bf16[2,576,1152]{2,1,0:T(8,128)(2,1)}, u32[]{:S(2)}) copy-start(bf16[2,576,1152]{2,1,0:T(8,128)(2,1)} %out_w.5) | copy-start | bytes 7962628
  16.6 34.1 %copy-start.8 = (bf16[1,64,2,1152]{3,2,1,0:T(2,128)(2,1)S(1)}, bf16[1,64,2,1152]{3,2,1,0:T(2,128)(2,1)}, u32[]{:S(2)}) copy-start(bf16[1,64,2,1152]{3,2,1,0:T(2,128)(2,1)} %param.12) | copy-start | bytes 884740
  16.6 34.1 %copy-start.13 = (f32[1,2,3,1152]{3,1,2,0:T(2,128)S(1)}, f32[1,2,3,1152]{3,1,2,0:T(2,128)}, u32[]{:S(2)}) copy-start(f32[1,2,3,1152]{3,1,2,0:T(2,128)} %param.8) | copy-start | bytes 82948
  59.9 17.9 %all-to-all-start.2 = ((bf16[4,640,128]{2,1,0:T(8,128)(2,1)}), bf16[4,640,128]{2,1,0:T(8,128)(2,1)S(1)}, u32[]{:S(2)}, u32[]{:S(2)}) async-start(bf16[4,640,128]{2,1,0:T(8,128)(2,1)} %get-tuple-element.23), calls=%async_computation.2 | async-start | bytes 1310720 | tf_op jit(solution)/shard_map/all_to_all | solution.py:412
  77.8 1.3 copy-start.9
  79.0 1.3 copy-start.10
  80.3 41.1 %copy-start.16 = (bf16[128,576]{1,0:T(8,128)(2,1)S(1)}, bf16[128,576]{1,0:T(8,128)(2,1)}, u32[]{:S(2)}) copy-start(bf16[128,576]{1,0:T(8,128)(2,1)} %get-tuple-element.19.q_in) | copy-start | bytes 442372
  84.5 3.0 %collective-permute-start = (bf16[2,2,8,40,288]{4,3,2,1,0:T(8,128)(2,1)}, bf16[2,2,8,40,288]{4,3,2,1,0:T(8,128)(2,1)}, u32[]{:S(2)}, u32[]{:S(2)}) collective-permute-start(bf16[2,2,8,40,288]{4,3,2,1,0:T(8,128)(2,1)} %get-tuple-element.25), channel_id=1, source_target_pairs={{0,64},{64,0},{1,65},{65,1},{2,66},{66,2},{3,67},{67,3},{4,68},{68... | collective-permute-start | bytes 2211848 | tf_op jit(solution)/shard_map/ppermute | solution.py:426
  87.5 1.2 copy-start.14
  90.9 14.2 %collective-permute-start.1 = (bf16[2,8,40,288]{3,2,1,0:T(8,128)(2,1)}, bf16[2,8,40,288]{3,2,1,0:T(8,128)(2,1)}, u32[]{:S(2)}, u32[]{:S(2)}) collective-permute-start(bf16[2,8,40,288]{3,2,1,0:T(8,128)(2,1)} %get-tuple-element.27), channel_id=1, source_target_pairs={{0,8},{8,0},{1,9},{9,1},{2,10},{10,2},{3,11},{11,3},{4,12},{12,4},... | collective-permute-start | bytes 1105928 | tf_op jit(solution)/shard_map/ppermute | solution.py:451
  92.4 22.9 %all-to-all-start.1 = ((bf16[64,2,1152]{2,1,0:T(2,128)(2,1)}), bf16[64,2,1152]{2,1,0:T(2,128)(2,1)S(1)}, u32[]{:S(2)}, u32[]{:S(2)}) async-start(bf16[64,2,1152]{2,1,0:T(2,128)(2,1)} %get-tuple-element.18), calls=%async_computation.1 | async-start | bytes 589824 | tf_op jit(solution)/shard_map/all_to_all | solution.py:413
  107.2 20.3 %copy-start.6 = (bf16[1,1,128,1152]{3,2,1,0:T(8,128)(2,1)S(1)}, bf16[1,1,128,1152]{3,2,1,0:T(8,128)(2,1)}, u32[]{:S(2)}) copy-start(bf16[1,1,128,1152]{3,2,1,0:T(8,128)(2,1)} %param.7) | copy-start | bytes 884740
  115.3 20.7 %all-to-all-start.3 = ((bf16[16,40,288]{2,1,0:T(8,128)(2,1)}), bf16[16,40,288]{2,1,0:T(8,128)(2,1)}, u32[]{:S(2)}, u32[]{:S(2)}) async-start(bf16[16,40,288]{2,1,0:T(8,128)(2,1)} %bitcast.24), calls=%async_computation.3 | async-start | bytes 983040 | tf_op jit(solution)/shard_map/all_to_all | solution.py:467
  121.4 1.0 copy-start.15
  122.3 0.9 copy-start.17
  123.2 0.9 copy-start.18
  127.6 3.3 %copy-start.1 = (bf16[2,1152,1728]{1,2,0:T(8,128)(2,1)S(1)}, bf16[2,1152,1728]{1,2,0:T(8,128)(2,1)}, u32[]{:S(2)}) copy-start(bf16[2,1152,1728]{1,2,0:T(8,128)(2,1)} %param.10) | copy-start | bytes 23887876
  130.8 1.0 copy-start.4
Sparse Core Ops, SparseCore 0:
  10.0 30.0 all-gather.4
  49.2 26.2 all-gather.2

commit v3 on v2

v3 whole, which is shorter than its diff:
```python
from functools import partial
import math

import jax
import jax.numpy as jnp
import numpy as np
from jax import lax
from jax.experimental import pallas as pl
from jax.experimental.pallas import tpu as pltpu
from jax.sharding import Mesh, PartitionSpec as P

D = 1152
HEADS = 8
HEAD_DIM = 72
HALF = HEAD_DIM // 2
HW = 576
LOC = 128
FRAMES = 64
TOK = 128
SCALE = HEAD_DIM ** (-0.5)
EPS = 1e-06
ROPE_BASE = 10000.0
QKV_COLS = 27
PROJ_ROWS = 9
BLOCK = 40
Y = 4
PARTS = 16
WIDTH = D // 4
F32 = jnp.float32
BF16 = jnp.bfloat16

NN = (((1,), (0,)), ((), ()))
NT = (((1,), (1,)), ((), ()))
TN = (((0,), (0,)), ((), ()))


def dot(a, b, dims=NN):
    return lax.dot_general(a, b, dims, preferred_element_type=F32)


def layer_norm(x):
    centered = x - jnp.mean(x, axis=-1, keepdims=True)
    inverse = lax.rsqrt(jnp.mean(centered * centered, axis=-1, keepdims=True) + EPS)
    return centered * inverse, inverse


def layer_norm_back(grad, unit, inverse):
    first = jnp.mean(grad, axis=-1, keepdims=True)
    second = jnp.mean(grad * unit, axis=-1, keepdims=True)
    return inverse * (grad - first - unit * second)


def split_heads(x):
    lane = lax.broadcasted_iota(jnp.int32, (1, HW), 1)
    parts = []
    for h in range(HEADS):
        mine = ((lane >= h * HEAD_DIM) & (lane < (h + 1) * HEAD_DIM)).astype(F32).astype(BF16)
        parts.append(x * mine)
    return jnp.concatenate(parts, axis=0)


def head(x, h):
    return x[:, h * TOK : (h + 1) * TOK]


def rows_of(parts):
    return jnp.concatenate(parts, axis=0)


def lanes_of(parts):
    return jnp.concatenate(parts, axis=1)


def attend(query, keys_by_head, values_by_head, allowed):
    scores = dot(query, keys_by_head, NT)
    probs = []
    for h in range(HEADS):
        s = head(scores, h) * SCALE
        if allowed is not None:
            s = jnp.where(allowed, s, -1e30)
        e = jnp.exp(s - jnp.max(s, axis=-1, keepdims=True))
        probs.append((e / jnp.sum(e, axis=-1, keepdims=True)).astype(BF16))
    return probs, dot(lanes_of(probs), values_by_head).astype(BF16)


def attend_back(probs, attended_grad, query, keys_by_head, values_by_head):
    prob_grads = dot(attended_grad, values_by_head, NT)
    values_grad = dot(rows_of(probs), split_heads(attended_grad), TN)
    score_grads = []
    for h in range(HEADS):
        p = probs[h].astype(F32)
        g = head(prob_grads, h)
        s = p * (g - jnp.sum(g * p, axis=-1, keepdims=True)) * SCALE
        score_grads.append(s.astype(BF16))
    query_grad = dot(lanes_of(score_grads), keys_by_head)
    keys_grad = dot(rows_of(score_grads), split_heads(query), TN)
    return query_grad, keys_grad, values_grad


def swap_halves(x):
    lane = lax.broadcasted_iota(jnp.int32, (1, HW), 1)
    first = lax.rem(lane, HEAD_DIM) < HALF
    later = jnp.concatenate([x[:, HALF:], x[:, :HALF]], axis=1)
    earlier = jnp.concatenate([x[:, HW - HALF :], x[:, : HW - HALF]], axis=1)
    return jnp.where(first, later, earlier)


def fetch(pairs, sems):
    copies = [pltpu.make_async_copy(src, dst, sems.at[i]) for i, (src, dst) in enumerate(pairs)]
    for c in copies:
        c.start()
    return copies


def store(pairs, sems):
    return fetch(pairs, sems)


def wait_all(copies):
    for c in copies:
        c.wait()


def regroup(x):
    main = [x[:, d * WIDTH : d * WIDTH + 256] for d in range(4)]
    tail = [x[:, d * WIDTH + 256 : (d + 1) * WIDTH] for d in range(4)]
    return jnp.concatenate(main + tail, axis=1)


def branch_grad_kernel(seed, mod, sent, kept, seed_v, sent_v, kept_v, sems):
    (load,) = fetch([(seed, seed_v)], sems.at[pl.ds(0, 1)])
    load.wait()
    g = seed_v[...].reshape(TOK, D).astype(F32)
    branch_grad = (mod[0, 2, 1:2, :] * g).astype(BF16)
    sent_v[...] = regroup(branch_grad)
    kept_v[...] = branch_grad
    wait_all(fetch([(sent_v, sent), (kept_v, kept)], sems.at[pl.ds(1, 2)]))


def rope_tables(pos):
    row = lax.broadcasted_iota(jnp.int32, (TOK, FRAMES), 0)
    frame = lax.broadcasted_iota(jnp.int32, (TOK, FRAMES), 1)
    mine = (row >= 2 * frame) & (row < 2 * frame + 2)
    time = jnp.sum(jnp.where(mine, pos.astype(F32), 0.0), axis=-1, keepdims=True)
    lane = lax.broadcasted_iota(jnp.int32, (1, HW), 1)
    frequency = jnp.exp(lax.rem(lane, HALF).astype(F32) * (-2.0 * math.log(ROPE_BASE) / HEAD_DIM))
    angles = time * frequency
    sign = jnp.where(lax.rem(lane, HEAD_DIM) < HALF, -1.0, 1.0)
    return jnp.cos(angles), jnp.sin(angles) * sign


def tables_kernel(pos, cos_out, sin_out, cos_v, sin_v, sems):
    cos_v[...], sin_v[...] = rope_tables(pos[...])
    wait_all(fetch([(cos_v, cos_out), (sin_v, sin_out)], sems))


def spatial_forward_kernel(
    place, tokens, mod, qkv_w, out_w, x1, q_out, k_out, v_out, p_out,
    tokens_v, mod_v, w_v, o_v, normed_v, x1_v, q_v, k_v, v_v, p_v, in_sem, out_sem,
):
    copies = fetch(
        [(tokens, tokens_v), (mod, mod_v)]
        + [(qkv_w.at[0, pl.ds(i * HW, HW)], w_v.at[pl.ds(i * HW, HW)]) for i in range(3)]
        + [(out_w.at[0], o_v)],
        in_sem,
    )
    wait_all(copies[:2])

    @pl.when(place[0] >= 0)
    def _():
        unit, _ = layer_norm(tokens_v[...].astype(F32))
        normed_v[...] = (unit * (1.0 + mod_v[0, 1, 0:1, :]) + mod_v[0, 0, 0:1, :]).astype(BF16)

    for i, held in enumerate((q_v, k_v, v_v)):
        copies[2 + i].wait()

        @pl.when(place[0] >= 0)
        def _(i=i, held=held):
            held[...] = dot(normed_v[...], w_v[i * HW : (i + 1) * HW, :], NT).astype(BF16)

    probs, attended = attend(q_v[...], split_heads(k_v[...]), split_heads(v_v[...]), None)
    for h in range(HEADS):
        p_v[h] = probs[h]
    saves = fetch([(q_v, q_out), (k_v, k_out), (v_v, v_out), (p_v, p_out)], out_sem.at[pl.ds(0, 4)])
    copies[5].wait()
    branch = dot(attended, o_v[...])
    x1_v[...] = (tokens_v[...].astype(F32) + mod_v[0, 2, 0:1, :] * branch).astype(BF16).reshape(FRAMES, 2, D)
    saves += fetch([(x1_v, x1)], out_sem.at[pl.ds(4, 1)])
    wait_all(saves)


def spatial_attention_back_kernel(
    grad, mod, out_w, q_in, k_in, v_in, p_in, result, o_v, q_v, k_v, v_v, p_v, sems
):
    copies = fetch([(out_w.at[0], o_v), (v_in, v_v), (p_in, p_v), (k_in, k_v), (q_in, q_v)], sems)
    g = grad[...].reshape(TOK, D).astype(F32)
    branch_grad = (mod[0, 2, 0:1, :] * g).astype(BF16)
    wait_all(copies)
    attended_grad = dot(branch_grad, o_v[...], NT).astype(BF16)
    probs = [p_v[h] for h in range(HEADS)]
    grads = attend_back(probs, attended_grad, q_v[...], split_heads(k_v[...]), split_heads(v_v[...]))
    result[...] = lanes_of(grads).astype(BF16)


def spatial_input_back_kernel(grad, tokens, mod, qkv_w, projected_grad, result, tokens_v, w_v, result_v, sems):
    copies = fetch([(tokens, tokens_v), (qkv_w.at[0], w_v)], sems.at[pl.ds(0, 2)])
    copies[0].wait()
    g = grad[...].reshape(TOK, D).astype(F32)
    unit, inverse = layer_norm(tokens_v[...].astype(F32))
    copies[1].wait()
    normed_grad = dot(projected_grad[...], w_v[...]).astype(BF16).astype(F32)
    x_grad = layer_norm_back(normed_grad * (1.0 + mod[0, 1, 0:1, :]), unit, inverse)
    result_v[...] = (g + x_grad).astype(BF16)
    wait_all(fetch([(result_v, result)], sems.at[pl.ds(2, 1)]))


def temporal_attention_kernel(
    place, located, mod, cosines, sines, qkv_w, out_w, branch_grad,
    attended_out, projected_grad, unit_out, inverse_out, w_out, sent, own, to_1, to_2, to_3,
    branch_v, o_v, cos_v, sin_v, sent_v, normed_v, qkv_v, factors_v, wide, in_sems, sems, factor_sems,
):
    copies = fetch(
        [(qkv_w.at[1, pl.ds(i * HW, HW)], w_out.at[pl.ds(i * HW, HW)]) for i in range(3)]
        + [(cosines, cos_v), (sines, sin_v), (out_w.at[1], o_v), (branch_grad, branch_v)],
        in_sems,
    )
    @pl.when(place[0] >= 0)
    def _():
        unit, inverse = layer_norm(located[...].reshape(TOK, D).astype(F32))
        unit_out[...] = unit
        inverse_out[...] = jnp.broadcast_to(inverse, (TOK, TOK))
        normed = (unit * (1.0 + mod[0, 1, 1:2, :]) + mod[0, 0, 1:2, :]).astype(BF16)
        normed_v[...] = normed
        sent_v[...] = regroup(normed)

    saves = fetch([(sent_v, sent)], sems)
    for i in range(3):
        copies[i].wait()

        @pl.when(place[0] >= 0)
        def _(i=i):
            qkv_v[i] = dot(normed_v[...], w_out[i * HW : (i + 1) * HW, :], NT).astype(BF16)

    parts = [qkv_v[i] for i in range(3)]
    wait_all(copies[3:5])
    cos, sin = cos_v[...], sin_v[...]

    def rotate(t):
        t = t.astype(F32)
        return (t * cos + swap_halves(t) * sin).astype(BF16)

    def rotate_back(t):
        t = t.astype(BF16).astype(F32)
        return t * cos + swap_halves(t * sin)

    q, k, v = rotate(parts[0]), rotate(parts[1]), parts[2]
    keys_by_head, values_by_head = split_heads(k), split_heads(v)
    row = lax.broadcasted_iota(jnp.int32, (TOK, TOK), 0)
    column = lax.broadcasted_iota(jnp.int32, (TOK, TOK), 1)
    same = lax.rem(row, 2) == lax.rem(column, 2)
    probs, attended = attend(q, keys_by_head, values_by_head, same)
    attended_out[...] = attended
    wait_all(copies[5:])
    attended_grad = dot(branch_v[...], o_v[...], NT).astype(BF16)
    q_grad, k_grad, v_grad = attend_back(probs, attended_grad, q, keys_by_head, values_by_head)
    grads = lanes_of([rotate_back(q_grad), rotate_back(k_grad), v_grad])
    projected_grad[...] = grads.astype(BF16)

    wide[: 3 * HW, :] = grads.T
    wide[3 * HW :, :] = attended.astype(F32).T
    empty = jnp.zeros((BLOCK - QKV_COLS - PROJ_ROWS, TOK), F32)
    for y in range(Y):
        pieces = []
        for s in range(PARTS):
            i = y * PARTS + s
            pieces += [
                wide[pl.ds(i * QKV_COLS, QKV_COLS), :],
                wide[pl.ds(3 * HW + i * PROJ_ROWS, PROJ_ROWS), :],
                empty,
            ]
        factors_v[y] = jnp.concatenate(pieces, axis=0).astype(BF16)
    saves += fetch(
        [(factors_v.at[lax.rem(place[0] + k, Y)], ref) for k, ref in enumerate((own, to_1, to_2, to_3))], factor_sems
    )
    wait_all(saves)


def temporal_input_back_kernel(projected_grad, qkv_w, seed, mod, unit, inverse, result, result_v, sem):
    g = seed[...].reshape(TOK, D).astype(F32)
    normed_grad = dot(projected_grad[...], qkv_w[...]).astype(BF16).astype(F32)
    x_grad = layer_norm_back(normed_grad * (1.0 + mod[0, 1, 1:2, :]), unit[...], inverse[:, 0:1])
    result_v[...] = (g + x_grad).astype(BF16).reshape(FRAMES, 2, D)
    save = pltpu.make_async_copy(result_v, result, sem)
    save.start()
    save.wait()


def block_out_kernel(attended, out_w, located, mod, result, o_v, located_v, result_v, sems):
    copies = fetch([(out_w.at[1], o_v), (located, located_v)], sems.at[pl.ds(0, 2)])
    wait_all(copies)
    x = located_v[...].reshape(TOK, D).astype(F32)
    branch = dot(attended[...], o_v[...])
    result_v[...] = (x + mod[0, 2, 1:2, :] * branch).astype(BF16).reshape(FRAMES, 2, D)
    wait_all(fetch([(result_v, result)], sems.at[pl.ds(2, 1)]))


def weight_grad_kernel(core, *refs):
    normed, branch_grad, factors = refs[0:Y], refs[Y : 2 * Y], refs[2 * Y : 3 * Y]
    keep, send, keep_v, send_v, sems = refs[3 * Y :]
    left = lanes_of([f[...] for f in factors])
    is_qkv = lax.rem(lax.broadcasted_iota(jnp.int32, (PARTS * BLOCK, 1), 0), BLOCK) < QKV_COLS
    from_normed = dot(left, rows_of([n[...] for n in normed]))
    from_branch = dot(left, rows_of([n[...] for n in branch_grad]))
    sums = jnp.where(is_qkv, from_normed, from_branch)
    tails = sums[:, 1024:].reshape(PARTS, 5, 8, TOK)
    first = core[0] == 0
    copies = []

    def chunk(d):
        main = [sums[:, d * 256 + i * TOK : d * 256 + (i + 1) * TOK].reshape(PARTS, BLOCK, TOK) for i in range(2)]
        packed = jnp.concatenate([tails[:, i, :, d * 32 : (d + 1) * 32] for i in range(4)], axis=-1)
        last = tails[:, 4]
        if d > 0:
            last = jnp.concatenate([last[:, :, d * 32 :], last[:, :, : d * 32]], axis=-1)
        return jnp.concatenate(main + [packed, last], axis=1)

    for x in range(2):
        a, b = chunk(2 * x), chunk(2 * x + 1)
        send_v[x] = jnp.where(first, b, a).astype(BF16)
        keep_v[x] = jnp.where(first, a, b).astype(BF16)
        copies += fetch([(send_v.at[x], send.at[x]), (keep_v.at[x], keep.at[x])], sems.at[x])
    wait_all(copies)


def add_kernel(a, b, result, result_v, sems):
    copies = []
    for i in range(2):
        result_v[i] = (a[i].astype(F32) + b[i].astype(F32)).astype(BF16)
        copies.append(pltpu.make_async_copy(result_v.at[i], result.at[i], sems.at[i]))
        copies[i].start()
    wait_all(copies)


def sum_kernel(parts, qkv, proj, qkv_v, proj_v, sems):
    total = parts[0].astype(F32)
    for i in range(1, 2 * PARTS):
        total = total + parts[i].astype(F32)
    packed, last = total[2 * BLOCK : 2 * BLOCK + 8], total[2 * BLOCK + 8 :]
    tail = jnp.concatenate([packed[:, i * 32 : (i + 1) * 32] for i in range(4)] + [last[:, :32]], axis=0)
    full = jnp.concatenate([total[:BLOCK], total[BLOCK : 2 * BLOCK], tail], axis=1)
    qkv_v[...] = full[:QKV_COLS]
    proj_v[...] = full[QKV_COLS : QKV_COLS + PROJ_ROWS]
    wait_all(fetch([(qkv_v, qkv), (proj_v, proj)], sems))


def call(kernel, name, inputs, outputs, scratch=(), mib=24, us=2.0):
    return pl.pallas_call(
        kernel,
        out_shape=tuple(space(shape, dtype) for space, dtype, shape in outputs),
        in_specs=[pl.BlockSpec(memory_space=space) for space, _ in inputs],
        out_specs=tuple(pl.BlockSpec(memory_space=space) for space, _, _ in outputs),
        scratch_shapes=list(scratch),
        compiler_params=pltpu.CompilerParams(vmem_limit_bytes=mib * 2**20),
        cost_estimate=pl.CostEstimate(flops=int(us * 1e9), bytes_accessed=int(us * 3e6), transcendentals=0),
        name=name,
    )(*[pltpu.with_memory_space_constraint(x, space) if space is not pltpu.SMEM else x for space, x in inputs])


def over(axis, size, k, x):
    return lax.ppermute(x, axis, [(i, (i + k) % size) for i in range(size)])


def hbm(n):
    return [pl.BlockSpec(memory_space=pltpu.HBM)] * n


def vmem(n):
    return [pl.BlockSpec(memory_space=pltpu.VMEM)] * n


def whole(*shape):
    return pl.BlockSpec(shape, lambda i: (0,) * len(shape))


def params(mib):
    return pltpu.CompilerParams(vmem_limit_bytes=mib * 2**20)


def out(dtype, *shape):
    return pltpu.HBM(shape, dtype)


def buf(dtype, *shape):
    return pltpu.VMEM(shape, dtype)


def dma(*n):
    return pltpu.SemaphoreType.DMA(n) if n else pltpu.SemaphoreType.DMA


HBM, VMEM, SMEM = pltpu.HBM, pltpu.VMEM, pltpu.SMEM
PAIRS = (FRAMES, 2, D)
MOD = (1, 3, 2, D)
QKV_W = (3 * HW, D)
OUT_W = (HW, D)
ATT = (TOK, HW)
PROB = (HEADS, TOK, TOK)
CHUNK = (96, TOK)
FACTOR = (PARTS * BLOCK, TOK)


def shards(tokens, modulation, frame_pos, qkv_weight, out_weight, seed_grad):
    seed = seed_grad.reshape(PAIRS)
    tokens = tokens.reshape(TOK, D)
    mod = modulation.transpose(0, 2, 1, 3)
    qkv_w = qkv_weight.swapaxes(1, 2)
    seq = ("y", "xl", "z")

    place = lax.axis_index("y").reshape(1).astype(jnp.int32)
    x1, q, k, v, p = call(
        spatial_forward_kernel,
        "spatial_forward",
        [(SMEM, place), (HBM, tokens), (HBM, mod), (HBM, qkv_w), (HBM, out_weight)],
        [(HBM, BF16, PAIRS), (HBM, BF16, ATT), (HBM, BF16, ATT), (HBM, BF16, ATT), (HBM, BF16, PROB)],
        [
            buf(BF16, TOK, D), buf(F32, *MOD), buf(BF16, *QKV_W), buf(BF16, *OUT_W), buf(BF16, TOK, D),
            buf(BF16, *PAIRS), buf(BF16, *ATT), buf(BF16, *ATT), buf(BF16, *ATT), buf(BF16, *PROB), dma(6), dma(5),
        ],
        us=5.0,
    )
    located = lax.all_to_all(x1, seq, split_axis=0, concat_axis=0, tiled=True)

    later_seed, later_pos, _ = lax.optimization_barrier((seed, frame_pos, x1))
    sent, branch_grad = call(
        branch_grad_kernel,
        "branch_grad",
        [(HBM, later_seed), (VMEM, mod)],
        [(HBM, BF16, (TOK, D)), (HBM, BF16, (TOK, D))],
        [buf(BF16, *PAIRS), buf(BF16, TOK, D), buf(BF16, TOK, D), dma(3)],
        us=2.0,
    )
    branch_all = [sent] + [over("y", Y, i, sent) for i in range(1, Y)]

    cosines, sines = call(
        tables_kernel,
        "tables",
        [(VMEM, later_pos.reshape(1, FRAMES))],
        [(HBM, F32, ATT), (HBM, F32, ATT)],
        [buf(F32, *ATT), buf(F32, *ATT), dma(2)],
        us=1.5,
    )
    located, branch_grad, cosines = lax.optimization_barrier((located, branch_grad, cosines))
    attended, projected_grad, unit, inverse, w1, normed, *factors = call(
        temporal_attention_kernel,
        "temporal_attention",
        [
            (SMEM, place), (VMEM, located), (VMEM, mod), (HBM, cosines), (HBM, sines), (HBM, qkv_w), (HBM, out_weight),
            (HBM, branch_grad),
        ],
        [
            (VMEM, BF16, ATT), (VMEM, BF16, (TOK, 3 * HW)), (VMEM, F32, (TOK, D)), (VMEM, F32, (TOK, TOK)),
            (VMEM, BF16, QKV_W), (HBM, BF16, (TOK, D)),
        ]
        + [(HBM, BF16, FACTOR)] * Y,
        [
            buf(BF16, TOK, D), buf(BF16, *OUT_W), buf(F32, *ATT), buf(F32, *ATT), buf(BF16, TOK, D),
            buf(BF16, TOK, D), buf(BF16, 3, *ATT), buf(BF16, Y, *FACTOR), buf(F32, 4 * HW, TOK), dma(7), dma(1), dma(Y),
        ],
        us=7.0,
    )
    normed_all = [normed] + [over("y", Y, i, normed) for i in range(1, Y)]
    factors = [factors[0]] + [over("y", Y, i, factors[i]) for i in range(1, Y)]
    (located_grad,) = call(
        temporal_input_back_kernel,
        "temporal_input_back",
        [(VMEM, projected_grad), (VMEM, w1), (VMEM, seed), (VMEM, mod), (VMEM, unit), (VMEM, inverse)],
        [(HBM, BF16, PAIRS)],
        [buf(BF16, *PAIRS), dma()],
        us=3.0,
    )
    framed_grad = lax.all_to_all(located_grad, seq, split_axis=0, concat_axis=0, tiled=True)

    core = lax.axis_index("core").reshape(1).astype(jnp.int32)
    keep, send = call(
        weight_grad_kernel,
        "weight_grad",
        [(SMEM, core)] + [(VMEM, x) for x in (*normed_all, *branch_all, *factors)],
        [(HBM, BF16, (2, PARTS, *CHUNK)), (HBM, BF16, (2, PARTS, *CHUNK))],
        [buf(BF16, 2, PARTS, *CHUNK), buf(BF16, 2, PARTS, *CHUNK), dma(2, 2)],
        us=4.6,
    )
    framed_grad, send = lax.optimization_barrier((framed_grad, send))
    received = lax.ppermute(send, "core", [(0, 1), (1, 0)])

    (halves,) = call(
        add_kernel,
        "add_cores",
        [(VMEM, keep), (VMEM, received)],
        [(HBM, BF16, (2, PARTS, *CHUNK))],
        [buf(BF16, 2, PARTS, *CHUNK), dma(2)],
        us=1.0,
    )
    parts = lax.all_to_all(
        halves.reshape(2 * PARTS, *CHUNK), ("xh", "xl", "z"), split_axis=0, concat_axis=0, tiled=True
    )

    framed_grad, attended, _ = lax.optimization_barrier((framed_grad, attended, halves))
    (projected_grad,) = call(
        spatial_attention_back_kernel,
        "spatial_attention_back",
        [(VMEM, framed_grad), (VMEM, mod), (HBM, out_weight), (HBM, q), (HBM, k), (HBM, v), (HBM, p)],
        [(VMEM, BF16, (TOK, 3 * HW))],
        [buf(BF16, *OUT_W), buf(BF16, *ATT), buf(BF16, *ATT), buf(BF16, *ATT), buf(BF16, *PROB), dma(5)],
        us=3.5,
    )
    (tokens_grad,) = call(
        spatial_input_back_kernel,
        "spatial_input_back",
        [(VMEM, framed_grad), (HBM, tokens), (VMEM, mod), (HBM, qkv_w), (VMEM, projected_grad)],
        [(HBM, BF16, (TOK, D))],
        [buf(BF16, TOK, D), buf(BF16, *QKV_W), buf(BF16, TOK, D), dma(3)],
        us=3.0,
    )
    (block_out,) = call(
        block_out_kernel,
        "block_out",
        [(VMEM, attended), (HBM, out_weight), (HBM, located), (VMEM, mod)],
        [(HBM, BF16, PAIRS)],
        [buf(BF16, *OUT_W), buf(BF16, *PAIRS), buf(BF16, *PAIRS), dma(3)],
        us=2.0,
    )
    qkv_grad, proj_grad = call(
        sum_kernel,
        "sum_parts",
        [(VMEM, parts)],
        [(HBM, F32, (QKV_COLS, WIDTH)), (HBM, F32, (PROJ_ROWS, WIDTH))],
        [buf(F32, QKV_COLS, WIDTH), buf(F32, PROJ_ROWS, WIDTH), dma(2)],
        us=1.5,
    )
    return (
        block_out.reshape(1, FRAMES, 2, D),
        tokens_grad.reshape(1, 1, LOC, D),
        qkv_grad.T,
        proj_grad,
    )


def solution(mesh):
    sizes = (2, 2, 4, 2, 8)
    split = Mesh(mesh.devices.reshape(sizes), ("xh", "core", "y", "xl", "z"))
    dp, seq = ("xh", "core"), ("y", "xl", "z")
    return jax.shard_map(
        shards,
        mesh=split,
        in_specs=(
            P(dp, seq, None, None),
            P(dp, None, None, None),
            P(),
            P(),
            P(),
            P(dp, None, seq, None),
        ),
        out_specs=(
            P(dp, None, seq, None),
            P(dp, seq, None, None),
            P(dp, seq),
            P(seq, dp),
        ),
        check_vma=False,
    )
```

time: 146 us -> 105 us (0.72)
  blocking collectives: 26.3 us -> 0 us
  local copies, waits for them, and re-layouts: 20.8 us -> 1.16 us
  starting transfers between devices: 20.6 us -> 37.7 us
  between operations: 14.3 us -> 1 us
  Pallas kernels: 28.6 us -> 34 us
  other arithmetic: 4.42 us -> 0 us
    all_to_all x1 -> x0, blocking collectives: 26.3 us -> none  [shards(): located = lax.all_to_all(x1, seq, split_axis=0, concat_axis=0, tiled=True)]
    unnamed x42 -> x16, local copies, waits for them, and re-layouts: 19.2 us -> 1.16 us
    ppermute x1 -> x9, starting transfers between devices: 1.47 us -> 13.1 us  [over(): return lax.ppermute(x, axis, [(i, (i + k) % size) for i in range(size)])]
    all_to_all x2, starting transfers between devices: 9.74 us -> 19 us  [the longest x1 12.7 us: shards(): located = lax.all_to_all(x1, seq, split_axis=0, concat_axis=0, tiled=True)]
    all_to_all x1, waiting for transfers between devices: 8.07 us -> 0.01 us  [shards(): lax.all_to_all(located_grad, seq, split_axis=0, concat_axis=0, tiled=True)]
    ppermute x1 -> x9, waiting for transfers between devices: 3.55 us -> 11.3 us  [over(): return lax.ppermute(x, axis, [(i, (i + k) % size) for i in range(size)])]
    pallas_call x8 -> x11, Pallas kernels: 28.6 us -> 34 us  [call(): pl.pallas_call(kernel, out_shape=tuple((space(shape, dtype) for space, dt...]
    all_to_all x1, starting transfers between devices: 9.19 us -> 5.54 us  [shards(): lax.all_to_all(located_grad, seq, split_axis=0, concat_axis=0, tiled=True)]
  transfers between devices with their start and end apart: 7 -> 13, of which waited for: 5 -> 6; matrix products, arithmetic and copies ran while one was open for 2% -> 0% of each run, Pallas kernels for 15% -> 26%
where the time goes in v3:
time: 105 us
  starting transfers between devices  37.7 us (36%)
  Pallas kernels  34 us (32%)
  waiting for transfers between devices  30.9 us (29%)
  local copies, waits for them, and re-layouts  1.16 us (1%)
    pallas_call x11, Pallas kernels, call(): pl.pallas_call(kernel, out_shape=tuple((space(shape, dtype) for space, dt...  34 us
    all_to_all x1, waiting for transfers between devices, shards(): lax.all_to_all(halves.reshape(2 * PARTS, *CHUNK), ('xh', 'xl', 'z'), spli...  13.3 us
    ppermute x9, starting transfers between devices, over(): return lax.ppermute(x, axis, [(i, (i + k) % size) for i in range(size)])  13.1 us
    all_to_all x1, starting transfers between devices, shards(): located = lax.all_to_all(x1, seq, split_axis=0, concat_axis=0, tiled=True)  12.7 us
    ppermute x9, waiting for transfers between devices, over(): return lax.ppermute(x, axis, [(i, (i + k) % size) for i in range(size)])  11.3 us
    all_to_all x1, starting transfers between devices, shards(): lax.all_to_all(halves.reshape(2 * PARTS, *CHUNK), ('xh', 'xl', 'z'), spli...  6.26 us
    all_to_all x1, starting transfers between devices, shards(): lax.all_to_all(located_grad, seq, split_axis=0, concat_axis=0, tiled=True)  5.54 us
    all_to_all x1, waiting for transfers between devices, shards(): located = lax.all_to_all(x1, seq, split_axis=0, concat_axis=0, tiled=True)  3.86 us
  transfers between devices with their start and end apart: 13, of which 6 were waited for; matrix products, arithmetic and copies ran while one was open for 0% of the time, Pallas kernels for 26%

profile of v3, /device:TPU:32, one launch (start us, length us, event | category | flops | bytes accessed | tf_op | source)
XLA Modules:
  0.0 104.8 jit_solution(17113587052386066289)
XLA Ops:
  0.6 0.0 copy-start.4
  0.6 5.5 %spatial_forward.1 = (bf16[64,2,1152]{2,1,0:T(2,128)(2,1)}, bf16[128,576]{1,0:T(8,128)(2,1)}, bf16[128,576]{1,0:T(8,128)(2,1)}, bf16[128,576]{1,0:T(8,128)(2,1)}, bf16[8,128,128]{2,1,0:T(8,128)(2,1)}) custom-call(s32[1]{0:T(128)} %bitcast.place, bf16[128,1152]{1,0:T(8,128)(2,1)} %bitcast.25, f32[1,3,2,1152]{3,2,1,0:T(2,128)} %bitcast.13, ...), custom_call_target="tpu_custom_call" | custom-call | flops 5000000000 | bytes 15000000 | tf_op jit(solution)/shard_map/spatial_forward/pallas_call | solution.py:357
  6.1 0.0 copy-start.5
  6.1 12.7 %all-to-all-start = ((bf16[64,2,1152]{2,1,0:T(2,128)(2,1)}), bf16[64,2,1152]{2,1,0:T(2,128)(2,1)S(1)}, u32[]{:S(2)}, u32[]{:S(2)}) async-start(bf16[64,2,1152]{2,1,0:T(2,128)(2,1)} %get-tuple-element.36), calls=%async_computation | async-start | bytes 589824 | tf_op jit(solution)/shard_map/all_to_all | solution.py:431
  18.8 0.0 copy-done.4
  18.9 2.0 %branch_grad.1 = (bf16[128,1152]{1,0:T(8,128)(2,1)}, bf16[128,1152]{1,0:T(8,128)(2,1)}) custom-call(bf16[64,2,1152]{2,1,0:T(2,128)(2,1)} %bitcast.11, f32[1,3,2,1152]{3,2,1,0:T(2,128)S(1)} %bitcast.14), custom_call_target="tpu_custom_call" | custom-call | flops 2000000000 | bytes 6000000 | tf_op jit(solution)/shard_map/branch_grad/pallas_call | solution.py:357
  20.9 1.5 %collective-permute-start.3 = (bf16[128,1152]{1,0:T(8,128)(2,1)}, bf16[128,1152]{1,0:T(8,128)(2,1)S(1)}, u32[]{:S(2)}, u32[]{:S(2)}) collective-permute-start(bf16[128,1152]{1,0:T(8,128)(2,1)} %get-tuple-element.50.refs_4_), channel_id=1, source_target_pairs={{0,16},{16,32},{32,48},{48,0},{1,17},{17,33},{33,49},{49,1},{2,18}... | collective-permute-start | bytes 884744 | tf_op jit(solution)/shard_map/ppermute | solution.py:370
  22.4 2.9 %collective-permute-start.4 = (bf16[128,1152]{1,0:T(8,128)(2,1)}, bf16[128,1152]{1,0:T(8,128)(2,1)S(1)}, u32[]{:S(2)}, u32[]{:S(2)}) collective-permute-start(bf16[128,1152]{1,0:T(8,128)(2,1)} %get-tuple-element.50.refs_4_), channel_id=1, source_target_pairs={{0,32},{16,48},{32,0},{48,16},{1,33},{17,49},{33,1},{49,17},{2,34}... | collective-permute-start | bytes 884744 | tf_op jit(solution)/shard_map/ppermute | solution.py:370
  25.3 1.4 %collective-permute-start.5 = (bf16[128,1152]{1,0:T(8,128)(2,1)}, bf16[128,1152]{1,0:T(8,128)(2,1)S(1)}, u32[]{:S(2)}, u32[]{:S(2)}) collective-permute-start(bf16[128,1152]{1,0:T(8,128)(2,1)} %get-tuple-element.50.refs_4_), channel_id=1, source_target_pairs={{0,48},{16,0},{32,16},{48,32},{1,49},{17,1},{33,17},{49,33},{2,50}... | collective-permute-start | bytes 884744 | tf_op jit(solution)/shard_map/ppermute | solution.py:370
  26.6 0.0 copy-done.5
  26.7 2.0 %tables.1 = (f32[128,576]{1,0:T(8,128)}, f32[128,576]{1,0:T(8,128)}) custom-call(s32[1,64]{1,0:T(1,128)S(1)} %bitcast.20), custom_call_target="tpu_custom_call" | custom-call | flops 1500000000 | bytes 4500000 | tf_op jit(solution)/shard_map/tables/pallas_call | solution.py:357
  28.7 3.9 %all-to-all-done.located = bf16[64,2,1152]{2,1,0:T(2,128)(2,1)S(1)} async-done(((bf16[64,2,1152]{2,1,0:T(2,128)(2,1)}), bf16[64,2,1152]{2,1,0:T(2,128)(2,1)S(1)}, u32[]{:S(2)}, u32[]{:S(2)}) %all-to-all-start) | async-done | bytes 294944 | tf_op jit(solution)/shard_map/all_to_all | solution.py:431
  32.5 0.0 copy-start
  32.5 0.0 copy-start.1
  32.5 7.7 %temporal_attention.1 = (bf16[128,576]{1,0:T(8,128)(2,1)S(1)}, bf16[128,1728]{1,0:T(8,128)(2,1)S(1)}, f32[128,1152]{1,0:T(8,128)S(1)}, f32[128,128]{1,0:T(8,128)...) custom-call(s32[1]{0:T(128)} %bitcast.place, ...), custom_call_target="tpu_custom_call" | custom-call | flops 7000000000 | bytes 21000000 | tf_op jit(solution)/shard_map/temporal_attention/pallas_call | solution.py:357
  40.2 0.0 copy-done
  40.2 0.1 collective-permute-start.6
  40.3 0.9 collective-permute-start
  41.3 0.0 collective-permute-done.3.refs_5_
  41.3 3.8 %collective-permute-start.1 = (bf16[128,1152]{1,0:T(8,128)(2,1)}, bf16[128,1152]{1,0:T(8,128)(2,1)S(1)}, u32[]{:S(2)}, u32[]{:S(2)}) collective-permute-start(bf16[128,1152]{1,0:T(8,128)(2,1)} %get-tuple-element.49.refs_0_), channel_id=1, source_target_pairs={{0,32},{16,48},{32,0},{48,16},{1,33},{17,49},{33,1},{49,17},{2,34}... | collective-permute-start | bytes 884744 | tf_op jit(solution)/shard_map/ppermute | solution.py:370
  45.0 0.0 collective-permute-done.4.refs_6_
  45.0 0.1 collective-permute-start.2
  45.2 0.0 collective-permute-done.5.refs_7_
  45.2 1.6 %collective-permute-start.7 = (bf16[640,128]{1,0:T(8,128)(2,1)}, bf16[640,128]{1,0:T(8,128)(2,1)S(1)}, u32[]{:S(2)}, u32[]{:S(2)}) collective-permute-start(bf16[640,128]{1,0:T(8,128)(2,1)} %get-tuple-element.53), channel_id=1, source_target_pairs={{0,32},{16,48},{32,0},{48,16},{1,33},{17,49},{33,1},{49,17},{2,34}... | collective-permute-start | bytes 491528 | tf_op jit(solution)/shard_map/ppermute | solution.py:370
  46.8 2.1 %collective-permute-done.6.refs_9_ = bf16[640,128]{1,0:T(8,128)(2,1)S(1)} collective-permute-done((bf16[640,128]{1,0:T(8,128)(2,1)}, bf16[640,128]{1,0:T(8,128)(2,1)S(1)}, u32[]{:S(2)}, u32[]{:S(2)}) %collective-permute-start.6) | collective-permute-done | bytes 163872 | tf_op jit(solution)/shard_map/ppermute | solution.py:370
  48.9 0.9 collective-permute-start.8
  49.7 0.0 copy-done.1
  49.7 0.0 copy-start.2
  49.7 0.0 copy-start.3
  49.7 0.0 copy-start.7
  49.8 1.9 %temporal_input_back.1 = bf16[64,2,1152]{2,1,0:T(2,128)(2,1)} custom-call(bf16[128,1728]{1,0:T(8,128)(2,1)S(1)} %get-tuple-element.45.projected_grad, bf16[1728,1152]{1,0:T(8,128)(2,1)S(1)} %get-tuple-element.46.qkv_w, bf16[64,2,1152]{2,1,0:T(2,128)(2,1)S(1)} %bitcast.12, f32[1,3,2,1152]{3,2,1,0:T(2,128)S(1)} %bitcast.16, ...), custom_call_target="tpu_custom_call" | custom-call | flops 3000000000 | bytes 9000000 | tf_op jit(solution)/shard_map/temporal_input_back/pallas_call | solution.py:357
  51.6 5.5 %all-to-all-start.1 = ((bf16[64,2,1152]{2,1,0:T(2,128)(2,1)}), bf16[64,2,1152]{2,1,0:T(2,128)(2,1)S(1)}, u32[]{:S(2)}, u32[]{:S(2)}) async-start(bf16[64,2,1152]{2,1,0:T(2,128)(2,1)} %temporal_input_back.1), calls=%async_computation.1 | async-start | bytes 589824 | tf_op jit(solution)/shard_map/all_to_all | solution.py:481
  57.2 6.7 %collective-permute-done.7.refs_10_ = bf16[640,128]{1,0:T(8,128)(2,1)S(1)} collective-permute-done((bf16[640,128]{1,0:T(8,128)(2,1)}, bf16[640,128]{1,0:T(8,128)(2,1)S(1)}, u32[]{:S(2)}, u32[]{:S(2)}) %collective-permute-start.7) | collective-permute-done | bytes 163872 | tf_op jit(solution)/shard_map/ppermute | solution.py:370
  63.9 2.4 %collective-permute-done.8.refs_11_ = bf16[640,128]{1,0:T(8,128)(2,1)S(1)} collective-permute-done((bf16[640,128]{1,0:T(8,128)(2,1)}, bf16[640,128]{1,0:T(8,128)(2,1)S(1)}, u32[]{:S(2)}, u32[]{:S(2)}) %collective-permute-start.8) | collective-permute-done | bytes 163872 | tf_op jit(solution)/shard_map/ppermute | solution.py:370
  66.3 0.0 collective-permute-done.refs_1_
  66.3 0.0 collective-permute-done.1.refs_2_
  66.3 0.0 collective-permute-done.2.refs_3_
  66.3 0.0 copy-done.2
  66.3 0.0 copy-done.3
  66.4 0.0 copy-done.7
  66.4 3.2 %weight_grad.1 = (bf16[2,16,96,128]{3,2,1,0:T(8,128)(2,1)}, bf16[2,16,96,128]{3,2,1,0:T(8,128)(2,1)}) custom-call(s32[1]{0:T(128)} %bitcast.6.core, bf16[128,1152]{1,0:T(8,128)(2,1)S(1)} %copy-done.3, bf16[128,1152]{1,0:T(8,128)(2,1)S(1)} %collective-permute-done.refs_1_, bf16[128,1152]{1,0:T(8,128)(2,1)S(1)} %collective-permute-done.1.refs_2_, ...), custom_call_target="tpu_custom_call" | custom-call | flops 4600000000 | bytes 13799999 | tf_op jit(solution)/shard_map/weight_grad/pallas_call | solution.py:357
  69.6 0.0 all-to-all-done.1.grad
  69.6 0.1 collective-permute-start.9
  69.7 2.5 %collective-permute-done.9.b = bf16[2,16,96,128]{3,2,1,0:T(8,128)(2,1)S(1)} collective-permute-done((bf16[2,16,96,128]{3,2,1,0:T(8,128)(2,1)}, bf16[2,16,96,128]{3,2,1,0:T(8,128)(2,1)S(1)}, u32[]{:S(2)}, u32[]{:S(2)}) %collective-permute-start.9) | collective-permute-done | bytes 786464 | tf_op jit(solution)/shard_map/ppermute | solution.py:493
  72.2 0.0 copy-start.6
  72.2 1.1 %copy-done.6 = bf16[2,16,96,128]{3,2,1,0:T(8,128)(2,1)S(1)} copy-done((bf16[2,16,96,128]{3,2,1,0:T(8,128)(2,1)S(1)}, bf16[2,16,96,128]{3,2,1,0:T(8,128)(2,1)}, u32[]{:S(2)}) %copy-start.6) | copy-done | bytes 786456
  73.3 1.0 add_cores.1
  74.3 6.3 %all-to-all-start.2 = ((bf16[32,96,128]{2,1,0:T(8,128)(2,1)}), bf16[32,96,128]{2,1,0:T(8,128)(2,1)S(1)}, u32[]{:S(2)}, u32[]{:S(2)}) async-start(bf16[32,96,128]{2,1,0:T(8,128)(2,1)} %bitcast.21), calls=%async_computation.2 | async-start | bytes 1572864 | tf_op jit(solution)/shard_map/all_to_all | solution.py:503
  80.6 2.6 %block_out.1 = bf16[64,2,1152]{2,1,0:T(2,128)(2,1)} custom-call(bf16[128,576]{1,0:T(8,128)(2,1)S(1)} %get-tuple-element.60.attended, bf16[2,576,1152]{2,1,0:T(8,128)(2,1)} %out_w.7, bf16[64,2,1152]{2,1,0:T(2,128)(2,1)} %copy-done, f32[1,3,2,1152]{3,2,1,0:T(2,128)S(1)} %bitcast.17), custom_call_target="tpu_custom_call" | custom-call | flops 2000000000 | bytes 6000000 | tf_op jit(solution)/shard_map/block_out/pallas_call | solution.py:357
  83.2 3.2 %spatial_attention_back.1.projected_grad = bf16[128,1728]{1,0:T(8,128)(2,1)S(1)} custom-call(bf16[64,2,1152]{2,1,0:T(2,128)(2,1)S(1)} %all-to-all-done.1.grad, f32[1,3,2,1152]{3,2,1,0:T(2,128)S(1)} %bitcast.18, bf16[2,576,1152]{2,1,0:T(8,128)(2,1)} %out_w.7, bf16[128,576]{1,0:T(8,128)(2,1)} %get-tuple-element.62.q_in, ...), custom_call_target="tpu_custom_call" | custom-call | flops 3500000000 | bytes 10500000 | tf_op jit(solution)/shard_map/spatial_attention_back/pallas_call | solution.py:357
  86.5 4.1 %spatial_input_back.1 = bf16[128,1152]{1,0:T(8,128)(2,1)} custom-call(bf16[64,2,1152]{2,1,0:T(2,128)(2,1)S(1)} %all-to-all-done.1.grad, bf16[128,1152]{1,0:T(8,128)(2,1)} %bitcast.26, f32[1,3,2,1152]{3,2,1,0:T(2,128)S(1)} %bitcast.19, bf16[2,1728,1152]{2,1,0:T(8,128)(2,1)} %bitcast.24, bf16[128,1728]{1,0:T(8,128)(2,1)S(1)} %spatial_attention_back.1.projected_grad), custom_call_target="tpu_custom_call" | custom-call | flops 3000000000 | bytes 9000000 | tf_op jit(solution)/shard_map/spatial_input_back/pallas_call | solution.py:357
  90.6 13.3 %all-to-all-done.2.parts = bf16[32,96,128]{2,1,0:T(8,128)(2,1)S(1)} async-done(((bf16[32,96,128]{2,1,0:T(8,128)(2,1)}), bf16[32,96,128]{2,1,0:T(8,128)(2,1)S(1)}, u32[]{:S(2)}, u32[]{:S(2)}) %all-to-all-start.2) | async-done | bytes 786464 | tf_op jit(solution)/shard_map/all_to_all | solution.py:503
  103.9 0.8 sum_parts.1
Async XLA Ops:
  0.6 18.2 %copy-start.4 = (f32[1,2,3,1152]{3,1,2,0:T(2,128)S(1)}, f32[1,2,3,1152]{3,1,2,0:T(2,128)}, u32[]{:S(2)}) copy-start(f32[1,2,3,1152]{3,1,2,0:T(2,128)} %param.7) | copy-start | bytes 82948
  6.1 20.5 %copy-start.5 = (s32[64]{0:T(128)S(1)}, s32[64]{0:T(128)}, u32[]{:S(2)}) copy-start(s32[64]{0:T(128)} %param.8) | copy-start | bytes 772
  6.1 26.4 %all-to-all-start = ((bf16[64,2,1152]{2,1,0:T(2,128)(2,1)}), bf16[64,2,1152]{2,1,0:T(2,128)(2,1)S(1)}, u32[]{:S(2)}, u32[]{:S(2)}) async-start(bf16[64,2,1152]{2,1,0:T(2,128)(2,1)} %get-tuple-element.36), calls=%async_computation | async-start | bytes 589824 | tf_op jit(solution)/shard_map/all_to_all | solution.py:431
  20.9 20.4 %collective-permute-start.3 = (bf16[128,1152]{1,0:T(8,128)(2,1)}, bf16[128,1152]{1,0:T(8,128)(2,1)S(1)}, u32[]{:S(2)}, u32[]{:S(2)}) collective-permute-start(bf16[128,1152]{1,0:T(8,128)(2,1)} %get-tuple-element.50.refs_4_), channel_id=1, source_target_pairs={{0,16},{16,32},{32,48},{48,0},{1,17},{17,33},{33,49},{49,1},{2,18}... | collective-permute-start | bytes 884744 | tf_op jit(solution)/shard_map/ppermute | solution.py:370
  22.4 22.6 %collective-permute-start.4 = (bf16[128,1152]{1,0:T(8,128)(2,1)}, bf16[128,1152]{1,0:T(8,128)(2,1)S(1)}, u32[]{:S(2)}, u32[]{:S(2)}) collective-permute-start(bf16[128,1152]{1,0:T(8,128)(2,1)} %get-tuple-element.50.refs_4_), channel_id=1, source_target_pairs={{0,32},{16,48},{32,0},{48,16},{1,33},{17,49},{33,1},{49,17},{2,34}... | collective-permute-start | bytes 884744 | tf_op jit(solution)/shard_map/ppermute | solution.py:370
  25.3 19.9 %collective-permute-start.5 = (bf16[128,1152]{1,0:T(8,128)(2,1)}, bf16[128,1152]{1,0:T(8,128)(2,1)S(1)}, u32[]{:S(2)}, u32[]{:S(2)}) collective-permute-start(bf16[128,1152]{1,0:T(8,128)(2,1)} %get-tuple-element.50.refs_4_), channel_id=1, source_target_pairs={{0,48},{16,0},{32,16},{48,32},{1,49},{17,1},{33,17},{49,33},{2,50}... | collective-permute-start | bytes 884744 | tf_op jit(solution)/shard_map/ppermute | solution.py:370
  32.5 7.7 %copy-start = (bf16[64,2,1152]{2,1,0:T(2,128)(2,1)}, bf16[64,2,1152]{2,1,0:T(2,128)(2,1)S(1)}, u32[]{:S(2)}) copy-start(bf16[64,2,1152]{2,1,0:T(2,128)(2,1)S(1)} %all-to-all-done.located) | copy-start | bytes 884740
  32.5 17.2 %copy-start.1 = (bf16[1,64,2,1152]{3,2,1,0:T(2,128)(2,1)S(1)}, bf16[1,64,2,1152]{3,2,1,0:T(2,128)(2,1)}, u32[]{:S(2)}) copy-start(bf16[1,64,2,1152]{3,2,1,0:T(2,128)(2,1)} %param.11) | copy-start | bytes 884740
  40.2 8.6 %collective-permute-start.6 = (bf16[640,128]{1,0:T(8,128)(2,1)}, bf16[640,128]{1,0:T(8,128)(2,1)S(1)}, u32[]{:S(2)}, u32[]{:S(2)}) collective-permute-start(bf16[640,128]{1,0:T(8,128)(2,1)} %get-tuple-element.52), channel_id=1, source_target_pairs={{0,16},{16,32},{32,48},{48,0},{1,17},{17,33},{33,49},{49,1},{2,18}... | collective-permute-start | bytes 491528 | tf_op jit(solution)/shard_map/ppermute | solution.py:370
  40.3 26.0 %collective-permute-start = (bf16[128,1152]{1,0:T(8,128)(2,1)}, bf16[128,1152]{1,0:T(8,128)(2,1)S(1)}, u32[]{:S(2)}, u32[]{:S(2)}) collective-permute-start(bf16[128,1152]{1,0:T(8,128)(2,1)} %get-tuple-element.49.refs_0_), channel_id=1, source_target_pairs={{0,16},{16,32},{32,48},{48,0},{1,17},{17,33},{33,49},{49,1},{2,18}... | collective-permute-start | bytes 884744 | tf_op jit(solution)/shard_map/ppermute | solution.py:370
  41.3 25.1 %collective-permute-start.1 = (bf16[128,1152]{1,0:T(8,128)(2,1)}, bf16[128,1152]{1,0:T(8,128)(2,1)S(1)}, u32[]{:S(2)}, u32[]{:S(2)}) collective-permute-start(bf16[128,1152]{1,0:T(8,128)(2,1)} %get-tuple-element.49.refs_0_), channel_id=1, source_target_pairs={{0,32},{16,48},{32,0},{48,16},{1,33},{17,49},{33,1},{49,17},{2,34}... | collective-permute-start | bytes 884744 | tf_op jit(solution)/shard_map/ppermute | solution.py:370
  45.0 21.3 %collective-permute-start.2 = (bf16[128,1152]{1,0:T(8,128)(2,1)}, bf16[128,1152]{1,0:T(8,128)(2,1)S(1)}, u32[]{:S(2)}, u32[]{:S(2)}) collective-permute-start(bf16[128,1152]{1,0:T(8,128)(2,1)} %get-tuple-element.49.refs_0_), channel_id=1, source_target_pairs={{0,48},{16,0},{32,16},{48,32},{1,49},{17,1},{33,17},{49,33},{2,50}... | collective-permute-start | bytes 884744 | tf_op jit(solution)/shard_map/ppermute | solution.py:370
  45.2 18.8 %collective-permute-start.7 = (bf16[640,128]{1,0:T(8,128)(2,1)}, bf16[640,128]{1,0:T(8,128)(2,1)S(1)}, u32[]{:S(2)}, u32[]{:S(2)}) collective-permute-start(bf16[640,128]{1,0:T(8,128)(2,1)} %get-tuple-element.53), channel_id=1, source_target_pairs={{0,32},{16,48},{32,0},{48,16},{1,33},{17,49},{33,1},{49,17},{2,34}... | collective-permute-start | bytes 491528 | tf_op jit(solution)/shard_map/ppermute | solution.py:370
  48.9 17.4 %collective-permute-start.8 = (bf16[640,128]{1,0:T(8,128)(2,1)}, bf16[640,128]{1,0:T(8,128)(2,1)S(1)}, u32[]{:S(2)}, u32[]{:S(2)}) collective-permute-start(bf16[640,128]{1,0:T(8,128)(2,1)} %get-tuple-element.54), channel_id=1, source_target_pairs={{0,48},{16,0},{32,16},{48,32},{1,49},{17,1},{33,17},{49,33},{2,50}... | collective-permute-start | bytes 491528 | tf_op jit(solution)/shard_map/ppermute | solution.py:370
  49.7 16.6 %copy-start.2 = (bf16[128,1152]{1,0:T(8,128)(2,1)S(1)}, bf16[128,1152]{1,0:T(8,128)(2,1)}, u32[]{:S(2)}) copy-start(bf16[128,1152]{1,0:T(8,128)(2,1)} %get-tuple-element.50.refs_4_) | copy-start | bytes 884740
  49.7 16.6 %copy-start.3 = (bf16[128,1152]{1,0:T(8,128)(2,1)S(1)}, bf16[128,1152]{1,0:T(8,128)(2,1)}, u32[]{:S(2)}) copy-start(bf16[128,1152]{1,0:T(8,128)(2,1)} %get-tuple-element.49.refs_0_) | copy-start | bytes 884740
  49.7 16.6 %copy-start.7 = (bf16[640,128]{1,0:T(8,128)(2,1)S(1)}, bf16[640,128]{1,0:T(8,128)(2,1)}, u32[]{:S(2)}) copy-start(bf16[640,128]{1,0:T(8,128)(2,1)} %get-tuple-element.51.refs_8_) | copy-start | bytes 491524
  51.6 18.0 %all-to-all-start.1 = ((bf16[64,2,1152]{2,1,0:T(2,128)(2,1)}), bf16[64,2,1152]{2,1,0:T(2,128)(2,1)S(1)}, u32[]{:S(2)}, u32[]{:S(2)}) async-start(bf16[64,2,1152]{2,1,0:T(2,128)(2,1)} %temporal_input_back.1), calls=%async_computation.1 | async-start | bytes 589824 | tf_op jit(solution)/shard_map/all_to_all | solution.py:481
  69.6 2.6 %collective-permute-start.9 = (bf16[2,16,96,128]{3,2,1,0:T(8,128)(2,1)}, bf16[2,16,96,128]{3,2,1,0:T(8,128)(2,1)S(1)}, u32[]{:S(2)}, u32[]{:S(2)}) collective-permute-start(bf16[2,16,96,128]{3,2,1,0:T(8,128)(2,1)} %get-tuple-element.59), channel_id=1, source_target_pairs={{0,64},{64,0},{1,65},{65,1},{2,66},{66,2},{3,67},{67,3},{4,68},{68... | collective-permute-start | bytes 2359304 | tf_op jit(solution)/shard_map/ppermute | solution.py:493
  72.2 1.1 %copy-start.6 = (bf16[2,16,96,128]{3,2,1,0:T(8,128)(2,1)S(1)}, bf16[2,16,96,128]{3,2,1,0:T(8,128)(2,1)}, u32[]{:S(2)}) copy-start(bf16[2,16,96,128]{3,2,1,0:T(8,128)(2,1)} %get-tuple-element.58.a) | copy-start | bytes 2359300
  74.3 29.6 %all-to-all-start.2 = ((bf16[32,96,128]{2,1,0:T(8,128)(2,1)}), bf16[32,96,128]{2,1,0:T(8,128)(2,1)S(1)}, u32[]{:S(2)}, u32[]{:S(2)}) async-start(bf16[32,96,128]{2,1,0:T(8,128)(2,1)} %bitcast.21), calls=%async_computation.2 | async-start | bytes 1572864 | tf_op jit(solution)/shard_map/all_to_all | solution.py:503

commit v4 on v3

--- a/solution.py
+++ b/solution.py
@@ -116,6 +116,11 @@
     return fetch(pairs, sems)
 
 
+def start_all(copies):
+    for c in copies:
+        c.start()
+
+
 def wait_all(copies):
     for c in copies:
         c.wait()
@@ -158,12 +163,10 @@
     place, tokens, mod, qkv_w, out_w, x1, q_out, k_out, v_out, p_out,
     tokens_v, mod_v, w_v, o_v, normed_v, x1_v, q_v, k_v, v_v, p_v, in_sem, out_sem,
 ):
-    copies = fetch(
-        [(tokens, tokens_v), (mod, mod_v)]
-        + [(qkv_w.at[0, pl.ds(i * HW, HW)], w_v.at[pl.ds(i * HW, HW)]) for i in range(3)]
-        + [(out_w.at[0], o_v)],
-        in_sem,
-    )
+    pairs = [(tokens, tokens_v), (mod, mod_v)]
+    pairs += [(qkv_w.at[0, pl.ds(i * HW, HW)], w_v.at[pl.ds(i * HW, HW)]) for i in range(3)] + [(out_w.at[0], o_v)]
+    copies = [pltpu.make_async_copy(src, dst, in_sem.at[i]) for i, (src, dst) in enumerate(pairs)]
+    start_all(copies)
     wait_all(copies[:2])
 
     @pl.when(place[0] >= 0)
@@ -216,14 +219,13 @@
 
 def temporal_attention_kernel(
     place, located, mod, cosines, sines, qkv_w, out_w, branch_grad,
-    attended_out, projected_grad, unit_out, inverse_out, w_out, sent, own, to_1, to_2, to_3,
+    attended_out, projected_grad, unit_out, inverse_out, w_out, own, to_1, to_2, to_3,
     branch_v, o_v, cos_v, sin_v, sent_v, normed_v, qkv_v, factors_v, wide, in_sems, sems, factor_sems,
 ):
-    copies = fetch(
-        [(qkv_w.at[1, pl.ds(i * HW, HW)], w_out.at[pl.ds(i * HW, HW)]) for i in range(3)]
-        + [(cosines, cos_v), (sines, sin_v), (out_w.at[1], o_v), (branch_grad, branch_v)],
-        in_sems,
-    )
+    pairs = [(qkv_w.at[1, pl.ds(i * HW, HW)], w_out.at[pl.ds(i * HW, HW)]) for i in range(3)]
+    pairs += [(cosines, cos_v), (sines, sin_v), (out_w.at[1], o_v), (branch_grad, branch_v)]
+    copies = [pltpu.make_async_copy(src, dst, in_sems.at[i]) for i, (src, dst) in enumerate(pairs)]
+    start_all(copies)
     @pl.when(place[0] >= 0)
     def _():
         unit, inverse = layer_norm(located[...].reshape(TOK, D).astype(F32))
@@ -231,9 +233,11 @@
         inverse_out[...] = jnp.broadcast_to(inverse, (TOK, TOK))
         normed = (unit * (1.0 + mod[0, 1, 1:2, :]) + mod[0, 0, 1:2, :]).astype(BF16)
         normed_v[...] = normed
-        sent_v[...] = regroup(normed)
-
-    saves = fetch([(sent_v, sent)], sems)
+        grouped = regroup(normed)
+        sent_v[...] = rows_of([grouped[:, t * TOK : (t + 1) * TOK] for t in range(D // TOK)])
+
+    messages = (own, to_1, to_2, to_3)
+    saves = fetch([(sent_v, ref.at[pl.ds(FACTOR[0], D)]) for ref in messages], sems)
     for i in range(3):
         copies[i].wait()
 
@@ -280,7 +284,8 @@
             ]
         factors_v[y] = jnp.concatenate(pieces, axis=0).astype(BF16)
     saves += fetch(
-        [(factors_v.at[lax.rem(place[0] + k, Y)], ref) for k, ref in enumerate((own, to_1, to_2, to_3))], factor_sems
+        [(factors_v.at[lax.rem(place[0] + k, Y)], ref.at[pl.ds(0, FACTOR[0])]) for k, ref in enumerate(messages)],
+        factor_sems,
     )
     wait_all(saves)
 
@@ -305,11 +310,12 @@
 
 
 def weight_grad_kernel(core, *refs):
-    normed, branch_grad, factors = refs[0:Y], refs[Y : 2 * Y], refs[2 * Y : 3 * Y]
-    keep, send, keep_v, send_v, sems = refs[3 * Y :]
-    left = lanes_of([f[...] for f in factors])
+    messages, branch_grad = refs[0:Y], refs[Y : 2 * Y]
+    keep, send_0, send_1, keep_v, send_v, sems = refs[2 * Y :]
+    left = lanes_of([m[: FACTOR[0]] for m in messages])
+    normed = [lanes_of([m[FACTOR[0] + t * TOK : FACTOR[0] + (t + 1) * TOK] for t in range(D // TOK)]) for m in messages]
     is_qkv = lax.rem(lax.broadcasted_iota(jnp.int32, (PARTS * BLOCK, 1), 0), BLOCK) < QKV_COLS
-    from_normed = dot(left, rows_of([n[...] for n in normed]))
+    from_normed = dot(left, rows_of(normed))
     from_branch = dot(left, rows_of([n[...] for n in branch_grad]))
     sums = jnp.where(is_qkv, from_normed, from_branch)
     tails = sums[:, 1024:].reshape(PARTS, 5, 8, TOK)
@@ -322,22 +328,28 @@
         last = tails[:, 4]
         if d > 0:
             last = jnp.concatenate([last[:, :, d * 32 :], last[:, :, : d * 32]], axis=-1)
-        return jnp.concatenate(main + [packed, last], axis=1)
+        rest = [m[:, 32:36] for m in main]
+        whole_chunk = jnp.concatenate([m[:, :32] for m in main] + rest + [packed, last], axis=1)
+        return whole_chunk.reshape(FLAT)
 
     for x in range(2):
         a, b = chunk(2 * x), chunk(2 * x + 1)
         send_v[x] = jnp.where(first, b, a).astype(BF16)
         keep_v[x] = jnp.where(first, a, b).astype(BF16)
-        copies += fetch([(send_v.at[x], send.at[x]), (keep_v.at[x], keep.at[x])], sems.at[x])
+        copies += fetch([(send_v.at[x], (send_0, send_1)[x]), (keep_v.at[x], keep.at[x])], sems.at[x])
     wait_all(copies)
 
 
-def add_kernel(a, b, result, result_v, sems):
+def load_kernel(*refs):
+    half = len(refs) // 2
+    wait_all(fetch(list(zip(refs[:half], refs[half : 2 * half], strict=True)), refs[-1]))
+
+
+def add_kernel(kept, received_0, received_1, result, result_v, sems):
     copies = []
-    for i in range(2):
-        result_v[i] = (a[i].astype(F32) + b[i].astype(F32)).astype(BF16)
-        copies.append(pltpu.make_async_copy(result_v.at[i], result.at[i], sems.at[i]))
-        copies[i].start()
+    for i, received in enumerate((received_0, received_1)):
+        result_v[i] = (kept[i].astype(F32) + received[...].astype(F32)).astype(BF16)
+        copies += fetch([(result_v.at[i], result.at[i])], sems.at[pl.ds(i, 1)])
     wait_all(copies)
 
 
@@ -345,9 +357,10 @@
     total = parts[0].astype(F32)
     for i in range(1, 2 * PARTS):
         total = total + parts[i].astype(F32)
-    packed, last = total[2 * BLOCK : 2 * BLOCK + 8], total[2 * BLOCK + 8 :]
-    tail = jnp.concatenate([packed[:, i * 32 : (i + 1) * 32] for i in range(4)] + [last[:, :32]], axis=0)
-    full = jnp.concatenate([total[:BLOCK], total[BLOCK : 2 * BLOCK], tail], axis=1)
+    packed, last = total[72:80], total[80:88]
+    tail = jnp.concatenate([packed[:, i * 32 : (i + 1) * 32] for i in range(4)] + [last[:4, :32]], axis=0)
+    main = [jnp.concatenate([total[:32], total[64:68]], axis=0), jnp.concatenate([total[32:64], total[68:72]], axis=0)]
+    full = jnp.concatenate(main + [tail], axis=1)
     qkv_v[...] = full[:QKV_COLS]
     proj_v[...] = full[QKV_COLS : QKV_COLS + PROJ_ROWS]
     wait_all(fetch([(qkv_v, qkv), (proj_v, proj)], sems))
@@ -405,8 +418,10 @@
 OUT_W = (HW, D)
 ATT = (TOK, HW)
 PROB = (HEADS, TOK, TOK)
-CHUNK = (96, TOK)
+CHUNK = (88, TOK)
+FLAT = (PARTS * 88, TOK)
 FACTOR = (PARTS * BLOCK, TOK)
+MESSAGE = (FACTOR[0] + D, TOK)
 
 
 def shards(tokens, modulation, frame_pos, qkv_weight, out_weight, seed_grad):
@@ -450,7 +465,7 @@
         us=1.5,
     )
     located, branch_grad, cosines = lax.optimization_barrier((located, branch_grad, cosines))
-    attended, projected_grad, unit, inverse, w1, normed, *factors = call(
+    attended, projected_grad, unit, inverse, w1, *messages = call(
         temporal_attention_kernel,
         "temporal_attention",
         [
@@ -459,17 +474,17 @@
         ],
         [
             (VMEM, BF16, ATT), (VMEM, BF16, (TOK, 3 * HW)), (VMEM, F32, (TOK, D)), (VMEM, F32, (TOK, TOK)),
-            (VMEM, BF16, QKV_W), (HBM, BF16, (TOK, D)),
+            (VMEM, BF16, QKV_W),
         ]
-        + [(HBM, BF16, FACTOR)] * Y,
+        + [(HBM, BF16, MESSAGE)] * Y,
         [
-            buf(BF16, TOK, D), buf(BF16, *OUT_W), buf(F32, *ATT), buf(F32, *ATT), buf(BF16, TOK, D),
-            buf(BF16, TOK, D), buf(BF16, 3, *ATT), buf(BF16, Y, *FACTOR), buf(F32, 4 * HW, TOK), dma(7), dma(1), dma(Y),
+            buf(BF16, TOK, D), buf(BF16, *OUT_W), buf(F32, *ATT), buf(F32, *ATT), buf(BF16, D, TOK),
+            buf(BF16, TOK, D), buf(BF16, 3, *ATT), buf(BF16, Y, *FACTOR), buf(F32, 4 * HW, TOK), dma(7), dma(Y), dma(Y),
         ],
         us=7.0,
     )
-    normed_all = [normed] + [over("y", Y, i, normed) for i in range(1, Y)]
-    factors = [factors[0]] + [over("y", Y, i, factors[i]) for i in range(1, Y)]
+    messages = [messages[0]] + [over("y", Y, i, messages[i]) for i in range(1, Y)]
+    projected_grad, branch_all = lax.optimization_barrier((projected_grad, branch_all))
     (located_grad,) = call(
         temporal_input_back_kernel,
         "temporal_input_back",
@@ -480,24 +495,39 @@
     )
     framed_grad = lax.all_to_all(located_grad, seq, split_axis=0, concat_axis=0, tiled=True)
 
+    own_message, own_branch, _ = lax.optimization_barrier((messages[0], branch_all[0], located_grad))
+    own_message, own_branch = call(
+        load_kernel,
+        "load_own",
+        [(HBM, own_message), (HBM, own_branch)],
+        [(VMEM, BF16, MESSAGE), (VMEM, BF16, (TOK, D))],
+        [dma(2)],
+        us=1.0,
+    )
+    messages, branch_all = [own_message] + messages[1:], [own_branch] + branch_all[1:]
     core = lax.axis_index("core").reshape(1).astype(jnp.int32)
-    keep, send = call(
+    keep, send_0, send_1 = call(
         weight_grad_kernel,
         "weight_grad",
-        [(SMEM, core)] + [(VMEM, x) for x in (*normed_all, *branch_all, *factors)],
-        [(HBM, BF16, (2, PARTS, *CHUNK)), (HBM, BF16, (2, PARTS, *CHUNK))],
-        [buf(BF16, 2, PARTS, *CHUNK), buf(BF16, 2, PARTS, *CHUNK), dma(2, 2)],
+        [(SMEM, core)] + [(VMEM, x) for x in (*messages, *branch_all)],
+        [(HBM, BF16, (2, *FLAT)), (HBM, BF16, FLAT), (HBM, BF16, FLAT)],
+        [buf(BF16, 2, *FLAT), buf(BF16, 2, *FLAT), dma(2, 2)],
         us=4.6,
     )
-    framed_grad, send = lax.optimization_barrier((framed_grad, send))
-    received = lax.ppermute(send, "core", [(0, 1), (1, 0)])
-
+    framed_grad, send_1 = lax.optimization_barrier((framed_grad, send_1))
+    swap = [(0, 1), (1, 0)]
+    received = [lax.ppermute(send, "core", swap) for send in (send_0, send_1)]
+
+    framed_grad, keep_later = lax.optimization_barrier((framed_grad, keep))
+    (kept,) = call(
+        load_kernel, "load", [(HBM, keep_later)], [(VMEM, BF16, (2, *FLAT))], [dma(1)], us=1.0
+    )
     (halves,) = call(
         add_kernel,
         "add_cores",
-        [(VMEM, keep), (VMEM, received)],
-        [(HBM, BF16, (2, PARTS, *CHUNK))],
-        [buf(BF16, 2, PARTS, *CHUNK), dma(2)],
+        [(VMEM, kept), (VMEM, received[0]), (VMEM, received[1])],
+        [(HBM, BF16, (2, *FLAT))],
+        [buf(BF16, 2, *FLAT), dma(2)],
         us=1.0,
     )
     parts = lax.all_to_all(

time: 105 us -> 103 us (0.981)
  Pallas kernels: 34 us -> 36.5 us
  waiting for transfers between devices: 30.9 us -> 29 us
  starting transfers between devices: 37.7 us -> 35.9 us
  local copies, waits for them, and re-layouts: 1.16 us -> 0.02 us
    ppermute x9 -> x6, starting transfers between devices: 13.1 us -> 9.47 us  [over(): return lax.ppermute(x, axis, [(i, (i + k) % size) for i in range(size)])]
    pallas_call x11 -> x13, Pallas kernels: 34 us -> 36.5 us  [call(): pl.pallas_call(kernel, out_shape=tuple((space(shape, dtype) for space, dt...]
    ppermute x1 -> x2, waiting for transfers between devices: 2.48 us -> 0.76 us  [shards(): received = [lax.ppermute(send, 'core', swap) for send in (send_0, send_1)]]
    all_to_all x1, starting transfers between devices: 5.54 us -> 6.95 us  [shards(): lax.all_to_all(located_grad, seq, split_axis=0, concat_axis=0, tiled=True)]
    all_to_all x1, waiting for transfers between devices: 13.3 us -> 12.1 us  [shards(): lax.all_to_all(halves.reshape(2 * PARTS, *CHUNK), ('xh', 'xl', 'z'), spli...]
    unnamed x16 -> x8, local copies, waits for them, and re-layouts: 1.16 us -> 0.02 us
    ppermute x9 -> x6, waiting for transfers between devices: 11.3 us -> 12.3 us  [over(): return lax.ppermute(x, axis, [(i, (i + k) % size) for i in range(size)])]
  transfers between devices with their start and end apart: 13 -> 11, of which waited for: 6 -> 6; matrix products, arithmetic and copies ran while one was open for 0% -> 0% of each run, Pallas kernels for 26% -> 29%
where the time goes in v4:
time: 103 us; the launch traced here: 102 us
  Pallas kernels  36.5 us (35%)
  starting transfers between devices  35.9 us (35%)
  waiting for transfers between devices  29 us (28%)
    pallas_call x13, Pallas kernels, call(): pl.pallas_call(kernel, out_shape=tuple((space(shape, dtype) for space, dt...  36.5 us
    all_to_all x1, starting transfers between devices, shards(): located = lax.all_to_all(x1, seq, split_axis=0, concat_axis=0, tiled=True)  12.7 us
    ppermute x6, waiting for transfers between devices, over(): return lax.ppermute(x, axis, [(i, (i + k) % size) for i in range(size)])  12.3 us
    all_to_all x1, waiting for transfers between devices, shards(): lax.all_to_all(halves.reshape(2 * PARTS, *CHUNK), ('xh', 'xl', 'z'), spli...  12.1 us
    ppermute x6, starting transfers between devices, over(): return lax.ppermute(x, axis, [(i, (i + k) % size) for i in range(size)])  9.47 us
    all_to_all x1, starting transfers between devices, shards(): lax.all_to_all(located_grad, seq, split_axis=0, concat_axis=0, tiled=True)  6.95 us
    all_to_all x1, starting transfers between devices, shards(): lax.all_to_all(halves.reshape(2 * PARTS, *CHUNK), ('xh', 'xl', 'z'), spli...  6.24 us
    all_to_all x1, waiting for transfers between devices, shards(): located = lax.all_to_all(x1, seq, split_axis=0, concat_axis=0, tiled=True)  3.81 us
  transfers between devices with their start and end apart: 11, of which 6 were waited for; matrix products, arithmetic and copies ran while one was open for 0% of the time, Pallas kernels for 29%

profile of v4, /device:TPU:32, one launch (start us, length us, event | category | flops | bytes accessed | tf_op | source)
XLA Modules:
  0.0 102.4 jit_solution(12709882624559044603)
XLA Ops:
  0.6 0.0 copy-start.2
  0.6 5.5 %spatial_forward.1 = (bf16[64,2,1152]{2,1,0:T(2,128)(2,1)}, bf16[128,576]{1,0:T(8,128)(2,1)}, bf16[128,576]{1,0:T(8,128)(2,1)}, bf16[128,576]{1,0:T(8,128)(2,1)}, bf16[8,128,128]{2,1,0:T(8,128)(2,1)}) custom-call(s32[1]{0:T(128)} %bitcast.place, bf16[128,1152]{1,0:T(8,128)(2,1)} %bitcast.25, f32[1,3,2,1152]{3,2,1,0:T(2,128)} %bitcast.13, ...), custom_call_target="tpu_custom_call" | custom-call | flops 5000000000 | bytes 15000000 | tf_op jit(solution)/shard_map/spatial_forward/pallas_call | solution.py:370
  6.1 0.0 copy-start.3
  6.1 12.7 %all-to-all-start = ((bf16[64,2,1152]{2,1,0:T(2,128)(2,1)}), bf16[64,2,1152]{2,1,0:T(2,128)(2,1)S(1)}, u32[]{:S(2)}, u32[]{:S(2)}) async-start(bf16[64,2,1152]{2,1,0:T(2,128)(2,1)} %get-tuple-element.47), calls=%async_computation | async-start | bytes 589824 | tf_op jit(solution)/shard_map/all_to_all | solution.py:446
  18.8 0.0 copy-done.2
  18.9 2.0 %branch_grad.1 = (bf16[128,1152]{1,0:T(8,128)(2,1)}, bf16[128,1152]{1,0:T(8,128)(2,1)}) custom-call(bf16[64,2,1152]{2,1,0:T(2,128)(2,1)} %bitcast.11, f32[1,3,2,1152]{3,2,1,0:T(2,128)S(1)} %bitcast.14), custom_call_target="tpu_custom_call" | custom-call | flops 2000000000 | bytes 6000000 | tf_op jit(solution)/shard_map/branch_grad/pallas_call | solution.py:370
  20.9 1.5 %collective-permute-start = (bf16[128,1152]{1,0:T(8,128)(2,1)}, bf16[128,1152]{1,0:T(8,128)(2,1)S(1)}, u32[]{:S(2)}, u32[]{:S(2)}) collective-permute-start(bf16[128,1152]{1,0:T(8,128)(2,1)} %get-tuple-element.65.refs_1_), channel_id=1, source_target_pairs={{0,16},{16,32},{32,48},{48,0},{1,17},{17,33},{33,49},{49,1},{2,18}... | collective-permute-start | bytes 884744 | tf_op jit(solution)/shard_map/ppermute | solution.py:383
  22.4 2.9 %collective-permute-start.1 = (bf16[128,1152]{1,0:T(8,128)(2,1)}, bf16[128,1152]{1,0:T(8,128)(2,1)S(1)}, u32[]{:S(2)}, u32[]{:S(2)}) collective-permute-start(bf16[128,1152]{1,0:T(8,128)(2,1)} %get-tuple-element.65.refs_1_), channel_id=1, source_target_pairs={{0,32},{16,48},{32,0},{48,16},{1,33},{17,49},{33,1},{49,17},{2,34}... | collective-permute-start | bytes 884744 | tf_op jit(solution)/shard_map/ppermute | solution.py:383
  25.3 1.4 %collective-permute-start.2 = (bf16[128,1152]{1,0:T(8,128)(2,1)}, bf16[128,1152]{1,0:T(8,128)(2,1)S(1)}, u32[]{:S(2)}, u32[]{:S(2)}) collective-permute-start(bf16[128,1152]{1,0:T(8,128)(2,1)} %get-tuple-element.65.refs_1_), channel_id=1, source_target_pairs={{0,48},{16,0},{32,16},{48,32},{1,49},{17,1},{33,17},{49,33},{2,50}... | collective-permute-start | bytes 884744 | tf_op jit(solution)/shard_map/ppermute | solution.py:383
  26.7 0.0 copy-done.3
  26.7 2.0 %tables.1 = (f32[128,576]{1,0:T(8,128)}, f32[128,576]{1,0:T(8,128)}) custom-call(s32[1,64]{1,0:T(1,128)S(1)} %bitcast.20), custom_call_target="tpu_custom_call" | custom-call | flops 1500000000 | bytes 4500000 | tf_op jit(solution)/shard_map/tables/pallas_call | solution.py:370
  28.7 3.8 %all-to-all-done.located = bf16[64,2,1152]{2,1,0:T(2,128)(2,1)S(1)} async-done(((bf16[64,2,1152]{2,1,0:T(2,128)(2,1)}), bf16[64,2,1152]{2,1,0:T(2,128)(2,1)S(1)}, u32[]{:S(2)}, u32[]{:S(2)}) %all-to-all-start) | async-done | bytes 294944 | tf_op jit(solution)/shard_map/all_to_all | solution.py:446
  32.5 0.0 copy-start
  32.5 0.0 copy-start.1
  32.5 8.0 %temporal_attention.1 = (bf16[128,576]{1,0:T(8,128)(2,1)S(1)}, bf16[128,1728]{1,0:T(8,128)(2,1)S(1)}, f32[128,1152]{1,0:T(8,128)S(1)}, f32[128,128]{1,0:T(8,128)...) custom-call(s32[1]{0:T(128)} %bitcast.place, ...), custom_call_target="tpu_custom_call" | custom-call | flops 7000000000 | bytes 21000000 | tf_op jit(solution)/shard_map/temporal_attention/pallas_call | solution.py:370
  40.6 0.0 copy-done
  40.6 0.1 collective-permute-start.3
  40.7 2.2 %collective-permute-start.4 = (bf16[1792,128]{1,0:T(8,128)(2,1)}, bf16[1792,128]{1,0:T(8,128)(2,1)S(1)}, u32[]{:S(2)}, u32[]{:S(2)}) collective-permute-start(bf16[1792,128]{1,0:T(8,128)(2,1)} %get-tuple-element.68), channel_id=1, source_target_pairs={{0,32},{16,48},{32,0},{48,16},{1,33},{17,49},{33,1},{49,17},{2,34}... | collective-permute-start | bytes 1376264 | tf_op jit(solution)/shard_map/ppermute | solution.py:383
  42.9 0.0 collective-permute-done.refs_5_
  42.9 1.4 %collective-permute-start.5 = (bf16[1792,128]{1,0:T(8,128)(2,1)}, bf16[1792,128]{1,0:T(8,128)(2,1)S(1)}, u32[]{:S(2)}, u32[]{:S(2)}) collective-permute-start(bf16[1792,128]{1,0:T(8,128)(2,1)} %get-tuple-element.69), channel_id=1, source_target_pairs={{0,48},{16,0},{32,16},{48,32},{1,49},{17,1},{33,17},{49,33},{2,50}... | collective-permute-start | bytes 1376264 | tf_op jit(solution)/shard_map/ppermute | solution.py:383
  44.3 0.0 collective-permute-done.1.refs_6_
  44.3 0.0 collective-permute-done.2.refs_7_
  44.3 0.0 copy-done.1
  44.3 1.9 %temporal_input_back.1 = bf16[64,2,1152]{2,1,0:T(2,128)(2,1)} custom-call(bf16[128,1728]{1,0:T(8,128)(2,1)S(1)} %get-tuple-element.58.projected_grad, bf16[1728,1152]{1,0:T(8,128)(2,1)S(1)} %get-tuple-element.59.qkv_w, bf16[64,2,1152]{2,1,0:T(2,128)(2,1)S(1)} %bitcast.12, f32[1,3,2,1152]{3,2,1,0:T(2,128)S(1)} %bitcast.16, ...), custom_call_target="tpu_custom_call" | custom-call | flops 3000000000 | bytes 9000000 | tf_op jit(solution)/shard_map/temporal_input_back/pallas_call | solution.py:370
  46.2 6.9 %all-to-all-start.1 = ((bf16[64,2,1152]{2,1,0:T(2,128)(2,1)}), bf16[64,2,1152]{2,1,0:T(2,128)(2,1)S(1)}, u32[]{:S(2)}, u32[]{:S(2)}) async-start(bf16[64,2,1152]{2,1,0:T(2,128)(2,1)} %temporal_input_back.1), calls=%async_computation.1 | async-start | bytes 589824 | tf_op jit(solution)/shard_map/all_to_all | solution.py:496
  53.1 1.1 %load_own.1 = (bf16[1792,128]{1,0:T(8,128)(2,1)S(1)}, bf16[128,1152]{1,0:T(8,128)(2,1)S(1)}) custom-call(bf16[1792,128]{1,0:T(8,128)(2,1)} %get-tuple-element.64.refs_0_, bf16[128,1152]{1,0:T(8,128)(2,1)} %get-tuple-element.65.refs_1_), custom_call_target="tpu_custom_call" | custom-call | flops 1000000000 | bytes 3000000 | tf_op jit(solution)/shard_map/load_own/pallas_call | solution.py:370
  54.3 11.7 %collective-permute-done.3.refs_1_ = bf16[1792,128]{1,0:T(8,128)(2,1)S(1)} collective-permute-done((bf16[1792,128]{1,0:T(8,128)(2,1)}, bf16[1792,128]{1,0:T(8,128)(2,1)S(1)}, u32[]{:S(2)}, u32[]{:S(2)}) %collective-permute-start.3) | collective-permute-done | bytes 458784 | tf_op jit(solution)/shard_map/ppermute | solution.py:383
  66.0 0.0 collective-permute-done.4.refs_2_
  66.0 0.6 collective-permute-done.5.refs_3_
  66.5 3.2 %weight_grad.1 = (bf16[2,1408,128]{2,1,0:T(8,128)(2,1)}, bf16[1408,128]{1,0:T(8,128)(2,1)}, bf16[1408,128]{1,0:T(8,128)(2,1)}) custom-call(s32[1]{0:T(128)} %bitcast.6.core, bf16[1792,128]{1,0:T(8,128)(2,1)S(1)} %get-tuple-element.66.refs_0_, bf16[1792,128]{1,0:T(8,128)(2,1)S(1)} %collective-permute-done.3.refs_1_, ...), custom_call_target="tpu_custom_call" | custom-call | flops 4600000000 | bytes 13799999 | tf_op jit(solution)/shard_map/weight_grad/pallas_call | solution.py:370
  69.8 0.1 collective-permute-start.6
  69.9 0.0 all-to-all-done.1.grad
  69.9 0.5 collective-permute-start.7
  70.4 1.1 %load.1.kept = bf16[2,1408,128]{2,1,0:T(8,128)(2,1)S(1)} custom-call(bf16[2,1408,128]{2,1,0:T(8,128)(2,1)} %get-tuple-element.79.refs_0_), custom_call_target="tpu_custom_call" | custom-call | flops 1000000000 | bytes 3000000 | tf_op jit(solution)/shard_map/load/pallas_call | solution.py:370
  71.5 0.2 collective-permute-done.6.received_0
  71.7 0.5 collective-permute-done.7.received_1
  72.2 1.0 add_cores.1
  73.2 6.2 %all-to-all-start.2 = ((bf16[32,88,128]{2,1,0:T(8,128)(2,1)}), bf16[32,88,128]{2,1,0:T(8,128)(2,1)S(1)}, u32[]{:S(2)}, u32[]{:S(2)}) async-start(bf16[32,88,128]{2,1,0:T(8,128)(2,1)} %bitcast.21), calls=%async_computation.2 | async-start | bytes 1441792 | tf_op jit(solution)/shard_map/all_to_all | solution.py:533
  79.5 2.6 %block_out.1 = bf16[64,2,1152]{2,1,0:T(2,128)(2,1)} custom-call(bf16[128,576]{1,0:T(8,128)(2,1)S(1)} %get-tuple-element.82.attended, bf16[2,576,1152]{2,1,0:T(8,128)(2,1)} %out_w.7, bf16[64,2,1152]{2,1,0:T(2,128)(2,1)} %copy-done, f32[1,3,2,1152]{3,2,1,0:T(2,128)S(1)} %bitcast.17), custom_call_target="tpu_custom_call" | custom-call | flops 2000000000 | bytes 6000000 | tf_op jit(solution)/shard_map/block_out/pallas_call | solution.py:370
  82.1 3.2 %spatial_attention_back.1.projected_grad = bf16[128,1728]{1,0:T(8,128)(2,1)S(1)} custom-call(bf16[64,2,1152]{2,1,0:T(2,128)(2,1)S(1)} %all-to-all-done.1.grad, f32[1,3,2,1152]{3,2,1,0:T(2,128)S(1)} %bitcast.18, bf16[2,576,1152]{2,1,0:T(8,128)(2,1)} %out_w.7, bf16[128,576]{1,0:T(8,128)(2,1)} %get-tuple-element.84.q_in, ...), custom_call_target="tpu_custom_call" | custom-call | flops 3500000000 | bytes 10500000 | tf_op jit(solution)/shard_map/spatial_attention_back/pallas_call | solution.py:370
  85.3 4.1 %spatial_input_back.1 = bf16[128,1152]{1,0:T(8,128)(2,1)} custom-call(bf16[64,2,1152]{2,1,0:T(2,128)(2,1)S(1)} %all-to-all-done.1.grad, bf16[128,1152]{1,0:T(8,128)(2,1)} %bitcast.26, f32[1,3,2,1152]{3,2,1,0:T(2,128)S(1)} %bitcast.19, bf16[2,1728,1152]{2,1,0:T(8,128)(2,1)} %bitcast.24, bf16[128,1728]{1,0:T(8,128)(2,1)S(1)} %spatial_attention_back.1.projected_grad), custom_call_target="tpu_custom_call" | custom-call | flops 3000000000 | bytes 9000000 | tf_op jit(solution)/shard_map/spatial_input_back/pallas_call | solution.py:370
  89.4 12.1 %all-to-all-done.2.parts = bf16[32,88,128]{2,1,0:T(8,128)(2,1)S(1)} async-done(((bf16[32,88,128]{2,1,0:T(8,128)(2,1)}), bf16[32,88,128]{2,1,0:T(8,128)(2,1)S(1)}, u32[]{:S(2)}, u32[]{:S(2)}) %all-to-all-start.2) | async-done | bytes 720928 | tf_op jit(solution)/shard_map/all_to_all | solution.py:533
  101.5 0.7 sum_parts.1
Async XLA Ops:
  0.6 18.2 %copy-start.2 = (f32[1,2,3,1152]{3,1,2,0:T(2,128)S(1)}, f32[1,2,3,1152]{3,1,2,0:T(2,128)}, u32[]{:S(2)}) copy-start(f32[1,2,3,1152]{3,1,2,0:T(2,128)} %param.7) | copy-start | bytes 82948
  6.1 20.5 %copy-start.3 = (s32[64]{0:T(128)S(1)}, s32[64]{0:T(128)}, u32[]{:S(2)}) copy-start(s32[64]{0:T(128)} %param.8) | copy-start | bytes 772
  6.1 26.4 %all-to-all-start = ((bf16[64,2,1152]{2,1,0:T(2,128)(2,1)}), bf16[64,2,1152]{2,1,0:T(2,128)(2,1)S(1)}, u32[]{:S(2)}, u32[]{:S(2)}) async-start(bf16[64,2,1152]{2,1,0:T(2,128)(2,1)} %get-tuple-element.47), calls=%async_computation | async-start | bytes 589824 | tf_op jit(solution)/shard_map/all_to_all | solution.py:446
  20.9 22.0 %collective-permute-start = (bf16[128,1152]{1,0:T(8,128)(2,1)}, bf16[128,1152]{1,0:T(8,128)(2,1)S(1)}, u32[]{:S(2)}, u32[]{:S(2)}) collective-permute-start(bf16[128,1152]{1,0:T(8,128)(2,1)} %get-tuple-element.65.refs_1_), channel_id=1, source_target_pairs={{0,16},{16,32},{32,48},{48,0},{1,17},{17,33},{33,49},{49,1},{2,18}... | collective-permute-start | bytes 884744 | tf_op jit(solution)/shard_map/ppermute | solution.py:383
  22.4 21.9 %collective-permute-start.1 = (bf16[128,1152]{1,0:T(8,128)(2,1)}, bf16[128,1152]{1,0:T(8,128)(2,1)S(1)}, u32[]{:S(2)}, u32[]{:S(2)}) collective-permute-start(bf16[128,1152]{1,0:T(8,128)(2,1)} %get-tuple-element.65.refs_1_), channel_id=1, source_target_pairs={{0,32},{16,48},{32,0},{48,16},{1,33},{17,49},{33,1},{49,17},{2,34}... | collective-permute-start | bytes 884744 | tf_op jit(solution)/shard_map/ppermute | solution.py:383
  25.3 19.0 %collective-permute-start.2 = (bf16[128,1152]{1,0:T(8,128)(2,1)}, bf16[128,1152]{1,0:T(8,128)(2,1)S(1)}, u32[]{:S(2)}, u32[]{:S(2)}) collective-permute-start(bf16[128,1152]{1,0:T(8,128)(2,1)} %get-tuple-element.65.refs_1_), channel_id=1, source_target_pairs={{0,48},{16,0},{32,16},{48,32},{1,49},{17,1},{33,17},{49,33},{2,50}... | collective-permute-start | bytes 884744 | tf_op jit(solution)/shard_map/ppermute | solution.py:383
  32.5 8.1 %copy-start = (bf16[64,2,1152]{2,1,0:T(2,128)(2,1)}, bf16[64,2,1152]{2,1,0:T(2,128)(2,1)S(1)}, u32[]{:S(2)}) copy-start(bf16[64,2,1152]{2,1,0:T(2,128)(2,1)S(1)} %all-to-all-done.located) | copy-start | bytes 884740
  32.5 11.8 %copy-start.1 = (bf16[1,64,2,1152]{3,2,1,0:T(2,128)(2,1)S(1)}, bf16[1,64,2,1152]{3,2,1,0:T(2,128)(2,1)}, u32[]{:S(2)}) copy-start(bf16[1,64,2,1152]{3,2,1,0:T(2,128)(2,1)} %param.11) | copy-start | bytes 884740
  40.6 25.4 %collective-permute-start.3 = (bf16[1792,128]{1,0:T(8,128)(2,1)}, bf16[1792,128]{1,0:T(8,128)(2,1)S(1)}, u32[]{:S(2)}, u32[]{:S(2)}) collective-permute-start(bf16[1792,128]{1,0:T(8,128)(2,1)} %get-tuple-element.67), channel_id=1, source_target_pairs={{0,16},{16,32},{32,48},{48,0},{1,17},{17,33},{33,49},{49,1},{2,18}... | collective-permute-start | bytes 1376264 | tf_op jit(solution)/shard_map/ppermute | solution.py:383
  40.7 25.3 %collective-permute-start.4 = (bf16[1792,128]{1,0:T(8,128)(2,1)}, bf16[1792,128]{1,0:T(8,128)(2,1)S(1)}, u32[]{:S(2)}, u32[]{:S(2)}) collective-permute-start(bf16[1792,128]{1,0:T(8,128)(2,1)} %get-tuple-element.68), channel_id=1, source_target_pairs={{0,32},{16,48},{32,0},{48,16},{1,33},{17,49},{33,1},{49,17},{2,34}... | collective-permute-start | bytes 1376264 | tf_op jit(solution)/shard_map/ppermute | solution.py:383
  42.9 23.7 %collective-permute-start.5 = (bf16[1792,128]{1,0:T(8,128)(2,1)}, bf16[1792,128]{1,0:T(8,128)(2,1)S(1)}, u32[]{:S(2)}, u32[]{:S(2)}) collective-permute-start(bf16[1792,128]{1,0:T(8,128)(2,1)} %get-tuple-element.69), channel_id=1, source_target_pairs={{0,48},{16,0},{32,16},{48,32},{1,49},{17,1},{33,17},{49,33},{2,50}... | collective-permute-start | bytes 1376264 | tf_op jit(solution)/shard_map/ppermute | solution.py:383
  46.2 23.7 %all-to-all-start.1 = ((bf16[64,2,1152]{2,1,0:T(2,128)(2,1)}), bf16[64,2,1152]{2,1,0:T(2,128)(2,1)S(1)}, u32[]{:S(2)}, u32[]{:S(2)}) async-start(bf16[64,2,1152]{2,1,0:T(2,128)(2,1)} %temporal_input_back.1), calls=%async_computation.1 | async-start | bytes 589824 | tf_op jit(solution)/shard_map/all_to_all | solution.py:496
  69.8 2.0 %collective-permute-start.6 = (bf16[1408,128]{1,0:T(8,128)(2,1)}, bf16[1408,128]{1,0:T(8,128)(2,1)S(1)}, u32[]{:S(2)}, u32[]{:S(2)}) collective-permute-start(bf16[1408,128]{1,0:T(8,128)(2,1)} %get-tuple-element.80), channel_id=1, source_target_pairs={{0,64},{64,0},{1,65},{65,1},{2,66},{66,2},{3,67},{67,3},{4,68},{68... | collective-permute-start | bytes 1081352 | tf_op jit(solution)/shard_map/ppermute | solution.py:519
  69.9 2.4 %collective-permute-start.7 = (bf16[1408,128]{1,0:T(8,128)(2,1)}, bf16[1408,128]{1,0:T(8,128)(2,1)S(1)}, u32[]{:S(2)}, u32[]{:S(2)}) collective-permute-start(bf16[1408,128]{1,0:T(8,128)(2,1)} %get-tuple-element.81), channel_id=1, source_target_pairs={{0,64},{64,0},{1,65},{65,1},{2,66},{66,2},{3,67},{67,3},{4,68},{68... | collective-permute-start | bytes 1081352 | tf_op jit(solution)/shard_map/ppermute | solution.py:519
  73.2 28.3 %all-to-all-start.2 = ((bf16[32,88,128]{2,1,0:T(8,128)(2,1)}), bf16[32,88,128]{2,1,0:T(8,128)(2,1)S(1)}, u32[]{:S(2)}, u32[]{:S(2)}) async-start(bf16[32,88,128]{2,1,0:T(8,128)(2,1)} %bitcast.21), calls=%async_computation.2 | async-start | bytes 1441792 | tf_op jit(solution)/shard_map/all_to_all | solution.py:533

commit v5 on v4

--- a/solution.py
+++ b/solution.py
@@ -132,16 +132,6 @@
     return jnp.concatenate(main + tail, axis=1)
 
 
-def branch_grad_kernel(seed, mod, sent, kept, seed_v, sent_v, kept_v, sems):
-    (load,) = fetch([(seed, seed_v)], sems.at[pl.ds(0, 1)])
-    load.wait()
-    g = seed_v[...].reshape(TOK, D).astype(F32)
-    branch_grad = (mod[0, 2, 1:2, :] * g).astype(BF16)
-    sent_v[...] = regroup(branch_grad)
-    kept_v[...] = branch_grad
-    wait_all(fetch([(sent_v, sent), (kept_v, kept)], sems.at[pl.ds(1, 2)]))
-
-
 def rope_tables(pos):
     row = lax.broadcasted_iota(jnp.int32, (TOK, FRAMES), 0)
     frame = lax.broadcasted_iota(jnp.int32, (TOK, FRAMES), 1)
@@ -154,9 +144,18 @@
     return jnp.cos(angles), jnp.sin(angles) * sign
 
 
-def tables_kernel(pos, cos_out, sin_out, cos_v, sin_v, sems):
+def branch_grad_kernel(
+    seed, pos, mod, sent, kept, cos_out, sin_out, seed_v, sent_v, kept_v, cos_v, sin_v, sems
+):
+    (load,) = fetch([(seed, seed_v)], sems.at[pl.ds(0, 1)])
     cos_v[...], sin_v[...] = rope_tables(pos[...])
-    wait_all(fetch([(cos_v, cos_out), (sin_v, sin_out)], sems))
+    saves = fetch([(cos_v, cos_out), (sin_v, sin_out)], sems.at[pl.ds(1, 2)])
+    load.wait()
+    g = seed_v[...].reshape(TOK, D).astype(F32)
+    branch_grad = (mod[0, 2, 1:2, :] * g).astype(BF16)
+    sent_v[...] = regroup(branch_grad)
+    kept_v[...] = branch_grad
+    wait_all(saves + fetch([(sent_v, sent), (kept_v, kept)], sems.at[pl.ds(3, 2)]))
 
 
 def spatial_forward_kernel(
@@ -217,33 +216,35 @@
     wait_all(fetch([(result_v, result)], sems.at[pl.ds(2, 1)]))
 
 
+def temporal_normed_kernel(located, mod, sent, grouped_out, kept, unit_out, inverse_out, sem):
+    unit, inverse = layer_norm(located[...].reshape(TOK, D).astype(F32))
+    normed = (unit * (1.0 + mod[0, 1, 1:2, :]) + mod[0, 0, 1:2, :]).astype(BF16)
+    grouped = regroup(normed)
+    grouped_out[...] = rows_of([grouped[:, t * TOK : (t + 1) * TOK] for t in range(D // TOK)])
+    save = pltpu.make_async_copy(grouped_out, sent, sem)
+    save.start()
+    kept[...] = normed
+    unit_out[...] = unit
+    inverse_out[...] = jnp.broadcast_to(inverse, (TOK, TOK))
+    save.wait()
+
+
 def temporal_attention_kernel(
-    place, located, mod, cosines, sines, qkv_w, out_w, branch_grad,
-    attended_out, projected_grad, unit_out, inverse_out, w_out, own, to_1, to_2, to_3,
-    branch_v, o_v, cos_v, sin_v, sent_v, normed_v, qkv_v, factors_v, wide, in_sems, sems, factor_sems,
+    place, normed, grouped, cosines, sines, qkv_w, out_w, branch_grad,
+    attended_out, normed_grad, own, to_1, to_2, to_3,
+    w_out, branch_v, o_v, cos_v, sin_v, qkv_v, factors_v, wide, in_sems, sems, factor_sems,
 ):
     pairs = [(qkv_w.at[1, pl.ds(i * HW, HW)], w_out.at[pl.ds(i * HW, HW)]) for i in range(3)]
     pairs += [(cosines, cos_v), (sines, sin_v), (out_w.at[1], o_v), (branch_grad, branch_v)]
-    copies = [pltpu.make_async_copy(src, dst, in_sems.at[i]) for i, (src, dst) in enumerate(pairs)]
-    start_all(copies)
-    @pl.when(place[0] >= 0)
-    def _():
-        unit, inverse = layer_norm(located[...].reshape(TOK, D).astype(F32))
-        unit_out[...] = unit
-        inverse_out[...] = jnp.broadcast_to(inverse, (TOK, TOK))
-        normed = (unit * (1.0 + mod[0, 1, 1:2, :]) + mod[0, 0, 1:2, :]).astype(BF16)
-        normed_v[...] = normed
-        grouped = regroup(normed)
-        sent_v[...] = rows_of([grouped[:, t * TOK : (t + 1) * TOK] for t in range(D // TOK)])
-
+    copies = fetch(pairs, in_sems)
     messages = (own, to_1, to_2, to_3)
-    saves = fetch([(sent_v, ref.at[pl.ds(FACTOR[0], D)]) for ref in messages], sems)
+    saves = fetch([(grouped, ref.at[pl.ds(FACTOR[0], D)]) for ref in (own, to_1, to_3)], sems)
     for i in range(3):
         copies[i].wait()
 
         @pl.when(place[0] >= 0)
         def _(i=i):
-            qkv_v[i] = dot(normed_v[...], w_out[i * HW : (i + 1) * HW, :], NT).astype(BF16)
+            qkv_v[i] = dot(normed[...], w_out[i * HW : (i + 1) * HW, :], NT).astype(BF16)
 
     parts = [qkv_v[i] for i in range(3)]
     wait_all(copies[3:5])
@@ -268,7 +269,6 @@
     attended_grad = dot(branch_v[...], o_v[...], NT).astype(BF16)
     q_grad, k_grad, v_grad = attend_back(probs, attended_grad, q, keys_by_head, values_by_head)
     grads = lanes_of([rotate_back(q_grad), rotate_back(k_grad), v_grad])
-    projected_grad[...] = grads.astype(BF16)
 
     wide[: 3 * HW, :] = grads.T
     wide[3 * HW :, :] = attended.astype(F32).T
@@ -287,13 +287,13 @@
         [(factors_v.at[lax.rem(place[0] + k, Y)], ref.at[pl.ds(0, FACTOR[0])]) for k, ref in enumerate(messages)],
         factor_sems,
     )
+    normed_grad[...] = dot(grads.astype(BF16), w_out[...]).astype(BF16)
     wait_all(saves)
 
 
-def temporal_input_back_kernel(projected_grad, qkv_w, seed, mod, unit, inverse, result, result_v, sem):
+def temporal_input_back_kernel(normed_grad, seed, mod, unit, inverse, result, result_v, sem):
     g = seed[...].reshape(TOK, D).astype(F32)
-    normed_grad = dot(projected_grad[...], qkv_w[...]).astype(BF16).astype(F32)
-    x_grad = layer_norm_back(normed_grad * (1.0 + mod[0, 1, 1:2, :]), unit[...], inverse[:, 0:1])
+    x_grad = layer_norm_back(normed_grad[...].astype(F32) * (1.0 + mod[0, 1, 1:2, :]), unit[...], inverse[:, 0:1])
     result_v[...] = (g + x_grad).astype(BF16).reshape(FRAMES, 2, D)
     save = pltpu.make_async_copy(result_v, result, sem)
     save.start()
@@ -310,10 +310,14 @@
 
 
 def weight_grad_kernel(core, *refs):
-    messages, branch_grad = refs[0:Y], refs[Y : 2 * Y]
-    keep, send_0, send_1, keep_v, send_v, sems = refs[2 * Y :]
+    messages, branch_grad, normed_far = refs[0:Y], refs[Y : 2 * Y], refs[2 * Y]
+    keep, *sends = refs[2 * Y + 1 : 2 * Y + 2 + PIECES]
+    keep_v, send_v, sems = refs[2 * Y + 2 + PIECES :]
     left = lanes_of([m[: FACTOR[0]] for m in messages])
-    normed = [lanes_of([m[FACTOR[0] + t * TOK : FACTOR[0] + (t + 1) * TOK] for t in range(D // TOK)]) for m in messages]
+    normed = []
+    for k, m in enumerate(messages):
+        ref, at = (normed_far, 0) if k == 2 else (m, FACTOR[0])
+        normed.append(lanes_of([ref[at + t * TOK : at + (t + 1) * TOK] for t in range(D // TOK)]))
     is_qkv = lax.rem(lax.broadcasted_iota(jnp.int32, (PARTS * BLOCK, 1), 0), BLOCK) < QKV_COLS
     from_normed = dot(left, rows_of(normed))
     from_branch = dot(left, rows_of([n[...] for n in branch_grad]))
@@ -336,7 +340,9 @@
         a, b = chunk(2 * x), chunk(2 * x + 1)
         send_v[x] = jnp.where(first, b, a).astype(BF16)
         keep_v[x] = jnp.where(first, a, b).astype(BF16)
-        copies += fetch([(send_v.at[x], (send_0, send_1)[x]), (keep_v.at[x], keep.at[x])], sems.at[x])
+        each = PIECES // 2
+        pairs = [(send_v.at[x, pl.ds(i * PIECE[0], PIECE[0])], sends[x * each + i]) for i in range(each)]
+        copies += fetch(pairs + [(keep_v.at[x], keep.at[x])], sems.at[x])
     wait_all(copies)
 
 
@@ -345,11 +351,14 @@
     wait_all(fetch(list(zip(refs[:half], refs[half : 2 * half], strict=True)), refs[-1]))
 
 
-def add_kernel(kept, received_0, received_1, result, result_v, sems):
+def add_kernel(kept, *refs):
+    received, (result, result_v, sems) = refs[:PIECES], refs[PIECES:]
     copies = []
-    for i, received in enumerate((received_0, received_1)):
-        result_v[i] = (kept[i].astype(F32) + received[...].astype(F32)).astype(BF16)
-        copies += fetch([(result_v.at[i], result.at[i])], sems.at[pl.ds(i, 1)])
+    for i, piece in enumerate(received):
+        half, rows = i // (PIECES // 2), pl.ds(i % (PIECES // 2) * PIECE[0], PIECE[0])
+        result_v[half, rows] = (kept[half, rows].astype(F32) + piece[...].astype(F32)).astype(BF16)
+        if i % (PIECES // 2) == PIECES // 2 - 1:
+            copies += fetch([(result_v.at[half], result.at[half])], sems.at[pl.ds(half, 1)])
     wait_all(copies)
 
 
@@ -420,6 +429,8 @@
 PROB = (HEADS, TOK, TOK)
 CHUNK = (88, TOK)
 FLAT = (PARTS * 88, TOK)
+PIECES = 2
+PIECE = (2 * FLAT[0] // PIECES, TOK)
 FACTOR = (PARTS * BLOCK, TOK)
 MESSAGE = (FACTOR[0] + D, TOK)
 
@@ -446,49 +457,51 @@
     located = lax.all_to_all(x1, seq, split_axis=0, concat_axis=0, tiled=True)
 
     later_seed, later_pos, _ = lax.optimization_barrier((seed, frame_pos, x1))
-    sent, branch_grad = call(
+    sent, branch_grad, cosines, sines = call(
         branch_grad_kernel,
         "branch_grad",
-        [(HBM, later_seed), (VMEM, mod)],
-        [(HBM, BF16, (TOK, D)), (HBM, BF16, (TOK, D))],
-        [buf(BF16, *PAIRS), buf(BF16, TOK, D), buf(BF16, TOK, D), dma(3)],
-        us=2.0,
+        [(HBM, later_seed), (VMEM, later_pos.reshape(1, FRAMES)), (VMEM, mod)],
+        [(HBM, BF16, (TOK, D)), (HBM, BF16, (TOK, D)), (HBM, F32, ATT), (HBM, F32, ATT)],
+        [buf(BF16, *PAIRS), buf(BF16, TOK, D), buf(BF16, TOK, D), buf(F32, *ATT), buf(F32, *ATT), dma(5)],
+        us=3.0,
     )
     branch_all = [sent] + [over("y", Y, i, sent) for i in range(1, Y)]
 
-    cosines, sines = call(
-        tables_kernel,
-        "tables",
-        [(VMEM, later_pos.reshape(1, FRAMES))],
-        [(HBM, F32, ATT), (HBM, F32, ATT)],
-        [buf(F32, *ATT), buf(F32, *ATT), dma(2)],
+    located, branch_grad, cosines = lax.optimization_barrier((located, branch_grad, cosines))
+    normed, grouped, normed_here, unit, inverse = call(
+        temporal_normed_kernel,
+        "temporal_normed",
+        [(VMEM, located), (VMEM, mod)],
+        [
+            (HBM, BF16, (D, TOK)), (VMEM, BF16, (D, TOK)), (VMEM, BF16, (TOK, D)), (VMEM, F32, (TOK, D)),
+            (VMEM, F32, (TOK, TOK)),
+        ],
+        [dma()],
         us=1.5,
     )
-    located, branch_grad, cosines = lax.optimization_barrier((located, branch_grad, cosines))
-    attended, projected_grad, unit, inverse, w1, *messages = call(
+    normed_far = over("y", Y, 2, normed)
+
+    attended, normed_grad, *messages = call(
         temporal_attention_kernel,
         "temporal_attention",
         [
-            (SMEM, place), (VMEM, located), (VMEM, mod), (HBM, cosines), (HBM, sines), (HBM, qkv_w), (HBM, out_weight),
-            (HBM, branch_grad),
+            (SMEM, place), (VMEM, normed_here), (VMEM, grouped), (HBM, cosines), (HBM, sines), (HBM, qkv_w),
+            (HBM, out_weight), (HBM, branch_grad),
         ],
+        [(VMEM, BF16, ATT), (VMEM, BF16, (TOK, D))]
+        + [(HBM, BF16, shape) for shape in (MESSAGE, MESSAGE, FACTOR, MESSAGE)],
         [
-            (VMEM, BF16, ATT), (VMEM, BF16, (TOK, 3 * HW)), (VMEM, F32, (TOK, D)), (VMEM, F32, (TOK, TOK)),
-            (VMEM, BF16, QKV_W),
-        ]
-        + [(HBM, BF16, MESSAGE)] * Y,
-        [
-            buf(BF16, TOK, D), buf(BF16, *OUT_W), buf(F32, *ATT), buf(F32, *ATT), buf(BF16, D, TOK),
-            buf(BF16, TOK, D), buf(BF16, 3, *ATT), buf(BF16, Y, *FACTOR), buf(F32, 4 * HW, TOK), dma(7), dma(Y), dma(Y),
+            buf(BF16, *QKV_W), buf(BF16, TOK, D), buf(BF16, *OUT_W), buf(F32, *ATT), buf(F32, *ATT), buf(BF16, 3, *ATT),
+            buf(BF16, Y, *FACTOR), buf(F32, 4 * HW, TOK), dma(7), dma(3), dma(Y),
         ],
         us=7.0,
     )
     messages = [messages[0]] + [over("y", Y, i, messages[i]) for i in range(1, Y)]
-    projected_grad, branch_all = lax.optimization_barrier((projected_grad, branch_all))
+    normed_grad, branch_all, normed_far = lax.optimization_barrier((normed_grad, branch_all, normed_far))
     (located_grad,) = call(
         temporal_input_back_kernel,
         "temporal_input_back",
-        [(VMEM, projected_grad), (VMEM, w1), (VMEM, seed), (VMEM, mod), (VMEM, unit), (VMEM, inverse)],
+        [(VMEM, normed_grad), (VMEM, seed), (VMEM, mod), (VMEM, unit), (VMEM, inverse)],
         [(HBM, BF16, PAIRS)],
         [buf(BF16, *PAIRS), dma()],
         us=3.0,
@@ -506,30 +519,29 @@
     )
     messages, branch_all = [own_message] + messages[1:], [own_branch] + branch_all[1:]
     core = lax.axis_index("core").reshape(1).astype(jnp.int32)
-    keep, send_0, send_1 = call(
+    keep, *sends = call(
         weight_grad_kernel,
         "weight_grad",
-        [(SMEM, core)] + [(VMEM, x) for x in (*messages, *branch_all)],
-        [(HBM, BF16, (2, *FLAT)), (HBM, BF16, FLAT), (HBM, BF16, FLAT)],
-        [buf(BF16, 2, *FLAT), buf(BF16, 2, *FLAT), dma(2, 2)],
+        [(SMEM, core)] + [(VMEM, x) for x in (*messages, *branch_all, normed_far)],
+        [(HBM, BF16, (2, *FLAT))] + [(HBM, BF16, PIECE)] * PIECES,
+        [buf(BF16, 2, *FLAT), buf(BF16, 2, *FLAT), dma(2, 1 + PIECES // 2)],
         us=4.6,
     )
-    framed_grad, send_1 = lax.optimization_barrier((framed_grad, send_1))
     swap = [(0, 1), (1, 0)]
-    received = [lax.ppermute(send, "core", swap) for send in (send_0, send_1)]
-
-    framed_grad, keep_later = lax.optimization_barrier((framed_grad, keep))
+    received = [lax.ppermute(send, "core", swap) for send in sends]
+
     (kept,) = call(
-        load_kernel, "load", [(HBM, keep_later)], [(VMEM, BF16, (2, *FLAT))], [dma(1)], us=1.0
+        load_kernel, "load", [(HBM, keep)], [(VMEM, BF16, (2, *FLAT))], [dma(1)], us=1.0
     )
     (halves,) = call(
         add_kernel,
         "add_cores",
-        [(VMEM, kept), (VMEM, received[0]), (VMEM, received[1])],
+        [(VMEM, kept)] + [(VMEM, x) for x in received],
         [(HBM, BF16, (2, *FLAT))],
         [buf(BF16, 2, *FLAT), dma(2)],
         us=1.0,
     )
+    framed_grad, halves = lax.optimization_barrier((framed_grad, halves))
     parts = lax.all_to_all(
         halves.reshape(2 * PARTS, *CHUNK), ("xh", "xl", "z"), split_axis=0, concat_axis=0, tiled=True
     )

time: 103 us -> 100 us (0.971)
  waiting for transfers between devices: 29 us -> 22.2 us
  starting transfers between devices: 35.9 us -> 38.7 us
  local copies, waits for them, and re-layouts: 0.02 us -> 1.91 us
    ppermute x6 -> x7, waiting for transfers between devices: 12.3 us -> 0.02 us  [over(): return lax.ppermute(x, axis, [(i, (i + k) % size) for i in range(size)])]
    all_to_all x1, waiting for transfers between devices: 0.01 us -> 4.21 us  [shards(): lax.all_to_all(located_grad, seq, split_axis=0, concat_axis=0, tiled=True)]
    ppermute x6 -> x7, starting transfers between devices: 9.47 us -> 11.4 us  [over(): return lax.ppermute(x, axis, [(i, (i + k) % size) for i in range(size)])]
    unnamed x8 -> x12, local copies, waits for them, and re-layouts: 0.02 us -> 1.91 us
    all_to_all x1, waiting for transfers between devices: 3.81 us -> 5.51 us  [shards(): located = lax.all_to_all(x1, seq, split_axis=0, concat_axis=0, tiled=True)]
    all_to_all x1, starting transfers between devices: 6.95 us -> 8.21 us  [shards(): lax.all_to_all(located_grad, seq, split_axis=0, concat_axis=0, tiled=True)]
  transfers between devices with their start and end apart: 11 -> 12, of which waited for: 6 -> 5; matrix products, arithmetic and copies ran while one was open for 0% -> 0% of each run, Pallas kernels for 29% -> 30%
where the time goes in v5:
time: 100 us; the launch traced here: 99.8 us
  starting transfers between devices  38.7 us (39%)
  Pallas kernels  35.9 us (36%)
  waiting for transfers between devices  22.2 us (22%)
  local copies, waits for them, and re-layouts  1.91 us (2%)
  between operations  1.04 us (1%)
    pallas_call x13, Pallas kernels, call(): pl.pallas_call(kernel, out_shape=tuple((space(shape, dtype) for space, dt...  35.9 us
    all_to_all x1, starting transfers between devices, shards(): located = lax.all_to_all(x1, seq, split_axis=0, concat_axis=0, tiled=True)  12.7 us
    all_to_all x1, waiting for transfers between devices, shards(): lax.all_to_all(halves.reshape(2 * PARTS, *CHUNK), ('xh', 'xl', 'z'), spli...  11.7 us
    ppermute x7, starting transfers between devices, over(): return lax.ppermute(x, axis, [(i, (i + k) % size) for i in range(size)])  11.4 us
    all_to_all x1, starting transfers between devices, shards(): lax.all_to_all(located_grad, seq, split_axis=0, concat_axis=0, tiled=True)  8.21 us
    all_to_all x1, starting transfers between devices, shards(): lax.all_to_all(halves.reshape(2 * PARTS, *CHUNK), ('xh', 'xl', 'z'), spli...  5.77 us
    all_to_all x1, waiting for transfers between devices, shards(): located = lax.all_to_all(x1, seq, split_axis=0, concat_axis=0, tiled=True)  5.51 us
    all_to_all x1, waiting for transfers between devices, shards(): lax.all_to_all(located_grad, seq, split_axis=0, concat_axis=0, tiled=True)  4.21 us
  transfers between devices with their start and end apart: 12, of which 5 were waited for; matrix products, arithmetic and copies ran while one was open for 0% of the time, Pallas kernels for 30%

profile of v5, /device:TPU:32, one launch (start us, length us, event | category | flops | bytes accessed | tf_op | source)
XLA Modules:
  0.0 99.8 jit_solution(13620285599892173578)
XLA Ops:
  0.6 0.0 copy-start.2
  0.6 0.0 copy-start.3
  0.7 5.5 %spatial_forward.1 = (bf16[64,2,1152]{2,1,0:T(2,128)(2,1)}, bf16[128,576]{1,0:T(8,128)(2,1)}, bf16[128,576]{1,0:T(8,128)(2,1)}, bf16[128,576]{1,0:T(8,128)(2,1)}, bf16[8,128,128]{2,1,0:T(8,128)(2,1)}) custom-call(s32[1]{0:T(128)} %bitcast.place, bf16[128,1152]{1,0:T(8,128)(2,1)} %bitcast.25, f32[1,3,2,1152]{3,2,1,0:T(2,128)} %bitcast.13, ...), custom_call_target="tpu_custom_call" | custom-call | flops 5000000000 | bytes 15000000 | tf_op jit(solution)/shard_map/spatial_forward/pallas_call | solution.py:379
  6.1 12.7 %all-to-all-start = ((bf16[64,2,1152]{2,1,0:T(2,128)(2,1)}), bf16[64,2,1152]{2,1,0:T(2,128)(2,1)S(1)}, u32[]{:S(2)}, u32[]{:S(2)}) async-start(bf16[64,2,1152]{2,1,0:T(2,128)(2,1)} %get-tuple-element.48), calls=%async_computation | async-start | bytes 589824 | tf_op jit(solution)/shard_map/all_to_all | solution.py:457
  18.8 0.0 copy-done.2
  18.9 0.0 copy-done.3
  18.9 2.4 %branch_grad.1 = (bf16[128,1152]{1,0:T(8,128)(2,1)}, bf16[128,1152]{1,0:T(8,128)(2,1)}, f32[128,576]{1,0:T(8,128)}, f32[128,576]{1,0:T(8,128)}) custom-call(bf16[64,2,1152]{2,1,0:T(2,128)(2,1)} %bitcast.11, s32[1,64]{1,0:T(1,128)S(1)} %bitcast.20, f32[1,3,2,1152]{3,2,1,0:T(2,128)S(1)} %bitcast.14), custom_call_target="tpu_custom_call" | custom-call | flops 3000000000 | bytes 9000000 | tf_op jit(solution)/shard_map/branch_grad/pallas_call | solution.py:379
  21.2 1.5 %collective-permute-start = (bf16[128,1152]{1,0:T(8,128)(2,1)}, bf16[128,1152]{1,0:T(8,128)(2,1)S(1)}, u32[]{:S(2)}, u32[]{:S(2)}) collective-permute-start(bf16[128,1152]{1,0:T(8,128)(2,1)} %get-tuple-element.68.refs_1_), channel_id=1, source_target_pairs={{0,16},{16,32},{32,48},{48,0},{1,17},{17,33},{33,49},{49,1},{2,18}... | collective-permute-start | bytes 884744 | tf_op jit(solution)/shard_map/ppermute | solution.py:392
  22.8 2.9 %collective-permute-start.1 = (bf16[128,1152]{1,0:T(8,128)(2,1)}, bf16[128,1152]{1,0:T(8,128)(2,1)S(1)}, u32[]{:S(2)}, u32[]{:S(2)}) collective-permute-start(bf16[128,1152]{1,0:T(8,128)(2,1)} %get-tuple-element.68.refs_1_), channel_id=1, source_target_pairs={{0,32},{16,48},{32,0},{48,16},{1,33},{17,49},{33,1},{49,17},{2,34}... | collective-permute-start | bytes 884744 | tf_op jit(solution)/shard_map/ppermute | solution.py:392
  25.7 1.4 %collective-permute-start.2 = (bf16[128,1152]{1,0:T(8,128)(2,1)}, bf16[128,1152]{1,0:T(8,128)(2,1)S(1)}, u32[]{:S(2)}, u32[]{:S(2)}) collective-permute-start(bf16[128,1152]{1,0:T(8,128)(2,1)} %get-tuple-element.68.refs_1_), channel_id=1, source_target_pairs={{0,48},{16,0},{32,16},{48,32},{1,49},{17,1},{33,17},{49,33},{2,50}... | collective-permute-start | bytes 884744 | tf_op jit(solution)/shard_map/ppermute | solution.py:392
  27.0 5.5 %all-to-all-done.located = bf16[64,2,1152]{2,1,0:T(2,128)(2,1)S(1)} async-done(((bf16[64,2,1152]{2,1,0:T(2,128)(2,1)}), bf16[64,2,1152]{2,1,0:T(2,128)(2,1)S(1)}, u32[]{:S(2)}, u32[]{:S(2)}) %all-to-all-start) | async-done | bytes 294944 | tf_op jit(solution)/shard_map/all_to_all | solution.py:457
  32.5 0.0 copy-start
  32.5 1.3 %temporal_normed.1 = (bf16[1152,128]{1,0:T(8,128)(2,1)}, bf16[1152,128]{1,0:T(8,128)(2,1)S(1)}, bf16[128,1152]{1,0:T(8,128)(2,1)S(1)}, f32[128,1152]{1,0:T(8,128)S(1)}, f32[128,128]{1,0:T(8,128)S(1)}) custom-call(bf16[64,2,1152]{2,1,0:T(2,128)(2,1)S(1)} %all-to-all-done.located, f32[1,3,2,1152]{3,2,1,0:T(2,128)S(1)} %bitcast.15), custom_call_target="tpu_custom_call" | custom-call | flops 1500000000 | bytes 4500000 | tf_op jit(solution)/shard_map/temporal_normed/pallas_call | solution.py:379
  33.9 0.0 copy-start.4
  33.9 0.8 copy-done.4
  34.7 1.0 collective-permute-start.3
  35.7 0.0 copy-start.1
  35.7 8.4 %temporal_attention.1 = (bf16[128,576]{1,0:T(8,128)(2,1)S(1)}, bf16[128,1152]{1,0:T(8,128)(2,1)S(1)}, bf16[1792,128]{1,0:T(8,128)(2,1)}, bf16[1792,128]{1,0:T(8,...) custom-call(s32[1]{0:T(128)} %bitcast.place, bf16[128,1152]{1,0:T(8,128)(2,1)S(1)} %get-tuple-element.54.normed, ...), custom_call_target="tpu_custom_call" | custom-call | flops 7000000000 | bytes 21000000 | tf_op jit(solution)/shard_map/temporal_attention/pallas_call | solution.py:379
  44.1 0.0 copy-done
  44.1 0.7 collective-permute-start.4
  44.8 0.0 collective-permute-done.refs_5_
  44.8 2.6 %collective-permute-start.6 = (bf16[1792,128]{1,0:T(8,128)(2,1)}, bf16[1792,128]{1,0:T(8,128)(2,1)S(1)}, u32[]{:S(2)}, u32[]{:S(2)}) collective-permute-start(bf16[1792,128]{1,0:T(8,128)(2,1)} %get-tuple-element.72), channel_id=1, source_target_pairs={{0,48},{16,0},{32,16},{48,32},{1,49},{17,1},{33,17},{49,33},{2,50}... | collective-permute-start | bytes 1376264 | tf_op jit(solution)/shard_map/ppermute | solution.py:392
  47.4 0.0 collective-permute-done.1.refs_6_
  47.4 1.3 %collective-permute-start.5 = (bf16[640,128]{1,0:T(8,128)(2,1)}, bf16[640,128]{1,0:T(8,128)(2,1)S(1)}, u32[]{:S(2)}, u32[]{:S(2)}) collective-permute-start(bf16[640,128]{1,0:T(8,128)(2,1)} %get-tuple-element.71), channel_id=1, source_target_pairs={{0,32},{16,48},{32,0},{48,16},{1,33},{17,49},{33,1},{49,17},{2,34}... | collective-permute-start | bytes 491528 | tf_op jit(solution)/shard_map/ppermute | solution.py:392
  48.8 0.0 collective-permute-done.2.refs_7_
  48.8 0.0 collective-permute-done.3.refs_8_
  48.8 0.0 copy-done.1
  48.8 0.0 copy-start.5
  48.8 1.1 %copy-done.5 = f32[128,1152]{1,0:T(8,128)S(1)} copy-done((f32[128,1152]{1,0:T(8,128)S(1)}, f32[128,1152]{1,0:T(8,128)}, u32[]{:S(2)}) %copy-start.5) | copy-done | bytes 589848
  49.8 1.3 %temporal_input_back.1 = bf16[64,2,1152]{2,1,0:T(2,128)(2,1)} custom-call(bf16[128,1152]{1,0:T(8,128)(2,1)S(1)} %get-tuple-element.62.normed_grad, bf16[64,2,1152]{2,1,0:T(2,128)(2,1)S(1)} %bitcast.12, f32[1,3,2,1152]{3,2,1,0:T(2,128)S(1)} %bitcast.16, f32[128,1152]{1,0:T(8,128)S(1)} %copy-done.5, f32[128,128]{1,0:T(8,128)S(1)} %get-tuple-element.64.inverse), custom_call_target="tpu_custom_call" | custom-call | flops 3000000000 | bytes 9000000 | tf_op jit(solution)/shard_map/temporal_input_back/pallas_call | solution.py:379
  51.1 8.2 %all-to-all-start.1 = ((bf16[64,2,1152]{2,1,0:T(2,128)(2,1)}), bf16[64,2,1152]{2,1,0:T(2,128)(2,1)S(1)}, u32[]{:S(2)}, u32[]{:S(2)}) async-start(bf16[64,2,1152]{2,1,0:T(2,128)(2,1)} %temporal_input_back.1), calls=%async_computation.1 | async-start | bytes 589824 | tf_op jit(solution)/shard_map/all_to_all | solution.py:509
  59.3 1.1 %load_own.1 = (bf16[1792,128]{1,0:T(8,128)(2,1)S(1)}, bf16[128,1152]{1,0:T(8,128)(2,1)S(1)}) custom-call(bf16[1792,128]{1,0:T(8,128)(2,1)} %get-tuple-element.67.refs_0_, bf16[128,1152]{1,0:T(8,128)(2,1)} %get-tuple-element.68.refs_1_), custom_call_target="tpu_custom_call" | custom-call | flops 1000000000 | bytes 3000000 | tf_op jit(solution)/shard_map/load_own/pallas_call | solution.py:379
  60.5 0.0 collective-permute-done.5.refs_2_
  60.5 0.0 collective-permute-done.4.refs_1_
  60.5 0.0 collective-permute-done.6.refs_3_
  60.5 3.2 %weight_grad.1 = (bf16[2,1408,128]{2,1,0:T(8,128)(2,1)}, bf16[1408,128]{1,0:T(8,128)(2,1)}, bf16[1408,128]{1,0:T(8,128)(2,1)}) custom-call(s32[1]{0:T(128)} %bitcast.6.core, bf16[1792,128]{1,0:T(8,128)(2,1)S(1)} %get-tuple-element.69.refs_0_, bf16[1792,128]{1,0:T(8,128)(2,1)S(1)} %collective-permute-done.4.refs_1_, ...), custom_call_target="tpu_custom_call" | custom-call | flops 4600000000 | bytes 13799999 | tf_op jit(solution)/shard_map/weight_grad/pallas_call | solution.py:379
  63.7 0.1 collective-permute-start.7
  63.8 0.5 collective-permute-start.8
  64.3 1.1 %load.1.kept = bf16[2,1408,128]{2,1,0:T(8,128)(2,1)S(1)} custom-call(bf16[2,1408,128]{2,1,0:T(8,128)(2,1)} %get-tuple-element.78.refs_0_), custom_call_target="tpu_custom_call" | custom-call | flops 1000000000 | bytes 3000000 | tf_op jit(solution)/shard_map/load/pallas_call | solution.py:379
  65.5 0.3 collective-permute-done.7.refs_0_
  65.7 0.5 collective-permute-done.8.refs_1_
  66.2 1.0 add_cores.1
  67.2 4.2 %all-to-all-done.1.grad = bf16[64,2,1152]{2,1,0:T(2,128)(2,1)S(1)} async-done(((bf16[64,2,1152]{2,1,0:T(2,128)(2,1)}), bf16[64,2,1152]{2,1,0:T(2,128)(2,1)S(1)}, u32[]{:S(2)}, u32[]{:S(2)}) %all-to-all-start.1) | async-done | bytes 294944 | tf_op jit(solution)/shard_map/all_to_all | solution.py:509
  71.4 5.8 %all-to-all-start.2 = ((bf16[32,88,128]{2,1,0:T(8,128)(2,1)}), bf16[32,88,128]{2,1,0:T(8,128)(2,1)S(1)}, u32[]{:S(2)}, u32[]{:S(2)}) async-start(bf16[32,88,128]{2,1,0:T(8,128)(2,1)} %bitcast.21), calls=%async_computation.2 | async-start | bytes 1441792 | tf_op jit(solution)/shard_map/all_to_all | solution.py:545
  77.2 2.6 %block_out.1 = bf16[64,2,1152]{2,1,0:T(2,128)(2,1)} custom-call(bf16[128,576]{1,0:T(8,128)(2,1)S(1)} %get-tuple-element.84.attended, bf16[2,576,1152]{2,1,0:T(8,128)(2,1)} %out_w.7, bf16[64,2,1152]{2,1,0:T(2,128)(2,1)} %copy-done, f32[1,3,2,1152]{3,2,1,0:T(2,128)S(1)} %bitcast.17), custom_call_target="tpu_custom_call" | custom-call | flops 2000000000 | bytes 6000000 | tf_op jit(solution)/shard_map/block_out/pallas_call | solution.py:379
  79.8 3.2 %spatial_attention_back.1.projected_grad = bf16[128,1728]{1,0:T(8,128)(2,1)S(1)} custom-call(bf16[64,2,1152]{2,1,0:T(2,128)(2,1)S(1)} %all-to-all-done.1.grad, f32[1,3,2,1152]{3,2,1,0:T(2,128)S(1)} %bitcast.18, bf16[2,576,1152]{2,1,0:T(8,128)(2,1)} %out_w.7, bf16[128,576]{1,0:T(8,128)(2,1)} %get-tuple-element.86.q_in, ...), custom_call_target="tpu_custom_call" | custom-call | flops 3500000000 | bytes 10500000 | tf_op jit(solution)/shard_map/spatial_attention_back/pallas_call | solution.py:379
  83.0 4.1 %spatial_input_back.1 = bf16[128,1152]{1,0:T(8,128)(2,1)} custom-call(bf16[64,2,1152]{2,1,0:T(2,128)(2,1)S(1)} %all-to-all-done.1.grad, bf16[128,1152]{1,0:T(8,128)(2,1)} %bitcast.26, f32[1,3,2,1152]{3,2,1,0:T(2,128)S(1)} %bitcast.19, bf16[2,1728,1152]{2,1,0:T(8,128)(2,1)} %bitcast.24, bf16[128,1728]{1,0:T(8,128)(2,1)S(1)} %spatial_attention_back.1.projected_grad), custom_call_target="tpu_custom_call" | custom-call | flops 3000000000 | bytes 9000000 | tf_op jit(solution)/shard_map/spatial_input_back/pallas_call | solution.py:379
  87.1 11.7 %all-to-all-done.2.parts = bf16[32,88,128]{2,1,0:T(8,128)(2,1)S(1)} async-done(((bf16[32,88,128]{2,1,0:T(8,128)(2,1)}), bf16[32,88,128]{2,1,0:T(8,128)(2,1)S(1)}, u32[]{:S(2)}, u32[]{:S(2)}) %all-to-all-start.2) | async-done | bytes 720928 | tf_op jit(solution)/shard_map/all_to_all | solution.py:545
  98.9 0.7 sum_parts.1
Async XLA Ops:
  0.6 18.2 %copy-start.2 = (f32[1,2,3,1152]{3,1,2,0:T(2,128)S(1)}, f32[1,2,3,1152]{3,1,2,0:T(2,128)}, u32[]{:S(2)}) copy-start(f32[1,2,3,1152]{3,1,2,0:T(2,128)} %param.7) | copy-start | bytes 82948
  0.6 18.2 %copy-start.3 = (s32[64]{0:T(128)S(1)}, s32[64]{0:T(128)}, u32[]{:S(2)}) copy-start(s32[64]{0:T(128)} %param.8) | copy-start | bytes 772
  6.1 26.4 %all-to-all-start = ((bf16[64,2,1152]{2,1,0:T(2,128)(2,1)}), bf16[64,2,1152]{2,1,0:T(2,128)(2,1)S(1)}, u32[]{:S(2)}, u32[]{:S(2)}) async-start(bf16[64,2,1152]{2,1,0:T(2,128)(2,1)} %get-tuple-element.48), calls=%async_computation | async-start | bytes 589824 | tf_op jit(solution)/shard_map/all_to_all | solution.py:457
  21.2 23.6 %collective-permute-start = (bf16[128,1152]{1,0:T(8,128)(2,1)}, bf16[128,1152]{1,0:T(8,128)(2,1)S(1)}, u32[]{:S(2)}, u32[]{:S(2)}) collective-permute-start(bf16[128,1152]{1,0:T(8,128)(2,1)} %get-tuple-element.68.refs_1_), channel_id=1, source_target_pairs={{0,16},{16,32},{32,48},{48,0},{1,17},{17,33},{33,49},{49,1},{2,18}... | collective-permute-start | bytes 884744 | tf_op jit(solution)/shard_map/ppermute | solution.py:392
  22.8 24.6 %collective-permute-start.1 = (bf16[128,1152]{1,0:T(8,128)(2,1)}, bf16[128,1152]{1,0:T(8,128)(2,1)S(1)}, u32[]{:S(2)}, u32[]{:S(2)}) collective-permute-start(bf16[128,1152]{1,0:T(8,128)(2,1)} %get-tuple-element.68.refs_1_), channel_id=1, source_target_pairs={{0,32},{16,48},{32,0},{48,16},{1,33},{17,49},{33,1},{49,17},{2,34}... | collective-permute-start | bytes 884744 | tf_op jit(solution)/shard_map/ppermute | solution.py:392
  25.7 23.1 %collective-permute-start.2 = (bf16[128,1152]{1,0:T(8,128)(2,1)}, bf16[128,1152]{1,0:T(8,128)(2,1)S(1)}, u32[]{:S(2)}, u32[]{:S(2)}) collective-permute-start(bf16[128,1152]{1,0:T(8,128)(2,1)} %get-tuple-element.68.refs_1_), channel_id=1, source_target_pairs={{0,48},{16,0},{32,16},{48,32},{1,49},{17,1},{33,17},{49,33},{2,50}... | collective-permute-start | bytes 884744 | tf_op jit(solution)/shard_map/ppermute | solution.py:392
  32.5 11.6 %copy-start = (bf16[64,2,1152]{2,1,0:T(2,128)(2,1)}, bf16[64,2,1152]{2,1,0:T(2,128)(2,1)S(1)}, u32[]{:S(2)}) copy-start(bf16[64,2,1152]{2,1,0:T(2,128)(2,1)S(1)} %all-to-all-done.located) | copy-start | bytes 884740
  33.9 0.8 copy-start.4
  34.7 14.0 %collective-permute-start.3 = (bf16[1152,128]{1,0:T(8,128)(2,1)}, bf16[1152,128]{1,0:T(8,128)(2,1)S(1)}, u32[]{:S(2)}, u32[]{:S(2)}) collective-permute-start(bf16[1152,128]{1,0:T(8,128)(2,1)} %get-tuple-element.61), channel_id=1, source_target_pairs={{0,32},{16,48},{32,0},{48,16},{1,33},{17,49},{33,1},{49,17},{2,34}... | collective-permute-start | bytes 884744 | tf_op jit(solution)/shard_map/ppermute | solution.py:392
  35.7 13.0 %copy-start.1 = (bf16[1,64,2,1152]{3,2,1,0:T(2,128)(2,1)S(1)}, bf16[1,64,2,1152]{3,2,1,0:T(2,128)(2,1)}, u32[]{:S(2)}) copy-start(bf16[1,64,2,1152]{3,2,1,0:T(2,128)(2,1)} %param.11) | copy-start | bytes 884740
  44.1 16.4 %collective-permute-start.4 = (bf16[1792,128]{1,0:T(8,128)(2,1)}, bf16[1792,128]{1,0:T(8,128)(2,1)S(1)}, u32[]{:S(2)}, u32[]{:S(2)}) collective-permute-start(bf16[1792,128]{1,0:T(8,128)(2,1)} %get-tuple-element.70), channel_id=1, source_target_pairs={{0,16},{16,32},{32,48},{48,0},{1,17},{17,33},{33,49},{49,1},{2,18}... | collective-permute-start | bytes 1376264 | tf_op jit(solution)/shard_map/ppermute | solution.py:392
  44.8 15.7 %collective-permute-start.6 = (bf16[1792,128]{1,0:T(8,128)(2,1)}, bf16[1792,128]{1,0:T(8,128)(2,1)S(1)}, u32[]{:S(2)}, u32[]{:S(2)}) collective-permute-start(bf16[1792,128]{1,0:T(8,128)(2,1)} %get-tuple-element.72), channel_id=1, source_target_pairs={{0,48},{16,0},{32,16},{48,32},{1,49},{17,1},{33,17},{49,33},{2,50}... | collective-permute-start | bytes 1376264 | tf_op jit(solution)/shard_map/ppermute | solution.py:392
  47.4 13.0 %collective-permute-start.5 = (bf16[640,128]{1,0:T(8,128)(2,1)}, bf16[640,128]{1,0:T(8,128)(2,1)S(1)}, u32[]{:S(2)}, u32[]{:S(2)}) collective-permute-start(bf16[640,128]{1,0:T(8,128)(2,1)} %get-tuple-element.71), channel_id=1, source_target_pairs={{0,32},{16,48},{32,0},{48,16},{1,33},{17,49},{33,1},{49,17},{2,34}... | collective-permute-start | bytes 491528 | tf_op jit(solution)/shard_map/ppermute | solution.py:392
  48.8 1.1 %copy-start.5 = (f32[128,1152]{1,0:T(8,128)S(1)}, f32[128,1152]{1,0:T(8,128)}, u32[]{:S(2)}) copy-start(f32[128,1152]{1,0:T(8,128)} %copy-done.4) | copy-start | bytes 1769476
  51.1 20.3 %all-to-all-start.1 = ((bf16[64,2,1152]{2,1,0:T(2,128)(2,1)}), bf16[64,2,1152]{2,1,0:T(2,128)(2,1)S(1)}, u32[]{:S(2)}, u32[]{:S(2)}) async-start(bf16[64,2,1152]{2,1,0:T(2,128)(2,1)} %temporal_input_back.1), calls=%async_computation.1 | async-start | bytes 589824 | tf_op jit(solution)/shard_map/all_to_all | solution.py:509
  63.7 2.0 %collective-permute-start.7 = (bf16[1408,128]{1,0:T(8,128)(2,1)}, bf16[1408,128]{1,0:T(8,128)(2,1)S(1)}, u32[]{:S(2)}, u32[]{:S(2)}) collective-permute-start(bf16[1408,128]{1,0:T(8,128)(2,1)} %get-tuple-element.79), channel_id=1, source_target_pairs={{0,64},{64,0},{1,65},{65,1},{2,66},{66,2},{3,67},{67,3},{4,68},{68... | collective-permute-start | bytes 1081352 | tf_op jit(solution)/shard_map/ppermute | solution.py:531
  63.8 2.4 %collective-permute-start.8 = (bf16[1408,128]{1,0:T(8,128)(2,1)}, bf16[1408,128]{1,0:T(8,128)(2,1)S(1)}, u32[]{:S(2)}, u32[]{:S(2)}) collective-permute-start(bf16[1408,128]{1,0:T(8,128)(2,1)} %get-tuple-element.80), channel_id=1, source_target_pairs={{0,64},{64,0},{1,65},{65,1},{2,66},{66,2},{3,67},{67,3},{4,68},{68... | collective-permute-start | bytes 1081352 | tf_op jit(solution)/shard_map/ppermute | solution.py:531
  71.4 27.5 %all-to-all-start.2 = ((bf16[32,88,128]{2,1,0:T(8,128)(2,1)}), bf16[32,88,128]{2,1,0:T(8,128)(2,1)S(1)}, u32[]{:S(2)}, u32[]{:S(2)}) async-start(bf16[32,88,128]{2,1,0:T(8,128)(2,1)} %bitcast.21), calls=%async_computation.2 | async-start | bytes 1441792 | tf_op jit(solution)/shard_map/all_to_all | solution.py:545

commit v6 on v5

--- a/solution.py
+++ b/solution.py
@@ -144,37 +144,33 @@
     return jnp.cos(angles), jnp.sin(angles) * sign
 
 
-def branch_grad_kernel(
-    seed, pos, mod, sent, kept, cos_out, sin_out, seed_v, sent_v, kept_v, cos_v, sin_v, sems
+def tables_kernel(pos, cos_out, sin_out, cos_v, sin_v, sems):
+    cos_v[...], sin_v[...] = rope_tables(pos[...])
+    wait_all(fetch([(cos_v, cos_out), (sin_v, sin_out)], sems))
+
+
+def spatial_forward_kernel(
+    place, tokens, mod, qkv_w, out_w, seed, x1, q_out, k_out, v_out, p_out, sent, kept,
+    seed_v, sent_v, kept_v, tokens_v, mod_v, w_v, o_v, normed_v, x1_v, q_v, k_v, v_v, p_v, in_sem, out_sem,
 ):
-    (load,) = fetch([(seed, seed_v)], sems.at[pl.ds(0, 1)])
-    cos_v[...], sin_v[...] = rope_tables(pos[...])
-    saves = fetch([(cos_v, cos_out), (sin_v, sin_out)], sems.at[pl.ds(1, 2)])
-    load.wait()
-    g = seed_v[...].reshape(TOK, D).astype(F32)
-    branch_grad = (mod[0, 2, 1:2, :] * g).astype(BF16)
-    sent_v[...] = regroup(branch_grad)
-    kept_v[...] = branch_grad
-    wait_all(saves + fetch([(sent_v, sent), (kept_v, kept)], sems.at[pl.ds(3, 2)]))
-
-
-def spatial_forward_kernel(
-    place, tokens, mod, qkv_w, out_w, x1, q_out, k_out, v_out, p_out,
-    tokens_v, mod_v, w_v, o_v, normed_v, x1_v, q_v, k_v, v_v, p_v, in_sem, out_sem,
-):
-    pairs = [(tokens, tokens_v), (mod, mod_v)]
+    pairs = [(tokens, tokens_v), (mod, mod_v), (seed, seed_v)]
     pairs += [(qkv_w.at[0, pl.ds(i * HW, HW)], w_v.at[pl.ds(i * HW, HW)]) for i in range(3)] + [(out_w.at[0], o_v)]
     copies = [pltpu.make_async_copy(src, dst, in_sem.at[i]) for i, (src, dst) in enumerate(pairs)]
     start_all(copies)
-    wait_all(copies[:2])
+    wait_all(copies[:3])
 
     @pl.when(place[0] >= 0)
     def _():
         unit, _ = layer_norm(tokens_v[...].astype(F32))
         normed_v[...] = (unit * (1.0 + mod_v[0, 1, 0:1, :]) + mod_v[0, 0, 0:1, :]).astype(BF16)
+        branch_grad = (mod_v[0, 2, 1:2, :] * seed_v[...].reshape(TOK, D).astype(F32)).astype(BF16)
+        sent_v[...] = regroup(branch_grad)
+        kept_v[...] = branch_grad
+
+    saves = fetch([(sent_v, sent), (kept_v, kept)], out_sem.at[pl.ds(5, 2)])
 
     for i, held in enumerate((q_v, k_v, v_v)):
-        copies[2 + i].wait()
+        copies[3 + i].wait()
 
         @pl.when(place[0] >= 0)
         def _(i=i, held=held):
@@ -183,8 +179,8 @@
     probs, attended = attend(q_v[...], split_heads(k_v[...]), split_heads(v_v[...]), None)
     for h in range(HEADS):
         p_v[h] = probs[h]
-    saves = fetch([(q_v, q_out), (k_v, k_out), (v_v, v_out), (p_v, p_out)], out_sem.at[pl.ds(0, 4)])
-    copies[5].wait()
+    saves += fetch([(q_v, q_out), (k_v, k_out), (v_v, v_out), (p_v, p_out)], out_sem.at[pl.ds(0, 4)])
+    copies[6].wait()
     branch = dot(attended, o_v[...])
     x1_v[...] = (tokens_v[...].astype(F32) + mod_v[0, 2, 0:1, :] * branch).astype(BF16).reshape(FRAMES, 2, D)
     saves += fetch([(x1_v, x1)], out_sem.at[pl.ds(4, 1)])
@@ -443,27 +439,30 @@
     seq = ("y", "xl", "z")
 
     place = lax.axis_index("y").reshape(1).astype(jnp.int32)
-    x1, q, k, v, p = call(
+    x1, q, k, v, p, sent, branch_grad = call(
         spatial_forward_kernel,
         "spatial_forward",
-        [(SMEM, place), (HBM, tokens), (HBM, mod), (HBM, qkv_w), (HBM, out_weight)],
-        [(HBM, BF16, PAIRS), (HBM, BF16, ATT), (HBM, BF16, ATT), (HBM, BF16, ATT), (HBM, BF16, PROB)],
+        [(SMEM, place), (HBM, tokens), (HBM, mod), (HBM, qkv_w), (HBM, out_weight), (HBM, seed)],
         [
-            buf(BF16, TOK, D), buf(F32, *MOD), buf(BF16, *QKV_W), buf(BF16, *OUT_W), buf(BF16, TOK, D),
-            buf(BF16, *PAIRS), buf(BF16, *ATT), buf(BF16, *ATT), buf(BF16, *ATT), buf(BF16, *PROB), dma(6), dma(5),
+            (HBM, BF16, PAIRS), (HBM, BF16, ATT), (HBM, BF16, ATT), (HBM, BF16, ATT), (HBM, BF16, PROB),
+            (HBM, BF16, (TOK, D)), (HBM, BF16, (TOK, D)),
+        ],
+        [
+            buf(BF16, *PAIRS), buf(BF16, TOK, D), buf(BF16, TOK, D), buf(BF16, TOK, D), buf(F32, *MOD), buf(BF16, *QKV_W), buf(BF16, *OUT_W), buf(BF16, TOK, D),
+            buf(BF16, *PAIRS), buf(BF16, *ATT), buf(BF16, *ATT), buf(BF16, *ATT), buf(BF16, *PROB), dma(7), dma(7),
         ],
         us=5.0,
     )
     located = lax.all_to_all(x1, seq, split_axis=0, concat_axis=0, tiled=True)
 
-    later_seed, later_pos, _ = lax.optimization_barrier((seed, frame_pos, x1))
-    sent, branch_grad, cosines, sines = call(
-        branch_grad_kernel,
-        "branch_grad",
-        [(HBM, later_seed), (VMEM, later_pos.reshape(1, FRAMES)), (VMEM, mod)],
-        [(HBM, BF16, (TOK, D)), (HBM, BF16, (TOK, D)), (HBM, F32, ATT), (HBM, F32, ATT)],
-        [buf(BF16, *PAIRS), buf(BF16, TOK, D), buf(BF16, TOK, D), buf(F32, *ATT), buf(F32, *ATT), dma(5)],
-        us=3.0,
+    later_pos, _ = lax.optimization_barrier((frame_pos, x1))
+    cosines, sines = call(
+        tables_kernel,
+        "tables",
+        [(VMEM, later_pos.reshape(1, FRAMES))],
+        [(HBM, F32, ATT), (HBM, F32, ATT)],
+        [buf(F32, *ATT), buf(F32, *ATT), dma(2)],
+        us=1.5,
     )
     branch_all = [sent] + [over("y", Y, i, sent) for i in range(1, Y)]
 

time: 100 us -> 98.8 us (0.988)
  starting transfers between devices: 38.7 us -> 37.1 us
    all_to_all x1, starting transfers between devices: 8.21 us -> 6.54 us  [shards(): lax.all_to_all(located_grad, seq, split_axis=0, concat_axis=0, tiled=True)]
    ppermute x7, waiting for transfers between devices: 0.02 us -> 1.46 us  [over(): return lax.ppermute(x, axis, [(i, (i + k) % size) for i in range(size)])]
    all_to_all x1, waiting for transfers between devices: 4.21 us -> 2.8 us  [shards(): lax.all_to_all(located_grad, seq, split_axis=0, concat_axis=0, tiled=True)]
  transfers between devices with their start and end apart: 12 -> 12, of which waited for: 5 -> 8; matrix products, arithmetic and copies ran while one was open for 0% -> 0% of each run, Pallas kernels for 30% -> 30%
where the time goes in v6:
time: 98.8 us; the launch traced here: 98.3 us
  starting transfers between devices  37.1 us (38%)
  Pallas kernels  35.7 us (36%)
  waiting for transfers between devices  22.5 us (23%)
  local copies, waits for them, and re-layouts  1.91 us (2%)
  between operations  1 us (1%)
    pallas_call x13, Pallas kernels, call(): pl.pallas_call(kernel, out_shape=tuple((space(shape, dtype) for space, dt...  35.7 us
    all_to_all x1, starting transfers between devices, shards(): located = lax.all_to_all(x1, seq, split_axis=0, concat_axis=0, tiled=True)  12.7 us
    all_to_all x1, waiting for transfers between devices, shards(): lax.all_to_all(halves.reshape(2 * PARTS, *CHUNK), ('xh', 'xl', 'z'), spli...  11.7 us
    ppermute x7, starting transfers between devices, over(): return lax.ppermute(x, axis, [(i, (i + k) % size) for i in range(size)])  11.4 us
    all_to_all x1, starting transfers between devices, shards(): lax.all_to_all(located_grad, seq, split_axis=0, concat_axis=0, tiled=True)  6.54 us
    all_to_all x1, starting transfers between devices, shards(): lax.all_to_all(halves.reshape(2 * PARTS, *CHUNK), ('xh', 'xl', 'z'), spli...  5.86 us
    all_to_all x1, waiting for transfers between devices, shards(): located = lax.all_to_all(x1, seq, split_axis=0, concat_axis=0, tiled=True)  5.85 us
    all_to_all x1, waiting for transfers between devices, shards(): lax.all_to_all(located_grad, seq, split_axis=0, concat_axis=0, tiled=True)  2.8 us
  transfers between devices with their start and end apart: 12, of which 8 were waited for; matrix products, arithmetic and copies ran while one was open for 0% of the time, Pallas kernels for 30%

profile of v6, /device:TPU:32, one launch (start us, length us, event | category | flops | bytes accessed | tf_op | source)
XLA Modules:
  0.0 98.3 jit_solution(17154837025185606492)
XLA Ops:
  0.6 0.0 copy-start.3
  0.6 0.0 copy-start.2
  0.7 5.6 %spatial_forward.1 = (bf16[64,2,1152]{2,1,0:T(2,128)(2,1)}, bf16[128,576]{1,0:T(8,128)(2,1)}, bf16[128,576]{1,0:T(8,128)(2,1)}, bf16[128,576]{1,0:T(8,128)(2,1)}...) custom-call(s32[1]{0:T(128)} %bitcast.place, bf16[128,1152]{1,0:T(8,128)(2,1)} %bitcast.24, ...), custom_call_target="tpu_custom_call" | custom-call | flops 5000000000 | bytes 15000000 | tf_op jit(solution)/shard_map/spatial_forward/pallas_call | solution.py:375
  6.3 12.7 %all-to-all-start = ((bf16[64,2,1152]{2,1,0:T(2,128)(2,1)}), bf16[64,2,1152]{2,1,0:T(2,128)(2,1)S(1)}, u32[]{:S(2)}, u32[]{:S(2)}) async-start(bf16[64,2,1152]{2,1,0:T(2,128)(2,1)} %get-tuple-element.47), calls=%async_computation | async-start | bytes 589824 | tf_op jit(solution)/shard_map/all_to_all | solution.py:456
  19.0 1.5 %collective-permute-start = (bf16[128,1152]{1,0:T(8,128)(2,1)}, bf16[128,1152]{1,0:T(8,128)(2,1)S(1)}, u32[]{:S(2)}, u32[]{:S(2)}) collective-permute-start(bf16[128,1152]{1,0:T(8,128)(2,1)} %get-tuple-element.66.refs_1_), channel_id=1, source_target_pairs={{0,16},{16,32},{32,48},{48,0},{1,17},{17,33},{33,49},{49,1},{2,18}... | collective-permute-start | bytes 884744 | tf_op jit(solution)/shard_map/ppermute | solution.py:388
  20.5 2.9 %collective-permute-start.1 = (bf16[128,1152]{1,0:T(8,128)(2,1)}, bf16[128,1152]{1,0:T(8,128)(2,1)S(1)}, u32[]{:S(2)}, u32[]{:S(2)}) collective-permute-start(bf16[128,1152]{1,0:T(8,128)(2,1)} %get-tuple-element.66.refs_1_), channel_id=1, source_target_pairs={{0,32},{16,48},{32,0},{48,16},{1,33},{17,49},{33,1},{49,17},{2,34}... | collective-permute-start | bytes 884744 | tf_op jit(solution)/shard_map/ppermute | solution.py:388
  23.4 1.4 %collective-permute-start.2 = (bf16[128,1152]{1,0:T(8,128)(2,1)}, bf16[128,1152]{1,0:T(8,128)(2,1)S(1)}, u32[]{:S(2)}, u32[]{:S(2)}) collective-permute-start(bf16[128,1152]{1,0:T(8,128)(2,1)} %get-tuple-element.66.refs_1_), channel_id=1, source_target_pairs={{0,48},{16,0},{32,16},{48,32},{1,49},{17,1},{33,17},{49,33},{2,50}... | collective-permute-start | bytes 884744 | tf_op jit(solution)/shard_map/ppermute | solution.py:388
  24.7 0.0 copy-done.3
  24.7 2.0 %tables.1 = (f32[128,576]{1,0:T(8,128)}, f32[128,576]{1,0:T(8,128)}) custom-call(s32[1,64]{1,0:T(1,128)S(1)} %bitcast.19), custom_call_target="tpu_custom_call" | custom-call | flops 1500000000 | bytes 4500000 | tf_op jit(solution)/shard_map/tables/pallas_call | solution.py:375
  26.8 5.8 %all-to-all-done.located = bf16[64,2,1152]{2,1,0:T(2,128)(2,1)S(1)} async-done(((bf16[64,2,1152]{2,1,0:T(2,128)(2,1)}), bf16[64,2,1152]{2,1,0:T(2,128)(2,1)S(1)}, u32[]{:S(2)}, u32[]{:S(2)}) %all-to-all-start) | async-done | bytes 294944 | tf_op jit(solution)/shard_map/all_to_all | solution.py:456
  32.6 0.0 copy-start
  32.6 0.0 copy-done.2
  32.7 1.3 %temporal_normed.1 = (bf16[1152,128]{1,0:T(8,128)(2,1)}, bf16[1152,128]{1,0:T(8,128)(2,1)S(1)}, bf16[128,1152]{1,0:T(8,128)(2,1)S(1)}, f32[128,1152]{1,0:T(8,128)S(1)}, f32[128,128]{1,0:T(8,128)S(1)}) custom-call(bf16[64,2,1152]{2,1,0:T(2,128)(2,1)S(1)} %all-to-all-done.located, f32[1,3,2,1152]{3,2,1,0:T(2,128)S(1)} %bitcast.14), custom_call_target="tpu_custom_call" | custom-call | flops 1500000000 | bytes 4500000 | tf_op jit(solution)/shard_map/temporal_normed/pallas_call | solution.py:375
  34.0 0.0 copy-start.4
  34.0 0.8 copy-done.4
  34.8 1.0 %collective-permute-start.3 = (bf16[1152,128]{1,0:T(8,128)(2,1)}, bf16[1152,128]{1,0:T(8,128)(2,1)S(1)}, u32[]{:S(2)}, u32[]{:S(2)}) collective-permute-start(bf16[1152,128]{1,0:T(8,128)(2,1)} %get-tuple-element.59), channel_id=1, source_target_pairs={{0,32},{16,48},{32,0},{48,16},{1,33},{17,49},{33,1},{49,17},{2,34}... | collective-permute-start | bytes 884744 | tf_op jit(solution)/shard_map/ppermute | solution.py:388
  35.8 0.0 copy-start.1
  35.8 8.4 %temporal_attention.1 = (bf16[128,576]{1,0:T(8,128)(2,1)S(1)}, bf16[128,1152]{1,0:T(8,128)(2,1)S(1)}, bf16[1792,128]{1,0:T(8,128)(2,1)}, bf16[1792,128]{1,0:T(8,...) custom-call(s32[1]{0:T(128)} %bitcast.place, bf16[128,1152]{1,0:T(8,128)(2,1)S(1)} %get-tuple-element.52.normed, ...), custom_call_target="tpu_custom_call" | custom-call | flops 7000000000 | bytes 21000000 | tf_op jit(solution)/shard_map/temporal_attention/pallas_call | solution.py:375
  44.2 0.0 copy-done
  44.2 0.7 collective-permute-start.4
  44.9 0.0 collective-permute-done.refs_5_
  44.9 2.6 %collective-permute-start.6 = (bf16[1792,128]{1,0:T(8,128)(2,1)}, bf16[1792,128]{1,0:T(8,128)(2,1)S(1)}, u32[]{:S(2)}, u32[]{:S(2)}) collective-permute-start(bf16[1792,128]{1,0:T(8,128)(2,1)} %get-tuple-element.70), channel_id=1, source_target_pairs={{0,48},{16,0},{32,16},{48,32},{1,49},{17,1},{33,17},{49,33},{2,50}... | collective-permute-start | bytes 1376264 | tf_op jit(solution)/shard_map/ppermute | solution.py:388
  47.5 0.0 collective-permute-done.1.refs_6_
  47.5 1.3 %collective-permute-start.5 = (bf16[640,128]{1,0:T(8,128)(2,1)}, bf16[640,128]{1,0:T(8,128)(2,1)S(1)}, u32[]{:S(2)}, u32[]{:S(2)}) collective-permute-start(bf16[640,128]{1,0:T(8,128)(2,1)} %get-tuple-element.69), channel_id=1, source_target_pairs={{0,32},{16,48},{32,0},{48,16},{1,33},{17,49},{33,1},{49,17},{2,34}... | collective-permute-start | bytes 491528 | tf_op jit(solution)/shard_map/ppermute | solution.py:388
  48.9 0.0 collective-permute-done.2.refs_7_
  48.9 0.0 collective-permute-done.3.refs_8_
  48.9 0.0 copy-done.1
  48.9 0.0 copy-start.5
  48.9 1.1 %copy-done.5 = f32[128,1152]{1,0:T(8,128)S(1)} copy-done((f32[128,1152]{1,0:T(8,128)S(1)}, f32[128,1152]{1,0:T(8,128)}, u32[]{:S(2)}) %copy-start.5) | copy-done | bytes 589848
  50.0 1.3 %temporal_input_back.1 = bf16[64,2,1152]{2,1,0:T(2,128)(2,1)} custom-call(bf16[128,1152]{1,0:T(8,128)(2,1)S(1)} %get-tuple-element.60.normed_grad, bf16[64,2,1152]{2,1,0:T(2,128)(2,1)S(1)} %bitcast.12, f32[1,3,2,1152]{3,2,1,0:T(2,128)S(1)} %bitcast.15, f32[128,1152]{1,0:T(8,128)S(1)} %copy-done.5, f32[128,128]{1,0:T(8,128)S(1)} %get-tuple-element.62.inverse), custom_call_target="tpu_custom_call" | custom-call | flops 3000000000 | bytes 9000000 | tf_op jit(solution)/shard_map/temporal_input_back/pallas_call | solution.py:375
  51.2 6.5 %all-to-all-start.1 = ((bf16[64,2,1152]{2,1,0:T(2,128)(2,1)}), bf16[64,2,1152]{2,1,0:T(2,128)(2,1)S(1)}, u32[]{:S(2)}, u32[]{:S(2)}) async-start(bf16[64,2,1152]{2,1,0:T(2,128)(2,1)} %temporal_input_back.1), calls=%async_computation.1 | async-start | bytes 589824 | tf_op jit(solution)/shard_map/all_to_all | solution.py:508
  57.8 1.1 %load_own.1 = (bf16[1792,128]{1,0:T(8,128)(2,1)S(1)}, bf16[128,1152]{1,0:T(8,128)(2,1)S(1)}) custom-call(bf16[1792,128]{1,0:T(8,128)(2,1)} %get-tuple-element.65.refs_0_, bf16[128,1152]{1,0:T(8,128)(2,1)} %get-tuple-element.66.refs_1_), custom_call_target="tpu_custom_call" | custom-call | flops 1000000000 | bytes 3000000 | tf_op jit(solution)/shard_map/load_own/pallas_call | solution.py:375
  58.9 0.9 collective-permute-done.5.refs_2_
  59.8 0.2 collective-permute-done.4.refs_1_
  60.0 0.4 collective-permute-done.6.refs_3_
  60.4 3.2 %weight_grad.1 = (bf16[2,1408,128]{2,1,0:T(8,128)(2,1)}, bf16[1408,128]{1,0:T(8,128)(2,1)}, bf16[1408,128]{1,0:T(8,128)(2,1)}) custom-call(s32[1]{0:T(128)} %bitcast.6.core, bf16[1792,128]{1,0:T(8,128)(2,1)S(1)} %get-tuple-element.67.refs_0_, bf16[1792,128]{1,0:T(8,128)(2,1)S(1)} %collective-permute-done.4.refs_1_, ...), custom_call_target="tpu_custom_call" | custom-call | flops 4600000000 | bytes 13799999 | tf_op jit(solution)/shard_map/weight_grad/pallas_call | solution.py:375
  63.6 0.1 collective-permute-start.7
  63.7 0.5 collective-permute-start.8
  64.2 1.1 %load.1.kept = bf16[2,1408,128]{2,1,0:T(8,128)(2,1)S(1)} custom-call(bf16[2,1408,128]{2,1,0:T(8,128)(2,1)} %get-tuple-element.76.refs_0_), custom_call_target="tpu_custom_call" | custom-call | flops 1000000000 | bytes 3000000 | tf_op jit(solution)/shard_map/load/pallas_call | solution.py:375
  65.3 0.3 collective-permute-done.7.refs_0_
  65.6 0.5 collective-permute-done.8.refs_1_
  66.1 1.0 add_cores.1
  67.1 2.8 %all-to-all-done.1.grad = bf16[64,2,1152]{2,1,0:T(2,128)(2,1)S(1)} async-done(((bf16[64,2,1152]{2,1,0:T(2,128)(2,1)}), bf16[64,2,1152]{2,1,0:T(2,128)(2,1)S(1)}, u32[]{:S(2)}, u32[]{:S(2)}) %all-to-all-start.1) | async-done | bytes 294944 | tf_op jit(solution)/shard_map/all_to_all | solution.py:508
  69.9 5.9 %all-to-all-start.2 = ((bf16[32,88,128]{2,1,0:T(8,128)(2,1)}), bf16[32,88,128]{2,1,0:T(8,128)(2,1)S(1)}, u32[]{:S(2)}, u32[]{:S(2)}) async-start(bf16[32,88,128]{2,1,0:T(8,128)(2,1)} %bitcast.20), calls=%async_computation.2 | async-start | bytes 1441792 | tf_op jit(solution)/shard_map/all_to_all | solution.py:544
  75.7 2.6 %block_out.1 = bf16[64,2,1152]{2,1,0:T(2,128)(2,1)} custom-call(bf16[128,576]{1,0:T(8,128)(2,1)S(1)} %get-tuple-element.82.attended, bf16[2,576,1152]{2,1,0:T(8,128)(2,1)} %out_w.7, bf16[64,2,1152]{2,1,0:T(2,128)(2,1)} %copy-done, f32[1,3,2,1152]{3,2,1,0:T(2,128)S(1)} %bitcast.16), custom_call_target="tpu_custom_call" | custom-call | flops 2000000000 | bytes 6000000 | tf_op jit(solution)/shard_map/block_out/pallas_call | solution.py:375
  78.3 3.2 %spatial_attention_back.1.projected_grad = bf16[128,1728]{1,0:T(8,128)(2,1)S(1)} custom-call(bf16[64,2,1152]{2,1,0:T(2,128)(2,1)S(1)} %all-to-all-done.1.grad, f32[1,3,2,1152]{3,2,1,0:T(2,128)S(1)} %bitcast.17, bf16[2,576,1152]{2,1,0:T(8,128)(2,1)} %out_w.7, bf16[128,576]{1,0:T(8,128)(2,1)} %get-tuple-element.84.q_in, ...), custom_call_target="tpu_custom_call" | custom-call | flops 3500000000 | bytes 10500000 | tf_op jit(solution)/shard_map/spatial_attention_back/pallas_call | solution.py:375
  81.6 4.1 %spatial_input_back.1 = bf16[128,1152]{1,0:T(8,128)(2,1)} custom-call(bf16[64,2,1152]{2,1,0:T(2,128)(2,1)S(1)} %all-to-all-done.1.grad, bf16[128,1152]{1,0:T(8,128)(2,1)} %bitcast.25, f32[1,3,2,1152]{3,2,1,0:T(2,128)S(1)} %bitcast.18, bf16[2,1728,1152]{2,1,0:T(8,128)(2,1)} %bitcast.23, bf16[128,1728]{1,0:T(8,128)(2,1)S(1)} %spatial_attention_back.1.projected_grad), custom_call_target="tpu_custom_call" | custom-call | flops 3000000000 | bytes 9000000 | tf_op jit(solution)/shard_map/spatial_input_back/pallas_call | solution.py:375
  85.7 11.7 %all-to-all-done.2.parts = bf16[32,88,128]{2,1,0:T(8,128)(2,1)S(1)} async-done(((bf16[32,88,128]{2,1,0:T(8,128)(2,1)}), bf16[32,88,128]{2,1,0:T(8,128)(2,1)S(1)}, u32[]{:S(2)}, u32[]{:S(2)}) %all-to-all-start.2) | async-done | bytes 720928 | tf_op jit(solution)/shard_map/all_to_all | solution.py:544
  97.3 0.7 sum_parts.1
Async XLA Ops:
  0.6 24.1 %copy-start.3 = (s32[64]{0:T(128)S(1)}, s32[64]{0:T(128)}, u32[]{:S(2)}) copy-start(s32[64]{0:T(128)} %param.8) | copy-start | bytes 772
  0.6 32.0 %copy-start.2 = (f32[1,2,3,1152]{3,1,2,0:T(2,128)S(1)}, f32[1,2,3,1152]{3,1,2,0:T(2,128)}, u32[]{:S(2)}) copy-start(f32[1,2,3,1152]{3,1,2,0:T(2,128)} %param.7) | copy-start | bytes 82948
  6.3 26.4 %all-to-all-start = ((bf16[64,2,1152]{2,1,0:T(2,128)(2,1)}), bf16[64,2,1152]{2,1,0:T(2,128)(2,1)S(1)}, u32[]{:S(2)}, u32[]{:S(2)}) async-start(bf16[64,2,1152]{2,1,0:T(2,128)(2,1)} %get-tuple-element.47), calls=%async_computation | async-start | bytes 589824 | tf_op jit(solution)/shard_map/all_to_all | solution.py:456
  19.0 26.0 %collective-permute-start = (bf16[128,1152]{1,0:T(8,128)(2,1)}, bf16[128,1152]{1,0:T(8,128)(2,1)S(1)}, u32[]{:S(2)}, u32[]{:S(2)}) collective-permute-start(bf16[128,1152]{1,0:T(8,128)(2,1)} %get-tuple-element.66.refs_1_), channel_id=1, source_target_pairs={{0,16},{16,32},{32,48},{48,0},{1,17},{17,33},{33,49},{49,1},{2,18}... | collective-permute-start | bytes 884744 | tf_op jit(solution)/shard_map/ppermute | solution.py:388
  20.5 27.0 %collective-permute-start.1 = (bf16[128,1152]{1,0:T(8,128)(2,1)}, bf16[128,1152]{1,0:T(8,128)(2,1)S(1)}, u32[]{:S(2)}, u32[]{:S(2)}) collective-permute-start(bf16[128,1152]{1,0:T(8,128)(2,1)} %get-tuple-element.66.refs_1_), channel_id=1, source_target_pairs={{0,32},{16,48},{32,0},{48,16},{1,33},{17,49},{33,1},{49,17},{2,34}... | collective-permute-start | bytes 884744 | tf_op jit(solution)/shard_map/ppermute | solution.py:388
  23.4 25.5 %collective-permute-start.2 = (bf16[128,1152]{1,0:T(8,128)(2,1)}, bf16[128,1152]{1,0:T(8,128)(2,1)S(1)}, u32[]{:S(2)}, u32[]{:S(2)}) collective-permute-start(bf16[128,1152]{1,0:T(8,128)(2,1)} %get-tuple-element.66.refs_1_), channel_id=1, source_target_pairs={{0,48},{16,0},{32,16},{48,32},{1,49},{17,1},{33,17},{49,33},{2,50}... | collective-permute-start | bytes 884744 | tf_op jit(solution)/shard_map/ppermute | solution.py:388
  32.6 11.6 %copy-start = (bf16[64,2,1152]{2,1,0:T(2,128)(2,1)}, bf16[64,2,1152]{2,1,0:T(2,128)(2,1)S(1)}, u32[]{:S(2)}) copy-start(bf16[64,2,1152]{2,1,0:T(2,128)(2,1)S(1)} %all-to-all-done.located) | copy-start | bytes 884740
  34.0 0.8 copy-start.4
  34.8 14.0 %collective-permute-start.3 = (bf16[1152,128]{1,0:T(8,128)(2,1)}, bf16[1152,128]{1,0:T(8,128)(2,1)S(1)}, u32[]{:S(2)}, u32[]{:S(2)}) collective-permute-start(bf16[1152,128]{1,0:T(8,128)(2,1)} %get-tuple-element.59), channel_id=1, source_target_pairs={{0,32},{16,48},{32,0},{48,16},{1,33},{17,49},{33,1},{49,17},{2,34}... | collective-permute-start | bytes 884744 | tf_op jit(solution)/shard_map/ppermute | solution.py:388
  35.8 13.0 %copy-start.1 = (bf16[1,64,2,1152]{3,2,1,0:T(2,128)(2,1)S(1)}, bf16[1,64,2,1152]{3,2,1,0:T(2,128)(2,1)}, u32[]{:S(2)}) copy-start(bf16[1,64,2,1152]{3,2,1,0:T(2,128)(2,1)} %param.11) | copy-start | bytes 884740
  44.2 15.8 %collective-permute-start.4 = (bf16[1792,128]{1,0:T(8,128)(2,1)}, bf16[1792,128]{1,0:T(8,128)(2,1)S(1)}, u32[]{:S(2)}, u32[]{:S(2)}) collective-permute-start(bf16[1792,128]{1,0:T(8,128)(2,1)} %get-tuple-element.68), channel_id=1, source_target_pairs={{0,16},{16,32},{32,48},{48,0},{1,17},{17,33},{33,49},{49,1},{2,18}... | collective-permute-start | bytes 1376264 | tf_op jit(solution)/shard_map/ppermute | solution.py:388
  44.9 15.5 %collective-permute-start.6 = (bf16[1792,128]{1,0:T(8,128)(2,1)}, bf16[1792,128]{1,0:T(8,128)(2,1)S(1)}, u32[]{:S(2)}, u32[]{:S(2)}) collective-permute-start(bf16[1792,128]{1,0:T(8,128)(2,1)} %get-tuple-element.70), channel_id=1, source_target_pairs={{0,48},{16,0},{32,16},{48,32},{1,49},{17,1},{33,17},{49,33},{2,50}... | collective-permute-start | bytes 1376264 | tf_op jit(solution)/shard_map/ppermute | solution.py:388
  47.5 12.2 %collective-permute-start.5 = (bf16[640,128]{1,0:T(8,128)(2,1)}, bf16[640,128]{1,0:T(8,128)(2,1)S(1)}, u32[]{:S(2)}, u32[]{:S(2)}) collective-permute-start(bf16[640,128]{1,0:T(8,128)(2,1)} %get-tuple-element.69), channel_id=1, source_target_pairs={{0,32},{16,48},{32,0},{48,16},{1,33},{17,49},{33,1},{49,17},{2,34}... | collective-permute-start | bytes 491528 | tf_op jit(solution)/shard_map/ppermute | solution.py:388
  48.9 1.1 %copy-start.5 = (f32[128,1152]{1,0:T(8,128)S(1)}, f32[128,1152]{1,0:T(8,128)}, u32[]{:S(2)}) copy-start(f32[128,1152]{1,0:T(8,128)} %copy-done.4) | copy-start | bytes 1769476
  51.2 18.6 %all-to-all-start.1 = ((bf16[64,2,1152]{2,1,0:T(2,128)(2,1)}), bf16[64,2,1152]{2,1,0:T(2,128)(2,1)S(1)}, u32[]{:S(2)}, u32[]{:S(2)}) async-start(bf16[64,2,1152]{2,1,0:T(2,128)(2,1)} %temporal_input_back.1), calls=%async_computation.1 | async-start | bytes 589824 | tf_op jit(solution)/shard_map/all_to_all | solution.py:508
  63.6 2.0 %collective-permute-start.7 = (bf16[1408,128]{1,0:T(8,128)(2,1)}, bf16[1408,128]{1,0:T(8,128)(2,1)S(1)}, u32[]{:S(2)}, u32[]{:S(2)}) collective-permute-start(bf16[1408,128]{1,0:T(8,128)(2,1)} %get-tuple-element.77), channel_id=1, source_target_pairs={{0,64},{64,0},{1,65},{65,1},{2,66},{66,2},{3,67},{67,3},{4,68},{68... | collective-permute-start | bytes 1081352 | tf_op jit(solution)/shard_map/ppermute | solution.py:530
  63.7 2.4 %collective-permute-start.8 = (bf16[1408,128]{1,0:T(8,128)(2,1)}, bf16[1408,128]{1,0:T(8,128)(2,1)S(1)}, u32[]{:S(2)}, u32[]{:S(2)}) collective-permute-start(bf16[1408,128]{1,0:T(8,128)(2,1)} %get-tuple-element.78), channel_id=1, source_target_pairs={{0,64},{64,0},{1,65},{65,1},{2,66},{66,2},{3,67},{67,3},{4,68},{68... | collective-permute-start | bytes 1081352 | tf_op jit(solution)/shard_map/ppermute | solution.py:530
  69.9 27.5 %all-to-all-start.2 = ((bf16[32,88,128]{2,1,0:T(8,128)(2,1)}), bf16[32,88,128]{2,1,0:T(8,128)(2,1)S(1)}, u32[]{:S(2)}, u32[]{:S(2)}) async-start(bf16[32,88,128]{2,1,0:T(8,128)(2,1)} %bitcast.20), calls=%async_computation.2 | async-start | bytes 1441792 | tf_op jit(solution)/shard_map/all_to_all | solution.py:544

commit v7 on v6

--- a/solution.py
+++ b/solution.py
@@ -220,7 +220,7 @@
     save = pltpu.make_async_copy(grouped_out, sent, sem)
     save.start()
     kept[...] = normed
-    unit_out[...] = unit
+    unit_out[...] = unit.astype(BF16)
     inverse_out[...] = jnp.broadcast_to(inverse, (TOK, TOK))
     save.wait()
 
@@ -289,7 +289,7 @@
 
 def temporal_input_back_kernel(normed_grad, seed, mod, unit, inverse, result, result_v, sem):
     g = seed[...].reshape(TOK, D).astype(F32)
-    x_grad = layer_norm_back(normed_grad[...].astype(F32) * (1.0 + mod[0, 1, 1:2, :]), unit[...], inverse[:, 0:1])
+    x_grad = layer_norm_back(normed_grad[...].astype(F32) * (1.0 + mod[0, 1, 1:2, :]), unit[...].astype(F32), inverse[:, 0:1])
     result_v[...] = (g + x_grad).astype(BF16).reshape(FRAMES, 2, D)
     save = pltpu.make_async_copy(result_v, result, sem)
     save.start()
@@ -472,7 +472,7 @@
         "temporal_normed",
         [(VMEM, located), (VMEM, mod)],
         [
-            (HBM, BF16, (D, TOK)), (VMEM, BF16, (D, TOK)), (VMEM, BF16, (TOK, D)), (VMEM, F32, (TOK, D)),
+            (HBM, BF16, (D, TOK)), (VMEM, BF16, (D, TOK)), (VMEM, BF16, (TOK, D)), (VMEM, BF16, (TOK, D)),
             (VMEM, F32, (TOK, TOK)),
         ],
         [dma()],

time: 98.8 us -> 98.7 us (level)
  no operation moved by 1% of the time
where the time goes in v7:
time: 98.7 us; the launch traced here: 98.2 us
  starting transfers between devices  37.2 us (38%)
  Pallas kernels  35.7 us (36%)
  waiting for transfers between devices  22.5 us (23%)
  local copies, waits for them, and re-layouts  1.68 us (2%)
  between operations  1 us (1%)
    pallas_call x13, Pallas kernels, call(): pl.pallas_call(kernel, out_shape=tuple((space(shape, dtype) for space, dt...  35.7 us
    all_to_all x1, starting transfers between devices, shards(): located = lax.all_to_all(x1, seq, split_axis=0, concat_axis=0, tiled=True)  12.7 us
    all_to_all x1, waiting for transfers between devices, shards(): lax.all_to_all(halves.reshape(2 * PARTS, *CHUNK), ('xh', 'xl', 'z'), spli...  11.7 us
    ppermute x7, starting transfers between devices, over(): return lax.ppermute(x, axis, [(i, (i + k) % size) for i in range(size)])  11.4 us
    all_to_all x1, starting transfers between devices, shards(): lax.all_to_all(located_grad, seq, split_axis=0, concat_axis=0, tiled=True)  6.65 us
    all_to_all x1, starting transfers between devices, shards(): lax.all_to_all(halves.reshape(2 * PARTS, *CHUNK), ('xh', 'xl', 'z'), spli...  5.87 us
    all_to_all x1, waiting for transfers between devices, shards(): located = lax.all_to_all(x1, seq, split_axis=0, concat_axis=0, tiled=True)  5.86 us
    all_to_all x1, waiting for transfers between devices, shards(): lax.all_to_all(located_grad, seq, split_axis=0, concat_axis=0, tiled=True)  2.8 us
  transfers between devices with their start and end apart: 12, of which 8 were waited for; matrix products, arithmetic and copies ran while one was open for 0% of the time, Pallas kernels for 30%

profile of v7, /device:TPU:32, one launch (start us, length us, event | category | flops | bytes accessed | tf_op | source)
XLA Modules:
  0.0 98.2 jit_solution(1533432843748041273)
XLA Ops:
  0.6 0.0 copy-start.3
  0.6 0.0 copy-start.2
  0.7 5.6 %spatial_forward.1 = (bf16[64,2,1152]{2,1,0:T(2,128)(2,1)}, bf16[128,576]{1,0:T(8,128)(2,1)}, bf16[128,576]{1,0:T(8,128)(2,1)}, bf16[128,576]{1,0:T(8,128)(2,1)}...) custom-call(s32[1]{0:T(128)} %bitcast.place, bf16[128,1152]{1,0:T(8,128)(2,1)} %bitcast.24, ...), custom_call_target="tpu_custom_call" | custom-call | flops 5000000000 | bytes 15000000 | tf_op jit(solution)/shard_map/spatial_forward/pallas_call | solution.py:375
  6.3 12.7 %all-to-all-start = ((bf16[64,2,1152]{2,1,0:T(2,128)(2,1)}), bf16[64,2,1152]{2,1,0:T(2,128)(2,1)S(1)}, u32[]{:S(2)}, u32[]{:S(2)}) async-start(bf16[64,2,1152]{2,1,0:T(2,128)(2,1)} %get-tuple-element.47), calls=%async_computation | async-start | bytes 589824 | tf_op jit(solution)/shard_map/all_to_all | solution.py:456
  19.0 1.5 %collective-permute-start = (bf16[128,1152]{1,0:T(8,128)(2,1)}, bf16[128,1152]{1,0:T(8,128)(2,1)S(1)}, u32[]{:S(2)}, u32[]{:S(2)}) collective-permute-start(bf16[128,1152]{1,0:T(8,128)(2,1)} %get-tuple-element.66.refs_1_), channel_id=1, source_target_pairs={{0,16},{16,32},{32,48},{48,0},{1,17},{17,33},{33,49},{49,1},{2,18}... | collective-permute-start | bytes 884744 | tf_op jit(solution)/shard_map/ppermute | solution.py:388
  20.5 2.9 %collective-permute-start.1 = (bf16[128,1152]{1,0:T(8,128)(2,1)}, bf16[128,1152]{1,0:T(8,128)(2,1)S(1)}, u32[]{:S(2)}, u32[]{:S(2)}) collective-permute-start(bf16[128,1152]{1,0:T(8,128)(2,1)} %get-tuple-element.66.refs_1_), channel_id=1, source_target_pairs={{0,32},{16,48},{32,0},{48,16},{1,33},{17,49},{33,1},{49,17},{2,34}... | collective-permute-start | bytes 884744 | tf_op jit(solution)/shard_map/ppermute | solution.py:388
  23.4 1.4 %collective-permute-start.2 = (bf16[128,1152]{1,0:T(8,128)(2,1)}, bf16[128,1152]{1,0:T(8,128)(2,1)S(1)}, u32[]{:S(2)}, u32[]{:S(2)}) collective-permute-start(bf16[128,1152]{1,0:T(8,128)(2,1)} %get-tuple-element.66.refs_1_), channel_id=1, source_target_pairs={{0,48},{16,0},{32,16},{48,32},{1,49},{17,1},{33,17},{49,33},{2,50}... | collective-permute-start | bytes 884744 | tf_op jit(solution)/shard_map/ppermute | solution.py:388
  24.7 0.0 copy-done.3
  24.7 2.0 %tables.1 = (f32[128,576]{1,0:T(8,128)}, f32[128,576]{1,0:T(8,128)}) custom-call(s32[1,64]{1,0:T(1,128)S(1)} %bitcast.19), custom_call_target="tpu_custom_call" | custom-call | flops 1500000000 | bytes 4500000 | tf_op jit(solution)/shard_map/tables/pallas_call | solution.py:375
  26.8 5.9 %all-to-all-done.located = bf16[64,2,1152]{2,1,0:T(2,128)(2,1)S(1)} async-done(((bf16[64,2,1152]{2,1,0:T(2,128)(2,1)}), bf16[64,2,1152]{2,1,0:T(2,128)(2,1)S(1)}, u32[]{:S(2)}, u32[]{:S(2)}) %all-to-all-start) | async-done | bytes 294944 | tf_op jit(solution)/shard_map/all_to_all | solution.py:456
  32.6 0.0 copy-start
  32.6 0.0 copy-done.2
  32.7 1.3 %temporal_normed.1 = (bf16[1152,128]{1,0:T(8,128)(2,1)}, bf16[1152,128]{1,0:T(8,128)(2,1)S(1)}, bf16[128,1152]{1,0:T(8,128)(2,1)S(1)}, bf16[128,1152]{1,0:T(8,128)(2,1)S(1)}, f32[128,128]{1,0:T(8,128)S(1)}) custom-call(bf16[64,2,1152]{2,1,0:T(2,128)(2,1)S(1)} %all-to-all-done.located, f32[1,3,2,1152]{3,2,1,0:T(2,128)S(1)} %bitcast.14), custom_call_target="tpu_custom_call" | custom-call | flops 1500000000 | bytes 4500000 | tf_op jit(solution)/shard_map/temporal_normed/pallas_call | solution.py:375
  34.0 1.1 %collective-permute-start.3 = (bf16[1152,128]{1,0:T(8,128)(2,1)}, bf16[1152,128]{1,0:T(8,128)(2,1)S(1)}, u32[]{:S(2)}, u32[]{:S(2)}) collective-permute-start(bf16[1152,128]{1,0:T(8,128)(2,1)} %get-tuple-element.59), channel_id=1, source_target_pairs={{0,32},{16,48},{32,0},{48,16},{1,33},{17,49},{33,1},{49,17},{2,34}... | collective-permute-start | bytes 884744 | tf_op jit(solution)/shard_map/ppermute | solution.py:388
  35.1 0.0 copy-start.1
  35.1 8.4 %temporal_attention.1 = (bf16[128,576]{1,0:T(8,128)(2,1)S(1)}, bf16[128,1152]{1,0:T(8,128)(2,1)S(1)}, bf16[1792,128]{1,0:T(8,128)(2,1)}, bf16[1792,128]{1,0:T(8,...) custom-call(s32[1]{0:T(128)} %bitcast.place, bf16[128,1152]{1,0:T(8,128)(2,1)S(1)} %get-tuple-element.52.normed, ...), custom_call_target="tpu_custom_call" | custom-call | flops 7000000000 | bytes 21000000 | tf_op jit(solution)/shard_map/temporal_attention/pallas_call | solution.py:375
  43.5 0.0 copy-done
  43.5 0.0 copy-start.4
  43.5 0.7 copy-done.4
  44.2 0.6 collective-permute-start.4
  44.8 0.0 collective-permute-done.refs_5_
  44.8 2.6 %collective-permute-start.6 = (bf16[1792,128]{1,0:T(8,128)(2,1)}, bf16[1792,128]{1,0:T(8,128)(2,1)S(1)}, u32[]{:S(2)}, u32[]{:S(2)}) collective-permute-start(bf16[1792,128]{1,0:T(8,128)(2,1)} %get-tuple-element.70), channel_id=1, source_target_pairs={{0,48},{16,0},{32,16},{48,32},{1,49},{17,1},{33,17},{49,33},{2,50}... | collective-permute-start | bytes 1376264 | tf_op jit(solution)/shard_map/ppermute | solution.py:388
  47.4 0.0 collective-permute-done.1.refs_6_
  47.4 1.3 %collective-permute-start.5 = (bf16[640,128]{1,0:T(8,128)(2,1)}, bf16[640,128]{1,0:T(8,128)(2,1)S(1)}, u32[]{:S(2)}, u32[]{:S(2)}) collective-permute-start(bf16[640,128]{1,0:T(8,128)(2,1)} %get-tuple-element.69), channel_id=1, source_target_pairs={{0,32},{16,48},{32,0},{48,16},{1,33},{17,49},{33,1},{49,17},{2,34}... | collective-permute-start | bytes 491528 | tf_op jit(solution)/shard_map/ppermute | solution.py:388
  48.8 0.0 collective-permute-done.2.refs_7_
  48.8 0.0 collective-permute-done.3.refs_8_
  48.8 0.0 copy-done.1
  48.8 0.0 copy-start.5
  48.8 1.0 copy-done.5
  49.7 1.3 %temporal_input_back.1 = bf16[64,2,1152]{2,1,0:T(2,128)(2,1)} custom-call(bf16[128,1152]{1,0:T(8,128)(2,1)S(1)} %copy-done.5, bf16[64,2,1152]{2,1,0:T(2,128)(2,1)S(1)} %bitcast.12, f32[1,3,2,1152]{3,2,1,0:T(2,128)S(1)} %bitcast.15, bf16[128,1152]{1,0:T(8,128)(2,1)S(1)} %get-tuple-element.61.unit, f32[128,128]{1,0:T(8,128)S(1)} %get-tuple-element.62.inverse), custom_call_target="tpu_custom_call" | custom-call | flops 3000000000 | bytes 9000000 | tf_op jit(solution)/shard_map/temporal_input_back/pallas_call | solution.py:375
  51.0 6.6 %all-to-all-start.1 = ((bf16[64,2,1152]{2,1,0:T(2,128)(2,1)}), bf16[64,2,1152]{2,1,0:T(2,128)(2,1)S(1)}, u32[]{:S(2)}, u32[]{:S(2)}) async-start(bf16[64,2,1152]{2,1,0:T(2,128)(2,1)} %temporal_input_back.1), calls=%async_computation.1 | async-start | bytes 589824 | tf_op jit(solution)/shard_map/all_to_all | solution.py:508
  57.7 1.1 %load_own.1 = (bf16[1792,128]{1,0:T(8,128)(2,1)S(1)}, bf16[128,1152]{1,0:T(8,128)(2,1)S(1)}) custom-call(bf16[1792,128]{1,0:T(8,128)(2,1)} %get-tuple-element.65.refs_0_, bf16[128,1152]{1,0:T(8,128)(2,1)} %get-tuple-element.66.refs_1_), custom_call_target="tpu_custom_call" | custom-call | flops 1000000000 | bytes 3000000 | tf_op jit(solution)/shard_map/load_own/pallas_call | solution.py:375
  58.8 0.9 collective-permute-done.5.refs_2_
  59.7 0.2 collective-permute-done.4.refs_1_
  59.9 0.4 collective-permute-done.6.refs_3_
  60.3 3.2 %weight_grad.1 = (bf16[2,1408,128]{2,1,0:T(8,128)(2,1)}, bf16[1408,128]{1,0:T(8,128)(2,1)}, bf16[1408,128]{1,0:T(8,128)(2,1)}) custom-call(s32[1]{0:T(128)} %bitcast.6.core, bf16[1792,128]{1,0:T(8,128)(2,1)S(1)} %get-tuple-element.67.refs_0_, bf16[1792,128]{1,0:T(8,128)(2,1)S(1)} %collective-permute-done.4.refs_1_, ...), custom_call_target="tpu_custom_call" | custom-call | flops 4600000000 | bytes 13799999 | tf_op jit(solution)/shard_map/weight_grad/pallas_call | solution.py:375
  63.5 0.1 collective-permute-start.7
  63.6 0.5 collective-permute-start.8
  64.1 1.1 %load.1.kept = bf16[2,1408,128]{2,1,0:T(8,128)(2,1)S(1)} custom-call(bf16[2,1408,128]{2,1,0:T(8,128)(2,1)} %get-tuple-element.76.refs_0_), custom_call_target="tpu_custom_call" | custom-call | flops 1000000000 | bytes 3000000 | tf_op jit(solution)/shard_map/load/pallas_call | solution.py:375
  65.2 0.3 collective-permute-done.7.refs_0_
  65.5 0.5 collective-permute-done.8.refs_1_
  66.0 1.0 add_cores.1
  66.9 2.8 %all-to-all-done.1.grad = bf16[64,2,1152]{2,1,0:T(2,128)(2,1)S(1)} async-done(((bf16[64,2,1152]{2,1,0:T(2,128)(2,1)}), bf16[64,2,1152]{2,1,0:T(2,128)(2,1)S(1)}, u32[]{:S(2)}, u32[]{:S(2)}) %all-to-all-start.1) | async-done | bytes 294944 | tf_op jit(solution)/shard_map/all_to_all | solution.py:508
  69.7 5.9 %all-to-all-start.2 = ((bf16[32,88,128]{2,1,0:T(8,128)(2,1)}), bf16[32,88,128]{2,1,0:T(8,128)(2,1)S(1)}, u32[]{:S(2)}, u32[]{:S(2)}) async-start(bf16[32,88,128]{2,1,0:T(8,128)(2,1)} %bitcast.20), calls=%async_computation.2 | async-start | bytes 1441792 | tf_op jit(solution)/shard_map/all_to_all | solution.py:544
  75.6 2.6 %block_out.1 = bf16[64,2,1152]{2,1,0:T(2,128)(2,1)} custom-call(bf16[128,576]{1,0:T(8,128)(2,1)S(1)} %get-tuple-element.82.attended, bf16[2,576,1152]{2,1,0:T(8,128)(2,1)} %out_w.7, bf16[64,2,1152]{2,1,0:T(2,128)(2,1)} %copy-done, f32[1,3,2,1152]{3,2,1,0:T(2,128)S(1)} %bitcast.16), custom_call_target="tpu_custom_call" | custom-call | flops 2000000000 | bytes 6000000 | tf_op jit(solution)/shard_map/block_out/pallas_call | solution.py:375
  78.2 3.2 %spatial_attention_back.1.projected_grad = bf16[128,1728]{1,0:T(8,128)(2,1)S(1)} custom-call(bf16[64,2,1152]{2,1,0:T(2,128)(2,1)S(1)} %all-to-all-done.1.grad, f32[1,3,2,1152]{3,2,1,0:T(2,128)S(1)} %bitcast.17, bf16[2,576,1152]{2,1,0:T(8,128)(2,1)} %out_w.7, bf16[128,576]{1,0:T(8,128)(2,1)} %get-tuple-element.84.q_in, ...), custom_call_target="tpu_custom_call" | custom-call | flops 3500000000 | bytes 10500000 | tf_op jit(solution)/shard_map/spatial_attention_back/pallas_call | solution.py:375
  81.5 4.1 %spatial_input_back.1 = bf16[128,1152]{1,0:T(8,128)(2,1)} custom-call(bf16[64,2,1152]{2,1,0:T(2,128)(2,1)S(1)} %all-to-all-done.1.grad, bf16[128,1152]{1,0:T(8,128)(2,1)} %bitcast.25, f32[1,3,2,1152]{3,2,1,0:T(2,128)S(1)} %bitcast.18, bf16[2,1728,1152]{2,1,0:T(8,128)(2,1)} %bitcast.23, bf16[128,1728]{1,0:T(8,128)(2,1)S(1)} %spatial_attention_back.1.projected_grad), custom_call_target="tpu_custom_call" | custom-call | flops 3000000000 | bytes 9000000 | tf_op jit(solution)/shard_map/spatial_input_back/pallas_call | solution.py:375
  85.6 11.7 %all-to-all-done.2.parts = bf16[32,88,128]{2,1,0:T(8,128)(2,1)S(1)} async-done(((bf16[32,88,128]{2,1,0:T(8,128)(2,1)}), bf16[32,88,128]{2,1,0:T(8,128)(2,1)S(1)}, u32[]{:S(2)}, u32[]{:S(2)}) %all-to-all-start.2) | async-done | bytes 720928 | tf_op jit(solution)/shard_map/all_to_all | solution.py:544
  97.2 0.7 sum_parts.1
Async XLA Ops:
  0.6 24.1 %copy-start.3 = (s32[64]{0:T(128)S(1)}, s32[64]{0:T(128)}, u32[]{:S(2)}) copy-start(s32[64]{0:T(128)} %param.8) | copy-start | bytes 772
  0.6 32.0 %copy-start.2 = (f32[1,2,3,1152]{3,1,2,0:T(2,128)S(1)}, f32[1,2,3,1152]{3,1,2,0:T(2,128)}, u32[]{:S(2)}) copy-start(f32[1,2,3,1152]{3,1,2,0:T(2,128)} %param.7) | copy-start | bytes 82948
  6.3 26.4 %all-to-all-start = ((bf16[64,2,1152]{2,1,0:T(2,128)(2,1)}), bf16[64,2,1152]{2,1,0:T(2,128)(2,1)S(1)}, u32[]{:S(2)}, u32[]{:S(2)}) async-start(bf16[64,2,1152]{2,1,0:T(2,128)(2,1)} %get-tuple-element.47), calls=%async_computation | async-start | bytes 589824 | tf_op jit(solution)/shard_map/all_to_all | solution.py:456
  19.0 25.8 %collective-permute-start = (bf16[128,1152]{1,0:T(8,128)(2,1)}, bf16[128,1152]{1,0:T(8,128)(2,1)S(1)}, u32[]{:S(2)}, u32[]{:S(2)}) collective-permute-start(bf16[128,1152]{1,0:T(8,128)(2,1)} %get-tuple-element.66.refs_1_), channel_id=1, source_target_pairs={{0,16},{16,32},{32,48},{48,0},{1,17},{17,33},{33,49},{49,1},{2,18}... | collective-permute-start | bytes 884744 | tf_op jit(solution)/shard_map/ppermute | solution.py:388
  20.5 26.9 %collective-permute-start.1 = (bf16[128,1152]{1,0:T(8,128)(2,1)}, bf16[128,1152]{1,0:T(8,128)(2,1)S(1)}, u32[]{:S(2)}, u32[]{:S(2)}) collective-permute-start(bf16[128,1152]{1,0:T(8,128)(2,1)} %get-tuple-element.66.refs_1_), channel_id=1, source_target_pairs={{0,32},{16,48},{32,0},{48,16},{1,33},{17,49},{33,1},{49,17},{2,34}... | collective-permute-start | bytes 884744 | tf_op jit(solution)/shard_map/ppermute | solution.py:388
  23.4 25.4 %collective-permute-start.2 = (bf16[128,1152]{1,0:T(8,128)(2,1)}, bf16[128,1152]{1,0:T(8,128)(2,1)S(1)}, u32[]{:S(2)}, u32[]{:S(2)}) collective-permute-start(bf16[128,1152]{1,0:T(8,128)(2,1)} %get-tuple-element.66.refs_1_), channel_id=1, source_target_pairs={{0,48},{16,0},{32,16},{48,32},{1,49},{17,1},{33,17},{49,33},{2,50}... | collective-permute-start | bytes 884744 | tf_op jit(solution)/shard_map/ppermute | solution.py:388
  32.6 10.8 %copy-start = (bf16[64,2,1152]{2,1,0:T(2,128)(2,1)}, bf16[64,2,1152]{2,1,0:T(2,128)(2,1)S(1)}, u32[]{:S(2)}) copy-start(bf16[64,2,1152]{2,1,0:T(2,128)(2,1)S(1)} %all-to-all-done.located) | copy-start | bytes 884740
  34.0 14.8 %collective-permute-start.3 = (bf16[1152,128]{1,0:T(8,128)(2,1)}, bf16[1152,128]{1,0:T(8,128)(2,1)S(1)}, u32[]{:S(2)}, u32[]{:S(2)}) collective-permute-start(bf16[1152,128]{1,0:T(8,128)(2,1)} %get-tuple-element.59), channel_id=1, source_target_pairs={{0,32},{16,48},{32,0},{48,16},{1,33},{17,49},{33,1},{49,17},{2,34}... | collective-permute-start | bytes 884744 | tf_op jit(solution)/shard_map/ppermute | solution.py:388
  35.1 13.7 %copy-start.1 = (bf16[1,64,2,1152]{3,2,1,0:T(2,128)(2,1)S(1)}, bf16[1,64,2,1152]{3,2,1,0:T(2,128)(2,1)}, u32[]{:S(2)}) copy-start(bf16[1,64,2,1152]{3,2,1,0:T(2,128)(2,1)} %param.11) | copy-start | bytes 884740
  43.5 0.7 copy-start.4
  44.2 15.7 %collective-permute-start.4 = (bf16[1792,128]{1,0:T(8,128)(2,1)}, bf16[1792,128]{1,0:T(8,128)(2,1)S(1)}, u32[]{:S(2)}, u32[]{:S(2)}) collective-permute-start(bf16[1792,128]{1,0:T(8,128)(2,1)} %get-tuple-element.68), channel_id=1, source_target_pairs={{0,16},{16,32},{32,48},{48,0},{1,17},{17,33},{33,49},{49,1},{2,18}... | collective-permute-start | bytes 1376264 | tf_op jit(solution)/shard_map/ppermute | solution.py:388
  44.8 15.5 %collective-permute-start.6 = (bf16[1792,128]{1,0:T(8,128)(2,1)}, bf16[1792,128]{1,0:T(8,128)(2,1)S(1)}, u32[]{:S(2)}, u32[]{:S(2)}) collective-permute-start(bf16[1792,128]{1,0:T(8,128)(2,1)} %get-tuple-element.70), channel_id=1, source_target_pairs={{0,48},{16,0},{32,16},{48,32},{1,49},{17,1},{33,17},{49,33},{2,50}... | collective-permute-start | bytes 1376264 | tf_op jit(solution)/shard_map/ppermute | solution.py:388
  47.4 12.2 %collective-permute-start.5 = (bf16[640,128]{1,0:T(8,128)(2,1)}, bf16[640,128]{1,0:T(8,128)(2,1)S(1)}, u32[]{:S(2)}, u32[]{:S(2)}) collective-permute-start(bf16[640,128]{1,0:T(8,128)(2,1)} %get-tuple-element.69), channel_id=1, source_target_pairs={{0,32},{16,48},{32,0},{48,16},{1,33},{17,49},{33,1},{49,17},{2,34}... | collective-permute-start | bytes 491528 | tf_op jit(solution)/shard_map/ppermute | solution.py:388
  48.8 1.0 copy-start.5
  51.0 18.7 %all-to-all-start.1 = ((bf16[64,2,1152]{2,1,0:T(2,128)(2,1)}), bf16[64,2,1152]{2,1,0:T(2,128)(2,1)S(1)}, u32[]{:S(2)}, u32[]{:S(2)}) async-start(bf16[64,2,1152]{2,1,0:T(2,128)(2,1)} %temporal_input_back.1), calls=%async_computation.1 | async-start | bytes 589824 | tf_op jit(solution)/shard_map/all_to_all | solution.py:508
  63.5 2.0 %collective-permute-start.7 = (bf16[1408,128]{1,0:T(8,128)(2,1)}, bf16[1408,128]{1,0:T(8,128)(2,1)S(1)}, u32[]{:S(2)}, u32[]{:S(2)}) collective-permute-start(bf16[1408,128]{1,0:T(8,128)(2,1)} %get-tuple-element.77), channel_id=1, source_target_pairs={{0,64},{64,0},{1,65},{65,1},{2,66},{66,2},{3,67},{67,3},{4,68},{68... | collective-permute-start | bytes 1081352 | tf_op jit(solution)/shard_map/ppermute | solution.py:530
  63.6 2.4 %collective-permute-start.8 = (bf16[1408,128]{1,0:T(8,128)(2,1)}, bf16[1408,128]{1,0:T(8,128)(2,1)S(1)}, u32[]{:S(2)}, u32[]{:S(2)}) collective-permute-start(bf16[1408,128]{1,0:T(8,128)(2,1)} %get-tuple-element.78), channel_id=1, source_target_pairs={{0,64},{64,0},{1,65},{65,1},{2,66},{66,2},{3,67},{67,3},{4,68},{68... | collective-permute-start | bytes 1081352 | tf_op jit(solution)/shard_map/ppermute | solution.py:530
  69.7 27.5 %all-to-all-start.2 = ((bf16[32,88,128]{2,1,0:T(8,128)(2,1)}), bf16[32,88,128]{2,1,0:T(8,128)(2,1)S(1)}, u32[]{:S(2)}, u32[]{:S(2)}) async-start(bf16[32,88,128]{2,1,0:T(8,128)(2,1)} %bitcast.20), calls=%async_computation.2 | async-start | bytes 1441792 | tf_op jit(solution)/shard_map/all_to_all | solution.py:544
